TPU v7x, 32 devices: a whole 2x2x4 slice. The times are simulated.
32 devices in a mesh: grp: 2 (over y), lat: 4 (over z), lon: 2 (over x), comp: 2 (over core).
Axes of the slice: x: 2, y: 2, z: 4, core: 2. Of those that a mesh axis runs over, the one named last changes fastest.
Arguments:
- atmos_state: bfloat16 [48, 32, 768], P(None, ('grp', 'lat', 'comp'), 'lon'), parts along dimension 1, may hold values from -6 to 6
- ocean_state: bfloat16 [40, 32, 768], P(None, ('grp', 'lat', 'comp'), 'lon'), parts along dimension 1, may hold values from -6 to 6
- ocean_mask: int32 [32, 768], P(('grp', 'lat', 'comp'), 'lon'), parts along dimension 0, may hold values 0 or 1
- atmos_in_w: bfloat16 [2, 9, 256, 48], replicated, may hold values from -0.3125 to 0.3125
- atmos_out_w: bfloat16 [2, 9, 48, 256], replicated, may hold values from -0.125 to 0.125
- ocean_in_w: bfloat16 [2, 9, 128, 48], replicated, may hold values from -0.3125 to 0.3125
- ocean_out_w: bfloat16 [2, 9, 40, 128], replicated, may hold values from -0.1875 to 0.1875
- flux_proj: bfloat16 [8, 48], replicated, may hold values from -0.875 to 0.875
- regrid_blocks: bfloat16 [64, 128, 128], replicated, may hold values from -0.5 to 0.5
- regrid_source_block: int32 [16, 2, 8, 2], P(('grp', 'lat', 'comp'), 'lon'), parts along dimension 0, may hold values from -1 to 5, as said below
- regrid_target_block: int32 [16, 2, 8, 2], P(('grp', 'lat', 'comp'), 'lon'), parts along dimension 0, may hold values from 0 to 5
- regrid_weight_block: int32 [16, 2, 8, 2], P(('grp', 'lat', 'comp'), 'lon'), parts along dimension 0, may hold values from 0 to 63
Outputs:
- atmos_next: bfloat16 [48, 32, 768], P(None, ('grp', 'lat', 'comp'), 'lon'), parts along dimension 1
- ocean_next: bfloat16 [40, 32, 768], P(None, ('grp', 'lat', 'comp'), 'lon'), parts along dimension 1
- surface_temp_on_atmosphere: float32 [32, 768], P(('grp', 'lat', 'comp'), 'lon'), parts along dimension 0
There are 2 independent parts, one for each index of `grp`. A program takes and returns all parts, laid end to end along the dimension named above; an argument that names none is the same for every part. Nothing has to cross between parts.
Inputs may be any that keep to these rules, and one draw needn't show every extreme that they name: `regrid_source_block`: empty slots hold -1, live ones a sub-block of the source tile; each tile has both slots to the next latitude tile (t + 1 modulo 8) live, and the share of live slots differs from one latitude tile to another.
All inputs are finite; a program needn't handle non-finite values. No bound on the sum of `ocean_mask` on one device may be relied on, other than what follows from the above.
Results may differ from a plain program's by a relative error of at most 0.02.
Values may be sent and summed in bfloat16 or wider, within the bound.
No kernel may reach another device: no remote copies, remote signals or barrier semaphores. Data moves between devices by JAX's collectives and lax.ppermute only.
A program may use at most 64 MiB of HBM per device.

v0:
```python
import jax
import jax.numpy as jnp
from jax import lax
from jax.sharding import PartitionSpec as P


def with_halo(cells, sides, width):
    for axis, dim in sides:
        count = lax.axis_size(axis)
        head = lax.slice_in_dim(cells, 0, width, axis=dim)
        tail = lax.slice_in_dim(cells, cells.shape[dim] - width, cells.shape[dim], axis=dim)
        cells = jnp.concatenate(
            [
                lax.ppermute(tail, axis, [(i, (i + 1) % count) for i in range(count)]),
                cells,
                lax.ppermute(head, axis, [((i + 1) % count, i) for i in range(count)]),
            ],
            axis=dim,
        )
    return cells


def clear_poles(wide, width):
    block_height = wide.shape[1]
    position = lax.axis_index(("lat", "comp"))
    final = lax.axis_size(("lat", "comp")) - 1
    row_ids = lax.iota(jnp.int32, block_height)
    outside = (position == 0) & (row_ids < width) | (position == final) & (
        row_ids >= block_height - width
    )
    return jnp.where(outside[None, :, None], jnp.zeros((), wide.dtype), wide)


def padded_rims(field):
    wide = with_halo(field, ((("lat", "comp"), 1), ("lon", 2)), 1)
    return clear_poles(wide, 1)


def apply_taps(padded, weights, block_height, block_breadth):
    total = jnp.zeros((weights.shape[1], block_height, block_breadth), jnp.float32)
    for row_tap in range(3):
        for col_tap in range(3):
            window = padded[:, row_tap : row_tap + block_height, col_tap : col_tap + block_breadth]
            total = total + jnp.einsum(
                "hc,crw->hrw",
                weights[row_tap * 3 + col_tap],
                window,
                preferred_element_type=jnp.float32,
            )
    return total


def conv_block(state, extra, w_in, w_out, wet):
    block_height, block_breadth = (state.shape[1], state.shape[2])
    source = state if extra is None else jnp.concatenate([state, extra], axis=0)
    hidden = jax.nn.gelu(apply_taps(padded_rims(source), w_in, block_height, block_breadth)).astype(
        jnp.bfloat16
    )
    hidden = padded_rims(hidden)
    total = state.astype(jnp.float32) + apply_taps(hidden, w_out, block_height, block_breadth)
    if wet is not None:
        total = total * wet
    return total.astype(jnp.bfloat16)


def send_fluxes(block_values, destination_blocks):
    arrived, arrived_targets = (
        lax.all_to_all(block_values, ("lat", "comp"), split_axis=0, concat_axis=0, tiled=True),
        lax.all_to_all(
            destination_blocks, ("lat", "comp"), split_axis=0, concat_axis=0, tiled=True
        ),
    )
    return (arrived, arrived_targets)


def send_back(block_values):
    return lax.all_to_all(block_values, ("lat", "comp"), split_axis=0, concat_axis=0, tiled=True)


def per_device(
    atmos_state,
    ocean_state,
    ocean_mask,
    atmos_in_w,
    atmos_out_w,
    ocean_in_w,
    ocean_out_w,
    flux_proj,
    regrid_blocks,
    regrid_source_block,
    regrid_target_block,
    regrid_weight_block,
):
    block_height, block_breadth = (atmos_state.shape[1], atmos_state.shape[2])
    cells_per_block = regrid_blocks.shape[1]
    subblock_count = block_height * block_breadth // cells_per_block
    peer_count = regrid_source_block.shape[2]
    slot_count = regrid_source_block.shape[3]
    flux_count = flux_proj.shape[0]
    atmosphere_model = atmos_state
    for layer in range(atmos_in_w.shape[0]):
        atmosphere_model = conv_block(
            atmosphere_model, None, atmos_in_w[layer], atmos_out_w[layer], None
        )
    surface_flux = jnp.einsum(
        "fc,crw->frw", flux_proj, atmosphere_model, preferred_element_type=jnp.float32
    ).astype(jnp.bfloat16)
    flux_blocks = surface_flux.reshape(flux_count, subblock_count, cells_per_block)
    sources = regrid_source_block.reshape(peer_count * slot_count)
    destination_blocks = regrid_target_block.reshape(peer_count * slot_count)
    weight_ids = regrid_weight_block.reshape(peer_count * slot_count)
    sub_ids = lax.iota(jnp.int32, subblock_count)
    select_blocks = (sources[:, None] == sub_ids[None, :]).astype(jnp.bfloat16)
    chosen = jnp.einsum(
        "ps,fsb->pfb", select_blocks, flux_blocks, preferred_element_type=jnp.float32
    ).astype(jnp.bfloat16)
    collected_values = jnp.take(regrid_blocks, weight_ids, axis=0)
    contrib = jnp.einsum(
        "pfb,pbd->pfd", chosen, collected_values, preferred_element_type=jnp.float32
    ).astype(jnp.bfloat16)
    arrived, arrived_targets = send_fluxes(
        contrib.reshape(peer_count, slot_count, flux_count, cells_per_block),
        destination_blocks.reshape(peer_count, slot_count),
    )
    place_blocks = (
        arrived_targets.reshape(peer_count * slot_count)[:, None] == sub_ids[None, :]
    ).astype(jnp.bfloat16)
    ocean_flux = jnp.einsum(
        "ps,pfd->fsd",
        place_blocks,
        arrived.reshape(peer_count * slot_count, flux_count, cells_per_block),
        preferred_element_type=jnp.float32,
    )
    ocean_flux = ocean_flux.astype(jnp.bfloat16).reshape(flux_count, block_height, block_breadth)
    wet = ocean_mask.astype(jnp.float32)[None]
    ocean_model = (ocean_state.astype(jnp.float32) * wet).astype(jnp.bfloat16)
    for layer in range(ocean_in_w.shape[0]):
        ocean_model = conv_block(
            ocean_model, ocean_flux, ocean_in_w[layer], ocean_out_w[layer], wet
        )
    surface_temp_block = ocean_model[0].reshape(subblock_count, cells_per_block)
    outgoing = jnp.einsum(
        "qb,be->qe", place_blocks, surface_temp_block, preferred_element_type=jnp.float32
    ).astype(jnp.bfloat16)
    received_back = send_back(outgoing.reshape(peer_count, slot_count, cells_per_block))
    received_back = received_back.reshape(peer_count * slot_count, cells_per_block)
    surface_temp_contributions = jnp.einsum(
        "tge,te->tg", collected_values, received_back, preferred_element_type=jnp.float32
    )
    surface_temp_grid = jnp.einsum(
        "yl,yo->lo",
        select_blocks.astype(jnp.float32),
        surface_temp_contributions,
        preferred_element_type=jnp.float32,
    )
    return (atmosphere_model, ocean_model, surface_temp_grid.reshape(block_height, block_breadth))


def solution(mesh):
    in_specs = (
        P(None, ("grp", "lat", "comp"), "lon"),
        P(None, ("grp", "lat", "comp"), "lon"),
        P(("grp", "lat", "comp"), "lon"),
        P(),
        P(),
        P(),
        P(),
        P(),
        P(),
        P(("grp", "lat", "comp"), "lon", None, None),
        P(("grp", "lat", "comp"), "lon", None, None),
        P(("grp", "lat", "comp"), "lon", None, None),
    )
    out_specs = (
        P(None, ("grp", "lat", "comp"), "lon"),
        P(None, ("grp", "lat", "comp"), "lon"),
        P(("grp", "lat", "comp"), "lon"),
    )
    return jax.shard_map(
        per_device, mesh=mesh, in_specs=in_specs, out_specs=out_specs, check_vma=False
    )
```

profile of v0, /device:TPU:0, one launch (start us, length us, event | category | flops | bytes accessed | tf_op | source)
XLA Modules:
  0.0 148.5 jit_solution(2461548447013409702)
XLA Ops:
  2.4 4.1 %collective-permute-start.1 = (bf16[48,1,384]{2,0,1:T(8,128)(2,1)S(1)}, bf16[48,1,384]{2,0,1:T(8,128)(2,1)S(1)}, u32[]{:S(2)}, u32[]{:S(2)}) collective-permute-start(bf16[48,1,384]{2,0,1:T(8,128)(2,1)S(1)} %copy.214), channel_id=1, source_target_pairs={{1,0},{4,1},{5,4},{8,5},{9,8},{12,9},{13,12},{0,13},{3,2},{6,3},{7... | collective-permute-start | bytes 110600 | tf_op jit(solution)/shard_map/ppermute | solution.py:16
  6.5 1.6 %collective-permute-done = bf16[48,1,384]{2,0,1:T(8,128)(2,1)S(1)} collective-permute-done((bf16[48,1,384]{2,0,1:T(8,128)(2,1)S(1)}, bf16[48,1,384]{2,0,1:T(8,128)(2,1)S(1)}, u32[]{:S(2)}, u32[]{:S(2)}) %collective-permute-start) | collective-permute-done | bytes 36896 | tf_op jit(solution)/shard_map/ppermute | solution.py:14
  9.1 2.1 %collective-permute-start.2 = (bf16[48,4,1]{2,0,1:T(8,128)(2,1)S(1)}, bf16[48,4,1]{2,0,1:T(8,128)(2,1)S(1)}, u32[]{:S(2)}, u32[]{:S(2)}) collective-permute-start(bf16[48,4,1]{2,0,1:T(8,128)(2,1)S(1)} %get-tuple-element.34), channel_id=1, source_target_pairs={{0,2},{2,0},{1,3},{3,1},{4,6},{6,4},{5,7},{7,5},{8,10},{10,8},{9,1... | collective-permute-start | bytes 1160 | tf_op jit(solution)/shard_map/ppermute | solution.py:14
  11.3 2.5 %collective-permute-done.2 = bf16[48,4,1]{2,0,1:T(8,128)(2,1)S(1)} collective-permute-done((bf16[48,4,1]{2,0,1:T(8,128)(2,1)S(1)}, bf16[48,4,1]{2,0,1:T(8,128)(2,1)S(1)}, u32[]{:S(2)}, u32[]{:S(2)}) %collective-permute-start.2) | collective-permute-done | bytes 416 | tf_op jit(solution)/shard_map/ppermute | solution.py:14
  13.7 1.5 %collective-permute-done.3 = bf16[48,4,1]{2,0,1:T(8,128)(2,1)S(1)} collective-permute-done((bf16[48,4,1]{2,0,1:T(8,128)(2,1)S(1)}, bf16[48,4,1]{2,0,1:T(8,128)(2,1)S(1)}, u32[]{:S(2)}, u32[]{:S(2)}) %collective-permute-start.3) | collective-permute-done | bytes 416 | tf_op jit(solution)/shard_map/ppermute | solution.py:16
  19.6 3.5 %collective-permute-start.5 = (bf16[256,1,384]{0,2,1:T(8,128)(2,1)S(1)}, bf16[256,1,384]{0,2,1:T(8,128)(2,1)S(1)}, u32[]{:S(2)}, u32[]{:S(2)}) collective-permute-start(bf16[256,1,384]{0,2,1:T(8,128)(2,1)S(1)} %get-tuple-element.23), channel_id=1, source_target_pairs={{1,0},{4,1},{5,4},{8,5},{9,8},{12,9},{13,12},{0,13},{3,2},{6,3},{7... | collective-permute-start | bytes 589832 | tf_op jit(solution)/shard_map/ppermute | solution.py:16
  23.1 4.7 %collective-permute-done.4 = bf16[256,1,384]{0,2,1:T(8,128)(2,1)S(1)} collective-permute-done((bf16[256,1,384]{0,2,1:T(8,128)(2,1)S(1)}, bf16[256,1,384]{0,2,1:T(8,128)(2,1)S(1)}, u32[]{:S(2)}, u32[]{:S(2)}) %collective-permute-start.4) | collective-permute-done | bytes 196640 | tf_op jit(solution)/shard_map/ppermute | solution.py:14
  28.1 1.8 %collective-permute-start.7 = (bf16[256,4,1]{0,2,1:T(2,128)(2,1)S(1)}, bf16[256,4,1]{0,2,1:T(2,128)(2,1)S(1)}, u32[]{:S(2)}, u32[]{:S(2)}) collective-permute-start(bf16[256,4,1]{0,2,1:T(2,128)(2,1)S(1)} %get-tuple-element.15), channel_id=1, source_target_pairs={{2,0},{0,2},{3,1},{1,3},{6,4},{4,6},{7,5},{5,7},{10,8},{8,10},{11,... | collective-permute-start | bytes 6152 | tf_op jit(solution)/shard_map/ppermute | solution.py:16
  29.9 1.6 %collective-permute-done.6 = bf16[256,4,1]{0,2,1:T(2,128)(2,1)S(1)} collective-permute-done((bf16[256,4,1]{0,2,1:T(2,128)(2,1)S(1)}, bf16[256,4,1]{0,2,1:T(2,128)(2,1)S(1)}, u32[]{:S(2)}, u32[]{:S(2)}) %collective-permute-start.6) | collective-permute-done | bytes 2080 | tf_op jit(solution)/shard_map/ppermute | solution.py:14
  34.7 3.5 %collective-permute-start.9 = (bf16[48,1,384]{2,0,1:T(8,128)(2,1)S(1)}, bf16[48,1,384]{2,0,1:T(8,128)(2,1)S(1)}, u32[]{:S(2)}, u32[]{:S(2)}) collective-permute-start(bf16[48,1,384]{2,0,1:T(8,128)(2,1)S(1)} %get-tuple-element.41), channel_id=1, source_target_pairs={{1,0},{4,1},{5,4},{8,5},{9,8},{12,9},{13,12},{0,13},{3,2},{6,3},{7... | collective-permute-start | bytes 110600 | tf_op jit(solution)/shard_map/ppermute | solution.py:16
  38.9 3.3 %all-to-all-start.1 = ((s32[8,1,2]{2,1,0:T(1,128)}), s32[8,1,2]{2,1,0:T(1,128)S(1)}, u32[]{:S(2)}, u32[]{:S(2)}) async-start(s32[8,1,2]{2,1,0:T(1,128)} %copy.143), calls=%async_computation.1 | async-start | bytes 8192 | tf_op jit(solution)/shard_map/all_to_all | solution.py:69
  42.5 1.8 %collective-permute-start.10 = (bf16[48,4,1]{2,0,1:T(8,128)(2,1)S(1)}, bf16[48,4,1]{2,0,1:T(8,128)(2,1)S(1)}, u32[]{:S(2)}, u32[]{:S(2)}) collective-permute-start(bf16[48,4,1]{2,0,1:T(8,128)(2,1)S(1)} %get-tuple-element.32), channel_id=1, source_target_pairs={{0,2},{2,0},{1,3},{3,1},{4,6},{6,4},{5,7},{7,5},{8,10},{10,8},{9,1... | collective-permute-start | bytes 1160 | tf_op jit(solution)/shard_map/ppermute | solution.py:14
  44.7 2.0 %collective-permute-done.10 = bf16[48,4,1]{2,0,1:T(8,128)(2,1)S(1)} collective-permute-done((bf16[48,4,1]{2,0,1:T(8,128)(2,1)S(1)}, bf16[48,4,1]{2,0,1:T(8,128)(2,1)S(1)}, u32[]{:S(2)}, u32[]{:S(2)}) %collective-permute-start.10) | collective-permute-done | bytes 416 | tf_op jit(solution)/shard_map/ppermute | solution.py:14
  46.7 1.8 %collective-permute-done.11 = bf16[48,4,1]{2,0,1:T(8,128)(2,1)S(1)} collective-permute-done((bf16[48,4,1]{2,0,1:T(8,128)(2,1)S(1)}, bf16[48,4,1]{2,0,1:T(8,128)(2,1)S(1)}, u32[]{:S(2)}, u32[]{:S(2)}) %collective-permute-start.11) | collective-permute-done | bytes 416 | tf_op jit(solution)/shard_map/ppermute | solution.py:16
  52.0 3.5 %collective-permute-start.13 = (bf16[256,1,384]{0,2,1:T(8,128)(2,1)S(1)}, bf16[256,1,384]{0,2,1:T(8,128)(2,1)S(1)}, u32[]{:S(2)}, u32[]{:S(2)}) collective-permute-start(bf16[256,1,384]{0,2,1:T(8,128)(2,1)S(1)} %get-tuple-element.21), channel_id=1, source_target_pairs={{1,0},{4,1},{5,4},{8,5},{9,8},{12,9},{13,12},{0,13},{3,2},{6,3},{7... | collective-permute-start | bytes 589832 | tf_op jit(solution)/shard_map/ppermute | solution.py:16
  55.6 3.5 %collective-permute-done.12 = bf16[256,1,384]{0,2,1:T(8,128)(2,1)S(1)} collective-permute-done((bf16[256,1,384]{0,2,1:T(8,128)(2,1)S(1)}, bf16[256,1,384]{0,2,1:T(8,128)(2,1)S(1)}, u32[]{:S(2)}, u32[]{:S(2)}) %collective-permute-start.12) | collective-permute-done | bytes 196640 | tf_op jit(solution)/shard_map/ppermute | solution.py:14
  74.7 3.3 %all-to-all-start = ((bf16[8,2,8,128]{3,2,1,0:T(8,128)(2,1)}), bf16[8,2,8,128]{3,2,1,0:T(8,128)(2,1)S(1)}, u32[]{:S(2)}, u32[]{:S(2)}) async-start(bf16[8,2,8,128]{3,2,1,0:T(8,128)(2,1)} %bitcast.80), calls=%async_computation | async-start | bytes 65536 | tf_op jit(solution)/shard_map/all_to_all | solution.py:68
  79.3 4.4 %all-to-all-done = bf16[8,2,8,128]{3,2,1,0:T(8,128)(2,1)S(1)} async-done(((bf16[8,2,8,128]{3,2,1,0:T(8,128)(2,1)}), bf16[8,2,8,128]{3,2,1,0:T(8,128)(2,1)S(1)}, u32[]{:S(2)}, u32[]{:S(2)}) %all-to-all-start) | async-done | bytes 32800 | tf_op jit(solution)/shard_map/all_to_all | solution.py:68
  84.0 3.5 %collective-permute-start.17 = (bf16[48,1,384]{2,0,1:T(8,128)(2,1)S(1)}, bf16[48,1,384]{2,0,1:T(8,128)(2,1)S(1)}, u32[]{:S(2)}, u32[]{:S(2)}) collective-permute-start(bf16[48,1,384]{2,0,1:T(8,128)(2,1)S(1)} %get-tuple-element.39), channel_id=1, source_target_pairs={{1,0},{4,1},{5,4},{8,5},{9,8},{12,9},{13,12},{0,13},{3,2},{6,3},{7... | collective-permute-start | bytes 110600 | tf_op jit(solution)/shard_map/ppermute | solution.py:16
  87.5 1.6 %collective-permute-done.16 = bf16[48,1,384]{2,0,1:T(8,128)(2,1)S(1)} collective-permute-done((bf16[48,1,384]{2,0,1:T(8,128)(2,1)S(1)}, bf16[48,1,384]{2,0,1:T(8,128)(2,1)S(1)}, u32[]{:S(2)}, u32[]{:S(2)}) %collective-permute-start.16) | collective-permute-done | bytes 36896 | tf_op jit(solution)/shard_map/ppermute | solution.py:14
  91.4 2.1 %collective-permute-done.18 = bf16[48,4,1]{2,0,1:T(8,128)(2,1)S(1)} collective-permute-done((bf16[48,4,1]{2,0,1:T(8,128)(2,1)S(1)}, bf16[48,4,1]{2,0,1:T(8,128)(2,1)S(1)}, u32[]{:S(2)}, u32[]{:S(2)}) %collective-permute-start.18) | collective-permute-done | bytes 416 | tf_op jit(solution)/shard_map/ppermute | solution.py:14
  97.4 3.5 %collective-permute-start.21 = (bf16[128,1,384]{0,2,1:T(8,128)(2,1)S(1)}, bf16[128,1,384]{0,2,1:T(8,128)(2,1)S(1)}, u32[]{:S(2)}, u32[]{:S(2)}) collective-permute-start(bf16[128,1,384]{0,2,1:T(8,128)(2,1)S(1)} %get-tuple-element.27), channel_id=1, source_target_pairs={{1,0},{4,1},{5,4},{8,5},{9,8},{12,9},{13,12},{0,13},{3,2},{6,3},{7... | collective-permute-start | bytes 294920 | tf_op jit(solution)/shard_map/ppermute | solution.py:16
  100.9 2.6 %collective-permute-done.20 = bf16[128,1,384]{0,2,1:T(8,128)(2,1)S(1)} collective-permute-done((bf16[128,1,384]{0,2,1:T(8,128)(2,1)S(1)}, bf16[128,1,384]{0,2,1:T(8,128)(2,1)S(1)}, u32[]{:S(2)}, u32[]{:S(2)}) %collective-permute-start.20) | collective-permute-done | bytes 98336 | tf_op jit(solution)/shard_map/ppermute | solution.py:14
  105.6 1.6 %collective-permute-done.22 = bf16[128,4,1]{0,2,1:T(2,128)(2,1)S(1)} collective-permute-done((bf16[128,4,1]{0,2,1:T(2,128)(2,1)S(1)}, bf16[128,4,1]{0,2,1:T(2,128)(2,1)S(1)}, u32[]{:S(2)}, u32[]{:S(2)}) %collective-permute-start.22) | collective-permute-done | bytes 1056 | tf_op jit(solution)/shard_map/ppermute | solution.py:14
  111.0 3.5 %collective-permute-start.25 = (bf16[48,1,384]{2,0,1:T(8,128)(2,1)S(1)}, bf16[48,1,384]{2,0,1:T(8,128)(2,1)S(1)}, u32[]{:S(2)}, u32[]{:S(2)}) collective-permute-start(bf16[48,1,384]{2,0,1:T(8,128)(2,1)S(1)} %get-tuple-element.37), channel_id=1, source_target_pairs={{1,0},{4,1},{5,4},{8,5},{9,8},{12,9},{13,12},{0,13},{3,2},{6,3},{7... | collective-permute-start | bytes 110600 | tf_op jit(solution)/shard_map/ppermute | solution.py:16
  114.5 1.6 %collective-permute-done.24 = bf16[48,1,384]{2,0,1:T(8,128)(2,1)S(1)} collective-permute-done((bf16[48,1,384]{2,0,1:T(8,128)(2,1)S(1)}, bf16[48,1,384]{2,0,1:T(8,128)(2,1)S(1)}, u32[]{:S(2)}, u32[]{:S(2)}) %collective-permute-start.24) | collective-permute-done | bytes 36896 | tf_op jit(solution)/shard_map/ppermute | solution.py:14
  118.3 2.1 %collective-permute-done.26 = bf16[48,4,1]{2,0,1:T(8,128)(2,1)S(1)} collective-permute-done((bf16[48,4,1]{2,0,1:T(8,128)(2,1)S(1)}, bf16[48,4,1]{2,0,1:T(8,128)(2,1)S(1)}, u32[]{:S(2)}, u32[]{:S(2)}) %collective-permute-start.26) | collective-permute-done | bytes 416 | tf_op jit(solution)/shard_map/ppermute | solution.py:14
  124.3 3.5 %collective-permute-start.29 = (bf16[128,1,384]{0,2,1:T(8,128)(2,1)S(1)}, bf16[128,1,384]{0,2,1:T(8,128)(2,1)S(1)}, u32[]{:S(2)}, u32[]{:S(2)}) collective-permute-start(bf16[128,1,384]{0,2,1:T(8,128)(2,1)S(1)} %get-tuple-element.25), channel_id=1, source_target_pairs={{1,0},{4,1},{5,4},{8,5},{9,8},{12,9},{13,12},{0,13},{3,2},{6,3},{7... | collective-permute-start | bytes 294920 | tf_op jit(solution)/shard_map/ppermute | solution.py:16
  127.8 2.6 %collective-permute-done.28 = bf16[128,1,384]{0,2,1:T(8,128)(2,1)S(1)} collective-permute-done((bf16[128,1,384]{0,2,1:T(8,128)(2,1)S(1)}, bf16[128,1,384]{0,2,1:T(8,128)(2,1)S(1)}, u32[]{:S(2)}, u32[]{:S(2)}) %collective-permute-start.28) | collective-permute-done | bytes 98336 | tf_op jit(solution)/shard_map/ppermute | solution.py:14
  132.6 1.6 %collective-permute-done.30 = bf16[128,4,1]{0,2,1:T(2,128)(2,1)S(1)} collective-permute-done((bf16[128,4,1]{0,2,1:T(2,128)(2,1)S(1)}, bf16[128,4,1]{0,2,1:T(2,128)(2,1)S(1)}, u32[]{:S(2)}, u32[]{:S(2)}) %collective-permute-start.30) | collective-permute-done | bytes 1056 | tf_op jit(solution)/shard_map/ppermute | solution.py:14
  138.6 3.2 %all-to-all-start.2 = ((bf16[8,2,128]{2,1,0:T(2,128)(2,1)}), bf16[8,2,128]{2,1,0:T(2,128)(2,1)S(1)}, u32[]{:S(2)}, u32[]{:S(2)}) async-start(bf16[8,2,128]{2,1,0:T(2,128)(2,1)} %bitcast.161), calls=%async_computation.2 | async-start | bytes 8192 | tf_op jit(solution)/shard_map/all_to_all | solution.py:77
  143.2 4.1 %all-to-all-done.2 = bf16[8,2,128]{2,1,0:T(2,128)(2,1)S(1)} async-done(((bf16[8,2,128]{2,1,0:T(2,128)(2,1)}), bf16[8,2,128]{2,1,0:T(2,128)(2,1)S(1)}, u32[]{:S(2)}, u32[]{:S(2)}) %all-to-all-start.2) | async-done | bytes 4128 | tf_op jit(solution)/shard_map/all_to_all | solution.py:77
  (198 shorter events, 59.3 us)
Async XLA Ops:
  1.9 6.2 %collective-permute-start = (bf16[48,1,384]{2,0,1:T(8,128)(2,1)S(1)}, bf16[48,1,384]{2,0,1:T(8,128)(2,1)S(1)}, u32[]{:S(2)}, u32[]{:S(2)}) collective-permute-start(bf16[48,1,384]{2,0,1:T(8,128)(2,1)S(1)} %copy.213), channel_id=1, source_target_pairs={{0,1},{1,4},{4,5},{5,8},{8,9},{9,12},{12,13},{13,0},{2,3},{3,6},{6... | collective-permute-start | bytes 110600 | tf_op jit(solution)/shard_map/ppermute | solution.py:14
  2.4 6.6 %collective-permute-start.1 = (bf16[48,1,384]{2,0,1:T(8,128)(2,1)S(1)}, bf16[48,1,384]{2,0,1:T(8,128)(2,1)S(1)}, u32[]{:S(2)}, u32[]{:S(2)}) collective-permute-start(bf16[48,1,384]{2,0,1:T(8,128)(2,1)S(1)} %copy.214), channel_id=1, source_target_pairs={{1,0},{4,1},{5,4},{8,5},{9,8},{12,9},{13,12},{0,13},{3,2},{6,3},{7... | collective-permute-start | bytes 110600 | tf_op jit(solution)/shard_map/ppermute | solution.py:16
  9.1 4.6 %collective-permute-start.2 = (bf16[48,4,1]{2,0,1:T(8,128)(2,1)S(1)}, bf16[48,4,1]{2,0,1:T(8,128)(2,1)S(1)}, u32[]{:S(2)}, u32[]{:S(2)}) collective-permute-start(bf16[48,4,1]{2,0,1:T(8,128)(2,1)S(1)} %get-tuple-element.34), channel_id=1, source_target_pairs={{0,2},{2,0},{1,3},{3,1},{4,6},{6,4},{5,7},{7,5},{8,10},{10,8},{9,1... | collective-permute-start | bytes 1160 | tf_op jit(solution)/shard_map/ppermute | solution.py:14
  11.2 4.1 %collective-permute-start.3 = (bf16[48,4,1]{2,0,1:T(8,128)(2,1)S(1)}, bf16[48,4,1]{2,0,1:T(8,128)(2,1)S(1)}, u32[]{:S(2)}, u32[]{:S(2)}) collective-permute-start(bf16[48,4,1]{2,0,1:T(8,128)(2,1)S(1)} %get-tuple-element.35), channel_id=1, source_target_pairs={{2,0},{0,2},{3,1},{1,3},{6,4},{4,6},{7,5},{5,7},{10,8},{8,10},{11,... | collective-permute-start | bytes 1160 | tf_op jit(solution)/shard_map/ppermute | solution.py:16
  19.5 8.3 %collective-permute-start.4 = (bf16[256,1,384]{0,2,1:T(8,128)(2,1)S(1)}, bf16[256,1,384]{0,2,1:T(8,128)(2,1)S(1)}, u32[]{:S(2)}, u32[]{:S(2)}) collective-permute-start(bf16[256,1,384]{0,2,1:T(8,128)(2,1)S(1)} %get-tuple-element.22), channel_id=1, source_target_pairs={{0,1},{1,4},{4,5},{5,8},{8,9},{9,12},{12,13},{13,0},{2,3},{3,6},{6... | collective-permute-start | bytes 589832 | tf_op jit(solution)/shard_map/ppermute | solution.py:14
  19.6 8.2 %collective-permute-start.5 = (bf16[256,1,384]{0,2,1:T(8,128)(2,1)S(1)}, bf16[256,1,384]{0,2,1:T(8,128)(2,1)S(1)}, u32[]{:S(2)}, u32[]{:S(2)}) collective-permute-start(bf16[256,1,384]{0,2,1:T(8,128)(2,1)S(1)} %get-tuple-element.23), channel_id=1, source_target_pairs={{1,0},{4,1},{5,4},{8,5},{9,8},{12,9},{13,12},{0,13},{3,2},{6,3},{7... | collective-permute-start | bytes 589832 | tf_op jit(solution)/shard_map/ppermute | solution.py:16
  27.8 3.7 %collective-permute-start.6 = (bf16[256,4,1]{0,2,1:T(2,128)(2,1)S(1)}, bf16[256,4,1]{0,2,1:T(2,128)(2,1)S(1)}, u32[]{:S(2)}, u32[]{:S(2)}) collective-permute-start(bf16[256,4,1]{0,2,1:T(2,128)(2,1)S(1)} %get-tuple-element.14), channel_id=1, source_target_pairs={{0,2},{2,0},{1,3},{3,1},{4,6},{6,4},{5,7},{7,5},{8,10},{10,8},{9,1... | collective-permute-start | bytes 6152 | tf_op jit(solution)/shard_map/ppermute | solution.py:14
  28.1 3.6 %collective-permute-start.7 = (bf16[256,4,1]{0,2,1:T(2,128)(2,1)S(1)}, bf16[256,4,1]{0,2,1:T(2,128)(2,1)S(1)}, u32[]{:S(2)}, u32[]{:S(2)}) collective-permute-start(bf16[256,4,1]{0,2,1:T(2,128)(2,1)S(1)} %get-tuple-element.15), channel_id=1, source_target_pairs={{2,0},{0,2},{3,1},{1,3},{6,4},{4,6},{7,5},{5,7},{10,8},{8,10},{11,... | collective-permute-start | bytes 6152 | tf_op jit(solution)/shard_map/ppermute | solution.py:16
  34.7 7.8 %collective-permute-start.8 = (bf16[48,1,384]{2,0,1:T(8,128)(2,1)S(1)}, bf16[48,1,384]{2,0,1:T(8,128)(2,1)S(1)}, u32[]{:S(2)}, u32[]{:S(2)}) collective-permute-start(bf16[48,1,384]{2,0,1:T(8,128)(2,1)S(1)} %get-tuple-element.40), channel_id=1, source_target_pairs={{0,1},{1,4},{4,5},{5,8},{8,9},{9,12},{12,13},{13,0},{2,3},{3,6},{6... | collective-permute-start | bytes 110600 | tf_op jit(solution)/shard_map/ppermute | solution.py:14
  34.7 7.7 %collective-permute-start.9 = (bf16[48,1,384]{2,0,1:T(8,128)(2,1)S(1)}, bf16[48,1,384]{2,0,1:T(8,128)(2,1)S(1)}, u32[]{:S(2)}, u32[]{:S(2)}) collective-permute-start(bf16[48,1,384]{2,0,1:T(8,128)(2,1)S(1)} %get-tuple-element.41), channel_id=1, source_target_pairs={{1,0},{4,1},{5,4},{8,5},{9,8},{12,9},{13,12},{0,13},{3,2},{6,3},{7... | collective-permute-start | bytes 110600 | tf_op jit(solution)/shard_map/ppermute | solution.py:16
  38.9 35.8 %all-to-all-start.1 = ((s32[8,1,2]{2,1,0:T(1,128)}), s32[8,1,2]{2,1,0:T(1,128)S(1)}, u32[]{:S(2)}, u32[]{:S(2)}) async-start(s32[8,1,2]{2,1,0:T(1,128)} %copy.143), calls=%async_computation.1 | async-start | bytes 8192 | tf_op jit(solution)/shard_map/all_to_all | solution.py:69
  42.5 4.2 %collective-permute-start.10 = (bf16[48,4,1]{2,0,1:T(8,128)(2,1)S(1)}, bf16[48,4,1]{2,0,1:T(8,128)(2,1)S(1)}, u32[]{:S(2)}, u32[]{:S(2)}) collective-permute-start(bf16[48,4,1]{2,0,1:T(8,128)(2,1)S(1)} %get-tuple-element.32), channel_id=1, source_target_pairs={{0,2},{2,0},{1,3},{3,1},{4,6},{6,4},{5,7},{7,5},{8,10},{10,8},{9,1... | collective-permute-start | bytes 1160 | tf_op jit(solution)/shard_map/ppermute | solution.py:14
  44.4 4.1 %collective-permute-start.11 = (bf16[48,4,1]{2,0,1:T(8,128)(2,1)S(1)}, bf16[48,4,1]{2,0,1:T(8,128)(2,1)S(1)}, u32[]{:S(2)}, u32[]{:S(2)}) collective-permute-start(bf16[48,4,1]{2,0,1:T(8,128)(2,1)S(1)} %get-tuple-element.33), channel_id=1, source_target_pairs={{2,0},{0,2},{3,1},{1,3},{6,4},{4,6},{7,5},{5,7},{10,8},{8,10},{11,... | collective-permute-start | bytes 1160 | tf_op jit(solution)/shard_map/ppermute | solution.py:16
  52.0 7.1 %collective-permute-start.12 = (bf16[256,1,384]{0,2,1:T(8,128)(2,1)S(1)}, bf16[256,1,384]{0,2,1:T(8,128)(2,1)S(1)}, u32[]{:S(2)}, u32[]{:S(2)}) collective-permute-start(bf16[256,1,384]{0,2,1:T(8,128)(2,1)S(1)} %get-tuple-element.20), channel_id=1, source_target_pairs={{0,1},{1,4},{4,5},{5,8},{8,9},{9,12},{12,13},{13,0},{2,3},{3,6},{6... | collective-permute-start | bytes 589832 | tf_op jit(solution)/shard_map/ppermute | solution.py:14
  52.0 7.0 %collective-permute-start.13 = (bf16[256,1,384]{0,2,1:T(8,128)(2,1)S(1)}, bf16[256,1,384]{0,2,1:T(8,128)(2,1)S(1)}, u32[]{:S(2)}, u32[]{:S(2)}) collective-permute-start(bf16[256,1,384]{0,2,1:T(8,128)(2,1)S(1)} %get-tuple-element.21), channel_id=1, source_target_pairs={{1,0},{4,1},{5,4},{8,5},{9,8},{12,9},{13,12},{0,13},{3,2},{6,3},{7... | collective-permute-start | bytes 589832 | tf_op jit(solution)/shard_map/ppermute | solution.py:16
  59.1 3.7 %collective-permute-start.14 = (bf16[256,4,1]{0,2,1:T(2,128)(2,1)S(1)}, bf16[256,4,1]{0,2,1:T(2,128)(2,1)S(1)}, u32[]{:S(2)}, u32[]{:S(2)}) collective-permute-start(bf16[256,4,1]{0,2,1:T(2,128)(2,1)S(1)} %get-tuple-element.12), channel_id=1, source_target_pairs={{0,2},{2,0},{1,3},{3,1},{4,6},{6,4},{5,7},{7,5},{8,10},{10,8},{9,1... | collective-permute-start | bytes 6152 | tf_op jit(solution)/shard_map/ppermute | solution.py:14
  74.7 9.0 %all-to-all-start = ((bf16[8,2,8,128]{3,2,1,0:T(8,128)(2,1)}), bf16[8,2,8,128]{3,2,1,0:T(8,128)(2,1)S(1)}, u32[]{:S(2)}, u32[]{:S(2)}) async-start(bf16[8,2,8,128]{3,2,1,0:T(8,128)(2,1)} %bitcast.80), calls=%async_computation | async-start | bytes 65536 | tf_op jit(solution)/shard_map/all_to_all | solution.py:68
  83.9 5.2 %collective-permute-start.16 = (bf16[48,1,384]{2,0,1:T(8,128)(2,1)S(1)}, bf16[48,1,384]{2,0,1:T(8,128)(2,1)S(1)}, u32[]{:S(2)}, u32[]{:S(2)}) collective-permute-start(bf16[48,1,384]{2,0,1:T(8,128)(2,1)S(1)} %get-tuple-element.38), channel_id=1, source_target_pairs={{0,1},{1,4},{4,5},{5,8},{8,9},{9,12},{12,13},{13,0},{2,3},{3,6},{6... | collective-permute-start | bytes 110600 | tf_op jit(solution)/shard_map/ppermute | solution.py:14
  84.0 5.2 %collective-permute-start.17 = (bf16[48,1,384]{2,0,1:T(8,128)(2,1)S(1)}, bf16[48,1,384]{2,0,1:T(8,128)(2,1)S(1)}, u32[]{:S(2)}, u32[]{:S(2)}) collective-permute-start(bf16[48,1,384]{2,0,1:T(8,128)(2,1)S(1)} %get-tuple-element.39), channel_id=1, source_target_pairs={{1,0},{4,1},{5,4},{8,5},{9,8},{12,9},{13,12},{0,13},{3,2},{6,3},{7... | collective-permute-start | bytes 110600 | tf_op jit(solution)/shard_map/ppermute | solution.py:16
  89.3 4.2 %collective-permute-start.18 = (bf16[48,4,1]{2,0,1:T(8,128)(2,1)S(1)}, bf16[48,4,1]{2,0,1:T(8,128)(2,1)S(1)}, u32[]{:S(2)}, u32[]{:S(2)}) collective-permute-start(bf16[48,4,1]{2,0,1:T(8,128)(2,1)S(1)} %get-tuple-element.30), channel_id=1, source_target_pairs={{0,2},{2,0},{1,3},{3,1},{4,6},{6,4},{5,7},{7,5},{8,10},{10,8},{9,1... | collective-permute-start | bytes 1160 | tf_op jit(solution)/shard_map/ppermute | solution.py:14
  90.3 4.1 %collective-permute-start.19 = (bf16[48,4,1]{2,0,1:T(8,128)(2,1)S(1)}, bf16[48,4,1]{2,0,1:T(8,128)(2,1)S(1)}, u32[]{:S(2)}, u32[]{:S(2)}) collective-permute-start(bf16[48,4,1]{2,0,1:T(8,128)(2,1)S(1)} %get-tuple-element.31), channel_id=1, source_target_pairs={{2,0},{0,2},{3,1},{1,3},{6,4},{4,6},{7,5},{5,7},{10,8},{8,10},{11,... | collective-permute-start | bytes 1160 | tf_op jit(solution)/shard_map/ppermute | solution.py:16
  97.3 6.2 %collective-permute-start.20 = (bf16[128,1,384]{0,2,1:T(8,128)(2,1)S(1)}, bf16[128,1,384]{0,2,1:T(8,128)(2,1)S(1)}, u32[]{:S(2)}, u32[]{:S(2)}) collective-permute-start(bf16[128,1,384]{0,2,1:T(8,128)(2,1)S(1)} %get-tuple-element.26), channel_id=1, source_target_pairs={{0,1},{1,4},{4,5},{5,8},{8,9},{9,12},{12,13},{13,0},{2,3},{3,6},{6... | collective-permute-start | bytes 294920 | tf_op jit(solution)/shard_map/ppermute | solution.py:14
  97.4 6.1 %collective-permute-start.21 = (bf16[128,1,384]{0,2,1:T(8,128)(2,1)S(1)}, bf16[128,1,384]{0,2,1:T(8,128)(2,1)S(1)}, u32[]{:S(2)}, u32[]{:S(2)}) collective-permute-start(bf16[128,1,384]{0,2,1:T(8,128)(2,1)S(1)} %get-tuple-element.27), channel_id=1, source_target_pairs={{1,0},{4,1},{5,4},{8,5},{9,8},{12,9},{13,12},{0,13},{3,2},{6,3},{7... | collective-permute-start | bytes 294920 | tf_op jit(solution)/shard_map/ppermute | solution.py:16
  103.5 3.7 %collective-permute-start.22 = (bf16[128,4,1]{0,2,1:T(2,128)(2,1)S(1)}, bf16[128,4,1]{0,2,1:T(2,128)(2,1)S(1)}, u32[]{:S(2)}, u32[]{:S(2)}) collective-permute-start(bf16[128,4,1]{0,2,1:T(2,128)(2,1)S(1)} %get-tuple-element.18), channel_id=1, source_target_pairs={{0,2},{2,0},{1,3},{3,1},{4,6},{6,4},{5,7},{7,5},{8,10},{10,8},{9,1... | collective-permute-start | bytes 3080 | tf_op jit(solution)/shard_map/ppermute | solution.py:14
  110.9 5.2 %collective-permute-start.24 = (bf16[48,1,384]{2,0,1:T(8,128)(2,1)S(1)}, bf16[48,1,384]{2,0,1:T(8,128)(2,1)S(1)}, u32[]{:S(2)}, u32[]{:S(2)}) collective-permute-start(bf16[48,1,384]{2,0,1:T(8,128)(2,1)S(1)} %get-tuple-element.36), channel_id=1, source_target_pairs={{0,1},{1,4},{4,5},{5,8},{8,9},{9,12},{12,13},{13,0},{2,3},{3,6},{6... | collective-permute-start | bytes 110600 | tf_op jit(solution)/shard_map/ppermute | solution.py:14
  111.0 5.2 %collective-permute-start.25 = (bf16[48,1,384]{2,0,1:T(8,128)(2,1)S(1)}, bf16[48,1,384]{2,0,1:T(8,128)(2,1)S(1)}, u32[]{:S(2)}, u32[]{:S(2)}) collective-permute-start(bf16[48,1,384]{2,0,1:T(8,128)(2,1)S(1)} %get-tuple-element.37), channel_id=1, source_target_pairs={{1,0},{4,1},{5,4},{8,5},{9,8},{12,9},{13,12},{0,13},{3,2},{6,3},{7... | collective-permute-start | bytes 110600 | tf_op jit(solution)/shard_map/ppermute | solution.py:16
  116.2 4.2 %collective-permute-start.26 = (bf16[48,4,1]{2,0,1:T(8,128)(2,1)S(1)}, bf16[48,4,1]{2,0,1:T(8,128)(2,1)S(1)}, u32[]{:S(2)}, u32[]{:S(2)}) collective-permute-start(bf16[48,4,1]{2,0,1:T(8,128)(2,1)S(1)} %get-tuple-element.28), channel_id=1, source_target_pairs={{0,2},{2,0},{1,3},{3,1},{4,6},{6,4},{5,7},{7,5},{8,10},{10,8},{9,1... | collective-permute-start | bytes 1160 | tf_op jit(solution)/shard_map/ppermute | solution.py:14
  117.3 4.1 %collective-permute-start.27 = (bf16[48,4,1]{2,0,1:T(8,128)(2,1)S(1)}, bf16[48,4,1]{2,0,1:T(8,128)(2,1)S(1)}, u32[]{:S(2)}, u32[]{:S(2)}) collective-permute-start(bf16[48,4,1]{2,0,1:T(8,128)(2,1)S(1)} %get-tuple-element.29), channel_id=1, source_target_pairs={{2,0},{0,2},{3,1},{1,3},{6,4},{4,6},{7,5},{5,7},{10,8},{8,10},{11,... | collective-permute-start | bytes 1160 | tf_op jit(solution)/shard_map/ppermute | solution.py:16
  124.2 6.2 %collective-permute-start.28 = (bf16[128,1,384]{0,2,1:T(8,128)(2,1)S(1)}, bf16[128,1,384]{0,2,1:T(8,128)(2,1)S(1)}, u32[]{:S(2)}, u32[]{:S(2)}) collective-permute-start(bf16[128,1,384]{0,2,1:T(8,128)(2,1)S(1)} %get-tuple-element.24), channel_id=1, source_target_pairs={{0,1},{1,4},{4,5},{5,8},{8,9},{9,12},{12,13},{13,0},{2,3},{3,6},{6... | collective-permute-start | bytes 294920 | tf_op jit(solution)/shard_map/ppermute | solution.py:14
  124.3 6.1 %collective-permute-start.29 = (bf16[128,1,384]{0,2,1:T(8,128)(2,1)S(1)}, bf16[128,1,384]{0,2,1:T(8,128)(2,1)S(1)}, u32[]{:S(2)}, u32[]{:S(2)}) collective-permute-start(bf16[128,1,384]{0,2,1:T(8,128)(2,1)S(1)} %get-tuple-element.25), channel_id=1, source_target_pairs={{1,0},{4,1},{5,4},{8,5},{9,8},{12,9},{13,12},{0,13},{3,2},{6,3},{7... | collective-permute-start | bytes 294920 | tf_op jit(solution)/shard_map/ppermute | solution.py:16
  130.5 3.7 %collective-permute-start.30 = (bf16[128,4,1]{0,2,1:T(2,128)(2,1)S(1)}, bf16[128,4,1]{0,2,1:T(2,128)(2,1)S(1)}, u32[]{:S(2)}, u32[]{:S(2)}) collective-permute-start(bf16[128,4,1]{0,2,1:T(2,128)(2,1)S(1)} %get-tuple-element.16), channel_id=1, source_target_pairs={{0,2},{2,0},{1,3},{3,1},{4,6},{6,4},{5,7},{7,5},{8,10},{10,8},{9,1... | collective-permute-start | bytes 3080 | tf_op jit(solution)/shard_map/ppermute | solution.py:14
  138.6 8.7 %all-to-all-start.2 = ((bf16[8,2,128]{2,1,0:T(2,128)(2,1)}), bf16[8,2,128]{2,1,0:T(2,128)(2,1)S(1)}, u32[]{:S(2)}, u32[]{:S(2)}) async-start(bf16[8,2,128]{2,1,0:T(2,128)(2,1)} %bitcast.161), calls=%async_computation.2 | async-start | bytes 8192 | tf_op jit(solution)/shard_map/all_to_all | solution.py:77
  (15 other events, 180.5 us)
where the time goes:
time: 149 us; the launch traced here: 148 us
  starting transfers between devices  56.4 us (38%)
  waiting for transfers between devices  49.4 us (33%)
  matrix products  31.6 us (21%)
  local copies, waits for them, and re-layouts  6.97 us (5%)
  other arithmetic  2.59 us (2%)
    ppermute x16, starting transfers between devices, with_halo(): lax.ppermute(head, axis, [((i + 1) % count, i) for i in range(count)])  35.9 us
    ppermute x16, waiting for transfers between devices, with_halo(): lax.ppermute(tail, axis, [(i, (i + 1) % count) for i in range(count)])  32.3 us
    dot_general x72, matrix products, apply_taps(): jnp.einsum('hc,crw->hrw', weights[row_tap * 3 + col_tap], window, preferr...  28.9 us
    ppermute x16, starting transfers between devices, with_halo(): lax.ppermute(tail, axis, [(i, (i + 1) % count) for i in range(count)])  10.6 us
    ppermute x16, waiting for transfers between devices, with_halo(): lax.ppermute(head, axis, [((i + 1) % count, i) for i in range(count)])  8.68 us
    all_to_all x1, waiting for transfers between devices, send_fluxes(): lax.all_to_all(block_values, ('lat', 'comp'), split_axis=0, concat_axis=0...  4.38 us
    all_to_all x1, waiting for transfers between devices, send_back(): lax.all_to_all(block_values, ('lat', 'comp'), split_axis=0, concat_axis=0...  4.11 us
    all_to_all x1, starting transfers between devices, send_fluxes(): lax.all_to_all(block_values, ('lat', 'comp'), split_axis=0, concat_axis=0...  3.34 us
  transfers between devices with their start and end apart: 35, of which 25 were waited for; matrix products, arithmetic and copies ran while one was open for 13% of the time, Pallas kernels for 0%

commit v1 on v0

--- a/solution.py
+++ b/solution.py
@@ -1,7 +1,16 @@
+import functools
+
 import jax
 import jax.numpy as jnp
 from jax import lax
+from jax.experimental import pallas as pl
+from jax.experimental.pallas import tpu as pltpu
 from jax.sharding import PartitionSpec as P
+
+BF = jnp.bfloat16
+F32 = jnp.float32
+EDGE = 8
+STRIP = 4 * EDGE
 
 
 def with_halo(cells, sides, width):
@@ -156,6 +165,462 @@
     return (atmosphere_model, ocean_model, surface_temp_grid.reshape(block_height, block_breadth))
 
 
+def gelu(v):
+    u = v * (0.7978845608 + 0.0356774081 * (v * v))
+    half = 0.5 * v
+    return half + half * jnp.tanh(u)
+
+
+def west(v):
+    return pltpu.roll(v, 1, 1)
+
+
+def east(v):
+    return pltpu.roll(v, v.shape[1] - 1, 1)
+
+
+def store_row(s_ref, slot, row, chans):
+    base = slot * 3 * chans
+    if not isinstance(base, int):
+        base = pl.multiple_of(base, 16)
+    taps = jnp.concatenate([west(row), row, east(row)], axis=0).astype(BF)
+    s_ref[pl.ds(base, 3 * chans), :] = taps
+
+
+def clear_ends(s_ref, rows, chans):
+    zero = jnp.zeros((3 * chans, s_ref.shape[1]), BF)
+    s_ref[0 : 3 * chans, :] = zero
+    s_ref[(rows + 1) * 3 * chans : (rows + 2) * 3 * chans, :] = zero
+
+
+def column_sum(z, outs):
+    return z[outs : 2 * outs] + west(z[0:outs]) + east(z[2 * outs : 3 * outs])
+
+
+def main_block(s_ref, w_in, w_out, chans, outs, rows, width, emit):
+    span = 9 * chans
+    ahead, behind = None, None
+    for pair in range(rows // 2):
+        r = 2 * pair
+        taps = jnp.concatenate(
+            [
+                s_ref[r * 3 * chans : r * 3 * chans + span, :],
+                s_ref[(r + 1) * 3 * chans : (r + 1) * 3 * chans + span, :],
+            ],
+            axis=1,
+        )
+        hidden = gelu(jnp.dot(w_in, taps, preferred_element_type=F32)).astype(BF)
+        z = jnp.dot(w_out, hidden, preferred_element_type=F32)
+        part = [
+            [z[a * 3 * outs : (a + 1) * 3 * outs, q * width : (q + 1) * width] for q in range(2)]
+            for a in range(3)
+        ]
+        if pair > 0:
+            emit(r - 1, column_sum(ahead + part[2][0], outs))
+            now = behind + part[1][0] + part[2][1]
+        else:
+            now = part[1][0] + part[2][1]
+        emit(r, column_sum(now, outs))
+        ahead = part[0][0] + part[1][1]
+        behind = part[0][1]
+    emit(rows - 1, column_sum(ahead, outs))
+
+
+def lanes_of(shape):
+    return lax.broadcasted_iota(jnp.int32, shape, len(shape) - 1)
+
+
+def edges_of(rows):
+    shape = (rows[0].shape[0], 128)
+    lane = lanes_of(shape)
+    total = jnp.zeros(shape, F32)
+    for i, row in enumerate(rows):
+        at = i * STRIP + EDGE
+        left = pltpu.roll(row[:, 0:128], at, 1)
+        total = jnp.where((lane >= at) & (lane < at + EDGE), left, total)
+        at = at + EDGE
+        width = row.shape[1]
+        right = pltpu.roll(row[:, width - 128 : width], (at + EDGE) % 128, 1)
+        total = jnp.where((lane >= at) & (lane < at + EDGE), right, total)
+    return total
+
+
+def with_neighbour(own, other):
+    place = lanes_of(own.shape) % STRIP
+    left = pltpu.roll(other, 128 - 2 * EDGE, 1)
+    right = pltpu.roll(other, 2 * EDGE, 1)
+    return jnp.where(place < EDGE, left, jnp.where(place >= 3 * EDGE, right, own))
+
+
+def strip_shift(v, a, b):
+    width = v.shape[1]
+    moved = pltpu.roll(v, (-((a - 1) * STRIP + b - 1)) % width, 1) if (a, b) != (1, 1) else v
+    lane = lanes_of(v.shape)
+    if a == 0:
+        moved = jnp.where(lane < STRIP, 0.0, moved)
+    if a == 2:
+        moved = jnp.where(lane >= width - STRIP, 0.0, moved)
+    return moved
+
+
+def strip_block(source, w_in, w_out, outs):
+    taps = jnp.concatenate(
+        [strip_shift(source, a, b) for a in range(3) for b in range(3)], axis=0
+    ).astype(BF)
+    hidden = gelu(jnp.dot(w_in, taps, preferred_element_type=F32)).astype(BF)
+    z = jnp.dot(w_out, hidden, preferred_element_type=F32)
+    total = z[4 * outs : 5 * outs]
+    for tap in range(9):
+        if tap != 4:
+            total = total + strip_shift(z[tap * outs : (tap + 1) * outs], tap // 3, tap % 3)
+    return total
+
+
+def mend_row(row, strip, r):
+    width = row.shape[1]
+    at = (r % 4) * STRIP + EDGE
+    lane = lanes_of((row.shape[0], 128))
+    left = pltpu.roll(strip, (-at) % 128, 1)
+    right = pltpu.roll(strip, (-(at + 2 * EDGE)) % 128, 1)
+    head = jnp.where(lane < 4, left, row[:, 0:128])
+    tail = jnp.where(lane >= 124, right, row[:, width - 128 : width])
+    return jnp.concatenate([head, row[:, 128 : width - 128], tail], axis=1)
+
+
+def edge_kernel(place_ref, *refs):
+    tiles, out_ref = refs[:-1], refs[-1]
+    lat, comp = place_ref[0], place_ref[1]
+    count = len(tiles) // 2
+    for k in range(count):
+        near = edges_of([tiles[k][r].astype(F32) for r in range(2)])
+        far = edges_of([tiles[count + k][r].astype(F32) for r in range(2)])
+        both = pltpu.roll(near, 64 * comp, 1) + pltpu.roll(far, 64 * (1 - comp), 1)
+        out_ref[lat ^ k] = both.astype(BF)
+
+
+def atmos_kernel(place_ref, *refs):
+    tiles, (win_ref, wout_ref, out_ref, s0_ref, s1_ref) = refs[:8], refs[8:]
+    lat, comp = place_ref[0], place_ref[1]
+    rows, chans, width = out_ref.shape
+    clear_ends(s0_ref, rows, chans)
+    clear_ends(s1_ref, rows, chans)
+    for i, tile in enumerate(tiles):
+        base = 4 * (lat ^ (i % 4)) + 2 * (comp if i < 4 else 1 - comp)
+        for r in range(2):
+            store_row(s0_ref, base + r + 1, tile[r].astype(F32), chans)
+    stacks = (s0_ref, s1_ref)
+    layers = win_ref.shape[0]
+    for layer in range(layers):
+        source = stacks[layer % 2]
+
+        def emit(r, y):
+            base = (3 * (r + 1) + 1) * chans
+            total = source[base : base + chans, :].astype(F32) + y
+            if layer == layers - 1:
+                out_ref[r] = total.astype(BF)
+            else:
+                store_row(stacks[(layer + 1) % 2], r + 1, total.astype(BF).astype(F32), chans)
+
+        main_block(source, win_ref[layer], wout_ref[layer], chans, chans, rows, width, emit)
+
+
+def flux_kernel(place_ref, own_ref, other_ref, main_ref, win_ref, wout_ref, proj_ref, blocks_ref,
+                *refs):
+    tiles = refs[:8]
+    next_ref, field_ref, extra_ref, edge_ref, merged, flux, total, table, index, sem = refs[8:]
+    lat, comp = place_ref[0], place_ref[1]
+    rows, chans, width = main_ref.shape
+    fluxes = proj_ref.shape[0]
+    per_row = width // 128
+    subs = 2 * per_row
+    slots = 2 * rows // 2
+
+    for i, tile in enumerate(tiles):
+        t = 2 * (lat ^ (i % 4)) + (comp if i < 4 else 1 - comp)
+        row = tile[0, 32:48, 0:128].astype(F32)[9:10]
+        table[pl.ds(t, 1), :] = row.astype(jnp.int32)
+    copy = pltpu.make_async_copy(table, index, sem)
+    copy.start()
+
+    strip = jnp.concatenate(
+        [
+            with_neighbour(own_ref[q].astype(F32), other_ref[q].astype(F32))
+            for q in range(own_ref.shape[0])
+        ],
+        axis=1,
+    )
+    for layer in range(win_ref.shape[0]):
+        strip = strip + strip_block(strip, win_ref[layer], wout_ref[layer], chans)
+        strip = strip.astype(BF).astype(F32)
+
+    for r in range(rows):
+        q = r // 4
+        row = mend_row(main_ref[r].astype(F32), strip[:, 128 * q : 128 * (q + 1)], r).astype(BF)
+        merged[r] = row
+        f = jnp.dot(proj_ref[...], row, preferred_element_type=F32)
+        for b in range(per_row):
+            flux[(r // 2) * subs + (r % 2) * per_row + b] = f[:, 128 * b : 128 * (b + 1)].astype(
+                BF
+            ).astype(F32)
+    base = 4 * lat + 2 * comp
+    for r in range(2):
+        next_ref[r] = merged[base + r]
+
+    total[...] = jnp.zeros(total.shape, F32)
+    copy.wait()
+
+    def one_tile(t, carry):
+        for slot in range(slots):
+            source = index[t, slot]
+            live = source >= 0
+            target = jnp.where(live, index[t, slots + slot], 6)
+            block = blocks_ref[index[t, 2 * slots + slot]]
+            value = flux[t * subs + jnp.maximum(source, 0)].astype(BF)
+            piece = jnp.dot(value, block, preferred_element_type=F32)
+            at = (slot // 2) * 8 + target
+            total[at] = total[at] + piece.astype(BF).astype(F32)
+        return carry
+
+    lax.fori_loop(0, rows // 2, one_tile, 0)
+
+    for i, tile in enumerate(tiles):
+        t = 2 * (lat ^ (i % 4)) + (comp if i < 4 else 1 - comp)
+        ends = []
+        for r in range(2):
+            arrived = jnp.concatenate(
+                [total[8 * t + r * per_row + b] for b in range(per_row)], axis=1
+            )
+            state = tile[r].astype(F32)
+            outs = state.shape[0] - fluxes
+            row = jnp.concatenate([state[0:outs], arrived], axis=0)
+            field_ref[2 * t + r] = row.astype(BF)
+            extra_ref[2 * t + r] = state[outs:]
+            ends.append(jnp.concatenate([row, state[outs:]], axis=0))
+        both = edges_of(ends)
+        half = comp if i < 4 else 1 - comp
+        edge_ref_at = lat ^ (i % 4)
+        moved = pltpu.roll(both, 64 * half, 1)
+        if i < 4:
+            edge_ref[edge_ref_at] = moved.astype(BF)
+        else:
+            edge_ref[edge_ref_at] = (edge_ref[edge_ref_at].astype(F32) + moved).astype(BF)
+
+
+def ocean_kernel(field_ref, extra_ref, win_ref, wout_ref, out_ref, s0_ref, s1_ref):
+    rows, chans, width = field_ref.shape
+    outs = out_ref.shape[1]
+    clear_ends(s0_ref, rows, chans)
+    clear_ends(s1_ref, rows, chans)
+    for r in range(rows):
+        store_row(s0_ref, r + 1, field_ref[r].astype(F32), chans)
+    stacks = (s0_ref, s1_ref)
+    layers = win_ref.shape[0]
+    for layer in range(layers):
+        source = stacks[layer % 2]
+
+        def emit(r, y):
+            base = (3 * (r + 1) + 1) * chans
+            state = source[base : base + chans, :].astype(F32)
+            wet = extra_ref[r, 0:1, :]
+            total = wet * (state[0:outs] + y)
+            if layer == layers - 1:
+                out_ref[r] = total.astype(BF)
+            else:
+                row = jnp.concatenate([total.astype(BF).astype(F32), state[outs:]], axis=0)
+                store_row(stacks[(layer + 1) % 2], r + 1, row, chans)
+
+        main_block(source, win_ref[layer], wout_ref[layer], chans, outs, rows, width, emit)
+
+
+def finish_kernel(place_ref, slots_ref, own_ref, other_ref, main_ref, win_ref, wout_ref, blocks_ref,
+                  next_ref, temp_ref, surface, total):
+    lat, comp = place_ref[0], place_ref[1]
+    rows, outs, width = main_ref.shape
+    chans = win_ref.shape[2] // 9
+    per_row = width // 128
+    strip = jnp.concatenate(
+        [
+            with_neighbour(own_ref[q].astype(F32), other_ref[q].astype(F32))
+            for q in range(own_ref.shape[0])
+        ],
+        axis=1,
+    )
+    wet = strip[chans : chans + 1]
+    state, fixed = strip[0:outs], strip[outs:chans]
+    for layer in range(win_ref.shape[0]):
+        source = jnp.concatenate([state, fixed], axis=0)
+        state = wet * (state + strip_block(source, win_ref[layer], wout_ref[layer], outs))
+        state = state.astype(BF).astype(F32)
+
+    for r in range(rows):
+        q = r // 4
+        top = mend_row(main_ref[r, 0:16, :].astype(F32)[0:8], state[0:8, 128 * q : 128 * (q + 1)], r)
+        for b in range(per_row):
+            surface[(r // 2) * 8 + (r % 2) * per_row + b] = top[:, 128 * b : 128 * (b + 1)]
+
+    base = 4 * lat + 2 * comp
+    own = jnp.zeros((outs, 128), F32)
+    for q in range(own_ref.shape[0]):
+        own = jnp.where(lat == q, state[:, 128 * q : 128 * (q + 1)], own)
+    own = pltpu.roll(own, jnp.where(comp == 1, 64, 0), 1)
+    for r in range(2):
+        next_ref[r] = mend_row(main_ref[base + r].astype(F32), own, r).astype(BF)
+
+    total[...] = jnp.zeros(total.shape, F32)
+    slots = slots_ref.shape[1]
+    for slot in range(slots):
+        source = slots_ref[0, slot]
+        target = slots_ref[1, slot]
+        block = blocks_ref[slots_ref[2, slot]]
+        value = surface[(slot // 2) * 8 + target].astype(BF)
+        piece = lax.dot_general(value, block, (((1,), (1,)), ((), ())), preferred_element_type=F32)
+        at = jnp.where(source >= 0, source, 6)
+        total[at] = total[at] + piece
+    for r in range(2):
+        temp_ref[r : r + 1, :] = jnp.concatenate(
+            [total[r * per_row + b][0:1] for b in range(per_row)], axis=1
+        )
+
+
+def call(kernel, out_shape, operands, scratch=(), smem=1, flops=0):
+    specs = [
+        pl.BlockSpec(memory_space=pltpu.SMEM if i < smem else pltpu.VMEM)
+        for i in range(len(operands))
+    ]
+    out_specs = jax.tree.map(lambda _: pl.BlockSpec(memory_space=pltpu.VMEM), out_shape)
+    return pl.pallas_call(
+        kernel,
+        out_shape=out_shape,
+        in_specs=specs,
+        out_specs=out_specs,
+        scratch_shapes=list(scratch),
+        compiler_params=pltpu.CompilerParams(vmem_limit_bytes=40 * 2**20),
+        cost_estimate=pl.CostEstimate(flops=flops, bytes_accessed=2**20, transcendentals=0),
+    )(*operands)
+
+
+def column_device(
+    atmos_state,
+    ocean_state,
+    ocean_mask,
+    atmos_in_w,
+    atmos_out_w,
+    ocean_in_w,
+    ocean_out_w,
+    flux_proj,
+    regrid_blocks,
+    regrid_source_block,
+    regrid_target_block,
+    regrid_weight_block,
+):
+    chans, height, width = atmos_state.shape
+    outs = ocean_state.shape[0]
+    lats = lax.axis_size("lat")
+    tiles = lats * lax.axis_size("comp")
+    rows = tiles * height
+    layers, _, hidden_a, _ = atmos_in_w.shape
+    hidden_o = ocean_in_w.shape[2]
+    fluxes = flux_proj.shape[0]
+    place = jnp.stack([lax.axis_index("lat"), lax.axis_index("comp")]).astype(jnp.int32)
+
+    def far(v, k):
+        return lax.ppermute(v, "lat", [(i, i ^ k) for i in range(lats)])
+
+    def swap(v, axis):
+        return lax.ppermute(v, axis, [(0, 1), (1, 0)])
+
+    def column(mine):
+        near = [mine] + [far(mine, k) for k in range(1, lats)]
+        return near + [swap(v, "comp") for v in near]
+
+    atmos = column(jnp.transpose(atmos_state, (1, 0, 2)))
+
+    slots = jnp.stack(
+        [
+            v.reshape(-1)
+            for v in (regrid_source_block, regrid_target_block, regrid_weight_block)
+        ]
+    )
+    index_row = jnp.pad(slots.reshape(-1).astype(BF), (0, width - slots.size))
+    wet = ocean_mask.astype(BF)[:, None, :]
+    payload = jnp.concatenate(
+        [
+            jnp.transpose(ocean_state, (1, 0, 2)) * wet,
+            wet,
+            jnp.broadcast_to(index_row[None, None], (height, 1, width)),
+            jnp.zeros((height, 6, width), BF),
+        ],
+        axis=1,
+    )
+    ocean = column(payload)
+
+    def taps_in(w):
+        return jnp.transpose(w, (0, 2, 1, 3)).reshape(w.shape[0], w.shape[2], 9 * w.shape[3])
+
+    def taps_out(w):
+        return w.reshape(w.shape[0], 9 * w.shape[2], w.shape[3])
+
+    win_a, wout_a = taps_in(atmos_in_w), taps_out(atmos_out_w)
+    win_o, wout_o = taps_in(ocean_in_w), taps_out(ocean_out_w)
+
+    def conv_flops(hidden, outs):
+        return 2 * layers * rows * width * 9 * hidden * (chans + outs)
+
+    edges = call(edge_kernel, jax.ShapeDtypeStruct((lats, chans, 128), BF), [place, *atmos])
+    edges_other = swap(edges, "lon")
+    stack = (rows + 2) * 3 * chans
+    main = call(
+        atmos_kernel,
+        jax.ShapeDtypeStruct((rows, chans, width), BF),
+        [place, *atmos, win_a, wout_a],
+        [pltpu.VMEM((stack, width), BF), pltpu.VMEM((stack, width), BF)],
+        flops=conv_flops(hidden_a, chans),
+    )
+    subs = height * width // 128
+    atmos_next, field, extra, ocean_edges = call(
+        flux_kernel,
+        (
+            jax.ShapeDtypeStruct((height, chans, width), BF),
+            jax.ShapeDtypeStruct((rows, chans, width), BF),
+            jax.ShapeDtypeStruct((rows, fluxes, width), F32),
+            jax.ShapeDtypeStruct((lats, chans + fluxes, 128), BF),
+        ),
+        [place, edges, edges_other, main, win_a, wout_a, flux_proj, regrid_blocks, *ocean],
+        [
+            pltpu.VMEM((rows, chans, width), BF),
+            pltpu.VMEM((tiles * subs, fluxes, 128), F32),
+            pltpu.VMEM((tiles * 8, fluxes, 128), F32),
+            pltpu.VMEM((tiles, 128), jnp.int32),
+            pltpu.SMEM((tiles, 128), jnp.int32),
+            pltpu.SemaphoreType.DMA,
+        ],
+    )
+    ocean_edges_other = swap(ocean_edges, "lon")
+    ocean_main = call(
+        ocean_kernel,
+        jax.ShapeDtypeStruct((rows, outs, width), BF),
+        [field, extra, win_o, wout_o],
+        [pltpu.VMEM((stack, width), BF), pltpu.VMEM((stack, width), BF)],
+        smem=0,
+        flops=conv_flops(hidden_o, outs),
+    )
+    ocean_next, surface_temp = call(
+        finish_kernel,
+        (
+            jax.ShapeDtypeStruct((height, outs, width), BF),
+            jax.ShapeDtypeStruct((height, width), F32),
+        ),
+        [place, slots, ocean_edges, ocean_edges_other, ocean_main, win_o, wout_o, regrid_blocks],
+        [pltpu.VMEM((tiles * 8, 8, 128), F32), pltpu.VMEM((8, 8, 128), F32)],
+        smem=2,
+    )
+    return (
+        jnp.transpose(atmos_next, (1, 0, 2)),
+        jnp.transpose(ocean_next, (1, 0, 2)),
+        surface_temp,
+    )
+
+
 def solution(mesh):
     in_specs = (
         P(None, ("grp", "lat", "comp"), "lon"),
@@ -176,6 +641,12 @@
         P(None, ("grp", "lat", "comp"), "lon"),
         P(("grp", "lat", "comp"), "lon"),
     )
+    shape = mesh.shape
+    short = (shape["lat"], shape["comp"], shape["lon"]) == (4, 2, 2)
     return jax.shard_map(
-        per_device, mesh=mesh, in_specs=in_specs, out_specs=out_specs, check_vma=False
-    )
+        column_device if short else per_device,
+        mesh=mesh,
+        in_specs=in_specs,
+        out_specs=out_specs,
+        check_vma=False,
+    )

time: 149 us -> 56.6 us (0.38)
  waiting for transfers between devices: 49.4 us -> 5.46 us
  starting transfers between devices: 56.4 us -> 13.6 us
  matrix products: 31.6 us -> 0 us
  Pallas kernels: 0 us -> 26.7 us
    ppermute x32 -> x16, waiting for transfers between devices: 40.9 us -> 5.46 us  [the longest x6 5.43 us: far(): return lax.ppermute(v, 'lat', [(i, i ^ k) for i in range(lats)])]
    ppermute x32 -> x16, starting transfers between devices: 46.5 us -> 13.6 us  [the longest x6 10.2 us: far(): return lax.ppermute(v, 'lat', [(i, i ^ k) for i in range(lats)])]
    dot_general x79 -> x0, matrix products: 31.6 us -> none  [the longest x72 28.9 us: apply_taps(): jnp.einsum('hc,crw->hrw', weights[row_tap * 3 + col_tap], window, preferr...]
    pallas_call x0 -> x5, Pallas kernels: none -> 26.7 us  [call(): pl.pallas_call(kernel, out_shape=out_shape, in_specs=specs, out_specs=out...]
    all_to_all x3 -> x0, starting transfers between devices: 9.88 us -> none  [the longest x1 3.34 us: send_fluxes(): lax.all_to_all(block_values, ('lat', 'comp'), split_axis=0, concat_axis=0...]
    all_to_all x3 -> x0, waiting for transfers between devices: 8.49 us -> none  [the longest x1 4.38 us: send_fluxes(): lax.all_to_all(block_values, ('lat', 'comp'), split_axis=0, concat_axis=0...]
    unnamed x32 -> x14, local copies, waits for them, and re-layouts: 2.51 us -> 4.59 us
    select_n x9 -> x0, other arithmetic: 1.71 us -> none  [the longest x8 1.71 us: clear_poles(): return jnp.where(outside[None, :, None], jnp.zeros((), wide.dtype), wide)]
  transfers between devices with their start and end apart: 35 -> 16, of which waited for: 25 -> 2; matrix products, arithmetic and copies ran while one was open for 13% -> 14% of each run, Pallas kernels for 0% -> 31%
where the time goes in v1:
time: 56.6 us; the launch traced here: 56.2 us
  Pallas kernels  26.7 us (47%)
  starting transfers between devices  13.6 us (24%)
  local copies, waits for them, and re-layouts  7.3 us (13%)
  waiting for transfers between devices  5.46 us (10%)
  other arithmetic  2.4 us (4%)
  between operations  0.81 us (1%)
    pallas_call x5, Pallas kernels, call(): pl.pallas_call(kernel, out_shape=out_shape, in_specs=specs, out_specs=out...  26.7 us
    ppermute x6, starting transfers between devices, far(): return lax.ppermute(v, 'lat', [(i, i ^ k) for i in range(lats)])  10.2 us
    ppermute x6, waiting for transfers between devices, far(): return lax.ppermute(v, 'lat', [(i, i ^ k) for i in range(lats)])  5.43 us
    unnamed x14, local copies, waits for them, and re-layouts  4.59 us
    ppermute x10, starting transfers between devices, swap(): return lax.ppermute(v, axis, [(0, 1), (1, 0)])  3.38 us
    reshape x2, local copies, waits for them, and re-layouts, taps_in(): jnp.transpose(w, (0, 2, 1, 3))  2.29 us
  transfers between devices with their start and end apart: 16, of which 2 were waited for; matrix products, arithmetic and copies ran while one was open for 14% of the time, Pallas kernels for 31%

profile of v1, /device:TPU:0, one launch (start us, length us, event | category | flops | bytes accessed | tf_op | source)
XLA Modules:
  0.0 56.2 jit_solution(16189236402799118089)
XLA Ops:
  0.6 0.9 %copy.40 = bf16[48,2,384]{2,0,1:T(8,128)(2,1)S(1)} copy(bf16[48,2,384]{2,1,0:T(2,128)(2,1)} %param.12) | data formatting | bytes 147456 | tf_op args[0]
  1.6 3.1 %collective-permute-start = (bf16[2,48,384]{2,1,0:T(8,128)(2,1)S(1)}, bf16[2,48,384]{2,1,0:T(8,128)(2,1)S(1)}, u32[]{:S(2)}, u32[]{:S(2)}) collective-permute-start(bf16[2,48,384]{2,1,0:T(8,128)(2,1)S(1)} %bitcast.27), channel_id=1, source_target_pairs={{0,4},{4,0},{8,12},{12,8},{1,5},{5,1},{9,13},{13,9},{2,6},{6,2},{1... | collective-permute-start | bytes 221192 | tf_op jit(solution)/shard_map/ppermute | solution.py:527
  4.7 2.6 %collective-permute-start.1 = (bf16[2,48,384]{2,1,0:T(8,128)(2,1)S(1)}, bf16[2,48,384]{2,1,0:T(8,128)(2,1)S(1)}, u32[]{:S(2)}, u32[]{:S(2)}) collective-permute-start(bf16[2,48,384]{2,1,0:T(8,128)(2,1)S(1)} %bitcast.28), channel_id=1, source_target_pairs={{0,8},{4,12},{8,0},{12,4},{1,9},{5,13},{9,1},{13,5},{2,10},{6,14},... | collective-permute-start | bytes 221192 | tf_op jit(solution)/shard_map/ppermute | solution.py:527
  7.3 0.7 %convert_element_type.11 = bf16[2,384]{1,0:T(2,128)(2,1)S(1)} convert(s32[2,384]{1,0:T(2,128)} %param.14) | non-fusion elementwise | flops 768 | bytes 4608 | tf_op jit(solution)/shard_map/convert_element_type | solution.py:545
  8.0 0.7 %convert_bitcast_fusion = bf16[2,1,384]{2,0,1:T(2,128)(2,1)S(1)} fusion(s32[2,384]{1,0:T(2,128)} %param.14), kind=kLoop, calls=%fused_computation.7 | loop fusion | flops 768 | bytes 4608 | tf_op jit(solution)/shard_map/broadcast_in_dim | solution.py:545
  8.7 0.8 %copy.28 = s32[1,1,8,2]{3,2,1,0:T(8,128)S(1)} copy(s32[1,1,8,2]{2,3,1,0:T(2,128)} %param.22) | data formatting | bytes 128 | tf_op args[10]
  9.4 0.1 stack_reshape.10
  9.5 0.8 %copy.29 = s32[1,1,8,2]{3,2,1,0:T(8,128)S(1)} copy(s32[1,1,8,2]{2,3,1,0:T(2,128)} %param.23) | data formatting | bytes 128 | tf_op args[11]
  10.2 0.1 stack_reshape.11
  10.3 0.8 %copy.27 = s32[1,1,8,2]{3,2,1,0:T(8,128)S(1)} copy(s32[1,1,8,2]{2,3,1,0:T(2,128)} %param.21) | data formatting | bytes 128 | tf_op args[9]
  11.1 0.1 stack_reshape.9
  11.2 0.1 convert_element_type.13
  11.3 0.8 %fusion = bf16[2,40,384]{2,1,0:T(8,128)(2,1)S(1)} fusion(bf16[40,2,384]{2,1,0:T(2,128)(2,1)} %param.13, bf16[2,384]{1,0:T(2,128)(2,1)S(1)} %convert_element_type.11), kind=kLoop, calls=%fused_computation.3 | loop fusion | flops 30720 | bytes 124416 | tf_op jit(solution)/shard_map/mul | solution.py:548
  12.2 0.1 maximum_maximum_fusion.refs_0_
  12.3 1.0 %collective-permute-start.8 = (bf16[2,48,384]{2,1,0:T(8,128)(2,1)S(1)}, bf16[2,48,384]{2,1,0:T(8,128)(2,1)S(1)}, u32[]{:S(2)}, u32[]{:S(2)}) collective-permute-start(bf16[2,48,384]{2,1,0:T(8,128)(2,1)S(1)} %maximum_maximum_fusion.refs_0_), channel_id=1, source_target_pairs={{0,4},{4,0},{8,12},{12,8},{1,5},{5,1},{9,13},{13,9},{2,6},{6,2},{1... | collective-permute-start | bytes 221192 | tf_op jit(solution)/shard_map/ppermute | solution.py:527
  13.3 1.2 %copy.25.refs_8_.win_ref = bf16[2,256,432]{2,1,0:T(8,128)(2,1)S(1)} copy(bf16[2,256,432]{1,2,0:T(8,128)(2,1)} %bitcast.37) | data formatting | bytes 884736 | tf_op jit(solution)/shard_map/reshape | solution.py:558
  14.5 1.1 %copy.32.win_ref = bf16[2,128,432]{2,1,0:T(8,128)(2,1)S(1)} copy(bf16[2,128,432]{1,2,0:T(8,128)(2,1)} %bitcast.38) | data formatting | bytes 442368 | tf_op jit(solution)/shard_map/reshape | solution.py:558
  15.6 3.6 %collective-permute-start.9 = (bf16[2,48,384]{2,1,0:T(8,128)(2,1)S(1)}, bf16[2,48,384]{2,1,0:T(8,128)(2,1)S(1)}, u32[]{:S(2)}, u32[]{:S(2)}) collective-permute-start(bf16[2,48,384]{2,1,0:T(8,128)(2,1)S(1)} %maximum_maximum_fusion.refs_0_), channel_id=1, source_target_pairs={{0,8},{4,12},{8,0},{12,4},{1,9},{5,13},{9,1},{13,5},{2,10},{6,14},... | collective-permute-start | bytes 221192 | tf_op jit(solution)/shard_map/ppermute | solution.py:527
  19.2 0.5 collective-permute-start.5
  19.7 0.1 collective-permute-start.6
  19.9 3.3 %collective-permute-done.9.refs_2_ = bf16[2,48,384]{2,1,0:T(8,128)(2,1)S(1)} collective-permute-done((bf16[2,48,384]{2,1,0:T(8,128)(2,1)S(1)}, bf16[2,48,384]{2,1,0:T(8,128)(2,1)S(1)}, u32[]{:S(2)}, u32[]{:S(2)}) %collective-permute-start.9) | collective-permute-done | bytes 73760 | tf_op jit(solution)/shard_map/ppermute | solution.py:527
  23.2 2.2 %collective-permute-done.10.refs_3_ = bf16[2,48,384]{2,1,0:T(8,128)(2,1)S(1)} collective-permute-done((bf16[2,48,384]{2,1,0:T(8,128)(2,1)S(1)}, bf16[2,48,384]{2,1,0:T(8,128)(2,1)S(1)}, u32[]{:S(2)}, u32[]{:S(2)}) %collective-permute-start.10) | collective-permute-done | bytes 73760 | tf_op jit(solution)/shard_map/ppermute | solution.py:527
  25.4 0.5 collective-permute-start.13
  25.9 0.9 %shard_map.139.own_ref = bf16[4,48,128]{2,1,0:T(8,128)(2,1)S(1)} custom-call(s32[2]{0:T(128)S(1)} %pad_add_fusion.1.place_ref, bf16[2,48,384]{2,1,0:T(8,128)(2,1)S(1)} %bitcast.31, bf16[2,48,384]{2,1,0:T(8,128)(2,1)S(1)} %collective-permute-done.refs_1_, bf16[2,48,384]{2,1,0:T(8,128)(2,1)S(1)} %collective-permute-done.1.refs_2_, ...), custom_call_target="tpu_custom_call" | custom-call | bytes 1048576 | tf_op jit(solution)/shard_map/pallas_call | solution.py:491
  26.8 1.5 %collective-permute-start.7 = (bf16[4,48,128]{2,1,0:T(8,128)(2,1)S(1)}, bf16[4,48,128]{2,1,0:T(8,128)(2,1)S(1)}, u32[]{:S(2)}, u32[]{:S(2)}) collective-permute-start(bf16[4,48,128]{2,1,0:T(8,128)(2,1)S(1)} %shard_map.139.own_ref), channel_id=1, source_target_pairs={{0,2},{2,0},{1,3},{3,1},{4,6},{6,4},{5,7},{7,5},{8,10},{10,8},{9,1... | collective-permute-start | bytes 147464 | tf_op jit(solution)/shard_map/ppermute | solution.py:530
  28.4 10.0 %shard_map.140.main_ref = bf16[16,48,384]{2,1,0:T(8,128)(2,1)S(1)} custom-call(s32[2]{0:T(128)S(1)} %pad_add_fusion.1.place_ref, bf16[2,48,384]{2,1,0:T(8,128)(2,1)S(1)} %bitcast.32, bf16[2,48,384]{2,1,0:T(8,128)(2,1)S(1)} %collective-permute-done.refs_1_, bf16[2,48,384]{2,1,0:T(8,128)(2,1)S(1)} %collective-permute-done.1.refs_2_, ...), custom_call_target="tpu_custom_call" | custom-call | flops 5435817984 | bytes 1048576 | tf_op jit(solution)/shard_map/pallas_call | solution.py:491
  38.5 6.0 %shard_map.141 = (bf16[2,48,384]{2,1,0:T(8,128)(2,1)S(1)}, bf16[16,48,384]{2,1,0:T(8,128)(2,1)S(1)}, f32[16,8,384]{2,1,0:T(8,128)S(1)}, bf16[4,56,128]{2,1,0:T(8,128)(2,1)S(1)}) custom-call(s32[2]{0:T(128)S(1)} %pad_add_fusion.1.place_ref, bf16[4,48,128]{2,1,0:T(8,128)(2,1)S(1)} %shard_map.139.own_ref, ...), custom_call_target="tpu_custom_call" | custom-call | bytes 1048576 | tf_op jit(solution)/shard_map/pallas_call | solution.py:491
  44.5 0.6 %collective-permute-start.15 = (bf16[4,56,128]{2,1,0:T(8,128)(2,1)S(1)}, bf16[4,56,128]{2,1,0:T(8,128)(2,1)S(1)}, u32[]{:S(2)}, u32[]{:S(2)}) collective-permute-start(bf16[4,56,128]{2,1,0:T(8,128)(2,1)S(1)} %get-tuple-element.10.own_ref), channel_id=1, source_target_pairs={{0,2},{2,0},{1,3},{3,1},{4,6},{6,4},{5,7},{7,5},{8,10},{10,8},{9,1... | collective-permute-start | bytes 172040 | tf_op jit(solution)/shard_map/ppermute | solution.py:530
  45.1 6.7 %shard_map.142.main_ref = bf16[16,40,384]{2,1,0:T(8,128)(2,1)S(1)} custom-call(bf16[16,48,384]{2,1,0:T(8,128)(2,1)S(1)} %get-tuple-element.11.field_ref, f32[16,8,384]{2,1,0:T(8,128)S(1)} %get-tuple-element.12.extra_ref, bf16[2,128,432]{2,1,0:T(8,128)(2,1)S(1)} %copy.32.win_ref, bf16[2,360,128]{2,1,0:T(8,128)(2,1)S(1)} %bitcast.33), custom_call_target="tpu_custom_call" | custom-call | flops 2491416576 | bytes 1048576 | tf_op jit(solution)/shard_map/pallas_call | solution.py:491
  51.8 0.7 %copy.34 = bf16[48,2,384]{2,1,0:T(2,128)(2,1)} copy(bf16[48,2,384]{2,0,1:T(8,128)(2,1)S(1)} %bitcast.35) | data formatting | bytes 147456
  52.5 3.1 %shard_map.143 = (bf16[2,40,384]{2,1,0:T(8,128)(2,1)S(1)}, f32[2,384]{1,0:T(2,128)}) custom-call(s32[2]{0:T(128)S(1)} %pad_add_fusion.1.place_ref, s32[3,16]{1,0:T(4,128)S(1)} %get-tuple-element.21.slots_ref, bf16[4,56,128]{2,1,0:T(8,128)(2,1)S(1)} %get-tuple-element.10.own_ref, bf16[4,56,128]{2,1,0:T(8,128)(2,1)S(1)} %collective-permute-done.15.other_ref, ...), custom_call_target="tpu_custom_call" | custom-call | bytes 1048576 | tf_op jit(solution)/shard_map/pallas_call | solution.py:491
  55.6 0.7 %copy.35 = bf16[40,2,384]{2,1,0:T(2,128)(2,1)} copy(bf16[40,2,384]{2,0,1:T(8,128)(2,1)S(1)} %bitcast.36) | data formatting | bytes 122880
  (36 shorter events, 0.4 us)
Async XLA Ops:
  0.6 27.7 %copy-start.1 = (bf16[2,9,48,256]{3,2,1,0:T(8,128)(2,1)S(1)}, bf16[2,9,48,256]{3,2,1,0:T(8,128)(2,1)}, u32[]{:S(2)}) copy-start(bf16[2,9,48,256]{3,2,1,0:T(8,128)(2,1)} %param.16) | copy-start | bytes 1327108
  1.6 14.0 %collective-permute-start = (bf16[2,48,384]{2,1,0:T(8,128)(2,1)S(1)}, bf16[2,48,384]{2,1,0:T(8,128)(2,1)S(1)}, u32[]{:S(2)}, u32[]{:S(2)}) collective-permute-start(bf16[2,48,384]{2,1,0:T(8,128)(2,1)S(1)} %bitcast.27), channel_id=1, source_target_pairs={{0,4},{4,0},{8,12},{12,8},{1,5},{5,1},{9,13},{13,9},{2,6},{6,2},{1... | collective-permute-start | bytes 221192 | tf_op jit(solution)/shard_map/ppermute | solution.py:527
  4.7 14.5 %collective-permute-start.1 = (bf16[2,48,384]{2,1,0:T(8,128)(2,1)S(1)}, bf16[2,48,384]{2,1,0:T(8,128)(2,1)S(1)}, u32[]{:S(2)}, u32[]{:S(2)}) collective-permute-start(bf16[2,48,384]{2,1,0:T(8,128)(2,1)S(1)} %bitcast.28), channel_id=1, source_target_pairs={{0,8},{4,12},{8,0},{12,4},{1,9},{5,13},{9,1},{13,5},{2,10},{6,14},... | collective-permute-start | bytes 221192 | tf_op jit(solution)/shard_map/ppermute | solution.py:527
  7.3 11.9 %collective-permute-start.2 = (bf16[2,48,384]{2,1,0:T(8,128)(2,1)S(1)}, bf16[2,48,384]{2,1,0:T(8,128)(2,1)S(1)}, u32[]{:S(2)}, u32[]{:S(2)}) collective-permute-start(bf16[2,48,384]{2,1,0:T(8,128)(2,1)S(1)} %bitcast.29), channel_id=1, source_target_pairs={{0,12},{4,8},{8,4},{12,0},{1,13},{5,9},{9,5},{13,1},{2,14},{6,10},... | collective-permute-start | bytes 221192 | tf_op jit(solution)/shard_map/ppermute | solution.py:527
  7.3 12.0 %collective-permute-start.3 = (bf16[2,48,384]{2,1,0:T(8,128)(2,1)S(1)}, bf16[2,48,384]{2,1,0:T(8,128)(2,1)S(1)}, u32[]{:S(2)}, u32[]{:S(2)}) collective-permute-start(bf16[2,48,384]{2,1,0:T(8,128)(2,1)S(1)} %bitcast.30), channel_id=1, source_target_pairs={{0,1},{1,0},{2,3},{3,2},{4,5},{5,4},{6,7},{7,6},{8,9},{9,8},{10,11... | collective-permute-start | bytes 221192 | tf_op jit(solution)/shard_map/ppermute | solution.py:530
  12.3 7.4 %collective-permute-start.8 = (bf16[2,48,384]{2,1,0:T(8,128)(2,1)S(1)}, bf16[2,48,384]{2,1,0:T(8,128)(2,1)S(1)}, u32[]{:S(2)}, u32[]{:S(2)}) collective-permute-start(bf16[2,48,384]{2,1,0:T(8,128)(2,1)S(1)} %maximum_maximum_fusion.refs_0_), channel_id=1, source_target_pairs={{0,4},{4,0},{8,12},{12,8},{1,5},{5,1},{9,13},{13,9},{2,6},{6,2},{1... | collective-permute-start | bytes 221192 | tf_op jit(solution)/shard_map/ppermute | solution.py:527
  15.6 7.6 %collective-permute-start.9 = (bf16[2,48,384]{2,1,0:T(8,128)(2,1)S(1)}, bf16[2,48,384]{2,1,0:T(8,128)(2,1)S(1)}, u32[]{:S(2)}, u32[]{:S(2)}) collective-permute-start(bf16[2,48,384]{2,1,0:T(8,128)(2,1)S(1)} %maximum_maximum_fusion.refs_0_), channel_id=1, source_target_pairs={{0,8},{4,12},{8,0},{12,4},{1,9},{5,13},{9,1},{13,5},{2,10},{6,14},... | collective-permute-start | bytes 221192 | tf_op jit(solution)/shard_map/ppermute | solution.py:527
  19.1 6.2 %collective-permute-start.10 = (bf16[2,48,384]{2,1,0:T(8,128)(2,1)S(1)}, bf16[2,48,384]{2,1,0:T(8,128)(2,1)S(1)}, u32[]{:S(2)}, u32[]{:S(2)}) collective-permute-start(bf16[2,48,384]{2,1,0:T(8,128)(2,1)S(1)} %maximum_maximum_fusion.refs_0_), channel_id=1, source_target_pairs={{0,12},{4,8},{8,4},{12,0},{1,13},{5,9},{9,5},{13,1},{2,14},{6,10},... | collective-permute-start | bytes 221192 | tf_op jit(solution)/shard_map/ppermute | solution.py:527
  19.2 6.2 %collective-permute-start.4 = (bf16[2,48,384]{2,1,0:T(8,128)(2,1)S(1)}, bf16[2,48,384]{2,1,0:T(8,128)(2,1)S(1)}, u32[]{:S(2)}, u32[]{:S(2)}) collective-permute-start(bf16[2,48,384]{2,1,0:T(8,128)(2,1)S(1)} %collective-permute-done.refs_1_), channel_id=1, source_target_pairs={{0,1},{1,0},{2,3},{3,2},{4,5},{5,4},{6,7},{7,6},{8,9},{9,8},{10,11... | collective-permute-start | bytes 221192 | tf_op jit(solution)/shard_map/ppermute | solution.py:530
  19.2 6.6 %collective-permute-start.5 = (bf16[2,48,384]{2,1,0:T(8,128)(2,1)S(1)}, bf16[2,48,384]{2,1,0:T(8,128)(2,1)S(1)}, u32[]{:S(2)}, u32[]{:S(2)}) collective-permute-start(bf16[2,48,384]{2,1,0:T(8,128)(2,1)S(1)} %collective-permute-done.1.refs_2_), channel_id=1, source_target_pairs={{0,1},{1,0},{2,3},{3,2},{4,5},{5,4},{6,7},{7,6},{8,9},{9,8},{10,11... | collective-permute-start | bytes 221192 | tf_op jit(solution)/shard_map/ppermute | solution.py:530
  19.7 6.2 %collective-permute-start.6 = (bf16[2,48,384]{2,1,0:T(8,128)(2,1)S(1)}, bf16[2,48,384]{2,1,0:T(8,128)(2,1)S(1)}, u32[]{:S(2)}, u32[]{:S(2)}) collective-permute-start(bf16[2,48,384]{2,1,0:T(8,128)(2,1)S(1)} %collective-permute-done.2.refs_3_), channel_id=1, source_target_pairs={{0,1},{1,0},{2,3},{3,2},{4,5},{5,4},{6,7},{7,6},{8,9},{9,8},{10,11... | collective-permute-start | bytes 221192 | tf_op jit(solution)/shard_map/ppermute | solution.py:530
  23.2 15.3 %collective-permute-start.11 = (bf16[2,48,384]{2,1,0:T(8,128)(2,1)S(1)}, bf16[2,48,384]{2,1,0:T(8,128)(2,1)S(1)}, u32[]{:S(2)}, u32[]{:S(2)}) collective-permute-start(bf16[2,48,384]{2,1,0:T(8,128)(2,1)S(1)} %maximum_maximum_fusion.refs_0_), channel_id=1, source_target_pairs={{0,1},{1,0},{2,3},{3,2},{4,5},{5,4},{6,7},{7,6},{8,9},{9,8},{10,11... | collective-permute-start | bytes 221192 | tf_op jit(solution)/shard_map/ppermute | solution.py:530
  25.4 13.1 %collective-permute-start.12 = (bf16[2,48,384]{2,1,0:T(8,128)(2,1)S(1)}, bf16[2,48,384]{2,1,0:T(8,128)(2,1)S(1)}, u32[]{:S(2)}, u32[]{:S(2)}) collective-permute-start(bf16[2,48,384]{2,1,0:T(8,128)(2,1)S(1)} %collective-permute-done.8.refs_1_), channel_id=1, source_target_pairs={{0,1},{1,0},{2,3},{3,2},{4,5},{5,4},{6,7},{7,6},{8,9},{9,8},{10,11... | collective-permute-start | bytes 221192 | tf_op jit(solution)/shard_map/ppermute | solution.py:530
  25.4 13.1 %collective-permute-start.13 = (bf16[2,48,384]{2,1,0:T(8,128)(2,1)S(1)}, bf16[2,48,384]{2,1,0:T(8,128)(2,1)S(1)}, u32[]{:S(2)}, u32[]{:S(2)}) collective-permute-start(bf16[2,48,384]{2,1,0:T(8,128)(2,1)S(1)} %collective-permute-done.9.refs_2_), channel_id=1, source_target_pairs={{0,1},{1,0},{2,3},{3,2},{4,5},{5,4},{6,7},{7,6},{8,9},{9,8},{10,11... | collective-permute-start | bytes 221192 | tf_op jit(solution)/shard_map/ppermute | solution.py:530
  25.9 12.6 %collective-permute-start.14 = (bf16[2,48,384]{2,1,0:T(8,128)(2,1)S(1)}, bf16[2,48,384]{2,1,0:T(8,128)(2,1)S(1)}, u32[]{:S(2)}, u32[]{:S(2)}) collective-permute-start(bf16[2,48,384]{2,1,0:T(8,128)(2,1)S(1)} %collective-permute-done.10.refs_3_), channel_id=1, source_target_pairs={{0,1},{1,0},{2,3},{3,2},{4,5},{5,4},{6,7},{7,6},{8,9},{9,8},{10,11... | collective-permute-start | bytes 221192 | tf_op jit(solution)/shard_map/ppermute | solution.py:530
  26.8 11.6 %collective-permute-start.7 = (bf16[4,48,128]{2,1,0:T(8,128)(2,1)S(1)}, bf16[4,48,128]{2,1,0:T(8,128)(2,1)S(1)}, u32[]{:S(2)}, u32[]{:S(2)}) collective-permute-start(bf16[4,48,128]{2,1,0:T(8,128)(2,1)S(1)} %shard_map.139.own_ref), channel_id=1, source_target_pairs={{0,2},{2,0},{1,3},{3,1},{4,6},{6,4},{5,7},{7,5},{8,10},{10,8},{9,1... | collective-permute-start | bytes 147464 | tf_op jit(solution)/shard_map/ppermute | solution.py:530
  28.4 10.1 %copy-start = (bf16[64,128,128]{2,1,0:T(8,128)(2,1)S(1)}, bf16[64,128,128]{2,1,0:T(8,128)(2,1)}, u32[]{:S(2)}) copy-start(bf16[64,128,128]{2,1,0:T(8,128)(2,1)} %blocks_ref.3) | copy-start | bytes 6291460
  28.4 10.1 %copy-start.3 = (bf16[8,48]{1,0:T(8,128)(2,1)S(1)}, bf16[8,48]{1,0:T(8,128)(2,1)}, u32[]{:S(2)}) copy-start(bf16[8,48]{1,0:T(8,128)(2,1)} %proj_ref.1) | copy-start | bytes 2308
  38.4 6.7 %copy-start.2 = (bf16[2,9,40,128]{3,2,1,0:T(8,128)(2,1)S(1)}, bf16[2,9,40,128]{3,2,1,0:T(8,128)(2,1)}, u32[]{:S(2)}) copy-start(bf16[2,9,40,128]{3,2,1,0:T(8,128)(2,1)} %param.18) | copy-start | bytes 552964
  44.5 8.0 %collective-permute-start.15 = (bf16[4,56,128]{2,1,0:T(8,128)(2,1)S(1)}, bf16[4,56,128]{2,1,0:T(8,128)(2,1)S(1)}, u32[]{:S(2)}, u32[]{:S(2)}) collective-permute-start(bf16[4,56,128]{2,1,0:T(8,128)(2,1)S(1)} %get-tuple-element.10.own_ref), channel_id=1, source_target_pairs={{0,2},{2,0},{1,3},{3,1},{4,6},{6,4},{5,7},{7,5},{8,10},{10,8},{9,1... | collective-permute-start | bytes 172040 | tf_op jit(solution)/shard_map/ppermute | solution.py:530

commit v2 on v1

--- a/solution.py
+++ b/solution.py
@@ -226,6 +226,10 @@
     emit(rows - 1, column_sum(ahead, outs))
 
 
+def turned(w_ref, layer):
+    return jnp.transpose(w_ref[layer])
+
+
 def lanes_of(shape):
     return lax.broadcasted_iota(jnp.int32, shape, len(shape) - 1)
 
@@ -287,61 +291,88 @@
     return jnp.concatenate([head, row[:, 128 : width - 128], tail], axis=1)
 
 
-def edge_kernel(place_ref, *refs):
-    tiles, out_ref = refs[:-1], refs[-1]
+def pack_atmos_kernel(atmos_ref, tile_ref):
+    for r in range(tile_ref.shape[0]):
+        tile_ref[r] = atmos_ref[:, r, :]
+
+
+def pack_ocean_kernel(source_hbm, target_hbm, weight_hbm, ocean_hbm, mask_hbm, tile_ref, source_ref,
+                      target_ref, weight_ref, ocean_ref, mask_ref, sems):
+    given = (source_hbm, target_hbm, weight_hbm, ocean_hbm, mask_hbm)
+    numbers = (source_ref, target_ref, weight_ref)
+    held = (*numbers, ocean_ref, mask_ref)
+    copies = [pltpu.make_async_copy(v, h, sems.at[i]) for i, (v, h) in enumerate(zip(given, held))]
+    for copy in copies:
+        copy.start()
+    for copy in copies:
+        copy.wait()
+    height, span, width = tile_ref.shape
+    slots, peers = source_ref.shape[2:]
+    listed = [ref[0, 0, s : s + 1, :].astype(F32) for ref in numbers for s in range(slots)]
+    listed.append(jnp.zeros((1, width - len(listed) * peers), F32))
+    listed = jnp.concatenate(listed, axis=1)
+    rest = jnp.zeros((span - ocean_ref.shape[0] - 2, width), F32)
+    for r in range(height):
+        wet = mask_ref[r : r + 1, :].astype(F32)
+        state = ocean_ref[:, r, :].astype(F32) * wet
+        tile_ref[r] = jnp.concatenate([state, wet, listed, rest], axis=0).astype(BF)
+
+
+def stack_kernel(place_ref, *refs):
+    tiles, (stack_ref, edge_ref) = refs[:8], refs[8:]
     lat, comp = place_ref[0], place_ref[1]
-    count = len(tiles) // 2
-    for k in range(count):
-        near = edges_of([tiles[k][r].astype(F32) for r in range(2)])
-        far = edges_of([tiles[count + k][r].astype(F32) for r in range(2)])
-        both = pltpu.roll(near, 64 * comp, 1) + pltpu.roll(far, 64 * (1 - comp), 1)
-        out_ref[lat ^ k] = both.astype(BF)
-
-
-def atmos_kernel(place_ref, *refs):
-    tiles, (win_ref, wout_ref, out_ref, s0_ref, s1_ref) = refs[:8], refs[8:]
-    lat, comp = place_ref[0], place_ref[1]
+    chans, width = tiles[0].shape[1:]
+    chips = edge_ref.shape[0]
+    clear_ends(stack_ref, 4 * chips, chans)
+    for k in range(chips):
+        both = jnp.zeros((chans, 128), F32)
+        for half, tile in ((comp, tiles[k]), (1 - comp, tiles[chips + k])):
+            pair = [tile[r].astype(F32) for r in range(2)]
+            for r in range(2):
+                store_row(stack_ref, 4 * (lat ^ k) + 2 * half + r + 1, pair[r], chans)
+            both = both + pltpu.roll(edges_of(pair), 64 * half, 1)
+        edge_ref[lat ^ k] = both.astype(BF)
+
+
+def first_kernel(stack_ref, win_ref, wout_ref, next_ref):
+    chans = wout_ref.shape[1] // 9
+    width = stack_ref.shape[1]
+    rows = stack_ref.shape[0] // (3 * chans) - 2
+    clear_ends(next_ref, rows, chans)
+
+    def emit(r, y):
+        base = (3 * (r + 1) + 1) * chans
+        total = stack_ref[base : base + chans, :].astype(F32) + y
+        store_row(next_ref, r + 1, total.astype(BF).astype(F32), chans)
+
+    main_block(stack_ref, turned(win_ref, 0), wout_ref[0], chans, chans, rows, width, emit)
+
+
+def second_kernel(place_ref, stack_ref, win_ref, wout_ref, *refs):
+    ocean_tiles, (out_ref, ocean_ref, sems) = refs[:4], refs[4:]
+    lat = place_ref[0]
     rows, chans, width = out_ref.shape
-    clear_ends(s0_ref, rows, chans)
-    clear_ends(s1_ref, rows, chans)
-    for i, tile in enumerate(tiles):
-        base = 4 * (lat ^ (i % 4)) + 2 * (comp if i < 4 else 1 - comp)
-        for r in range(2):
-            store_row(s0_ref, base + r + 1, tile[r].astype(F32), chans)
-    stacks = (s0_ref, s1_ref)
-    layers = win_ref.shape[0]
-    for layer in range(layers):
-        source = stacks[layer % 2]
-
-        def emit(r, y):
-            base = (3 * (r + 1) + 1) * chans
-            total = source[base : base + chans, :].astype(F32) + y
-            if layer == layers - 1:
-                out_ref[r] = total.astype(BF)
-            else:
-                store_row(stacks[(layer + 1) % 2], r + 1, total.astype(BF).astype(F32), chans)
-
-        main_block(source, win_ref[layer], wout_ref[layer], chans, chans, rows, width, emit)
-
-
-def flux_kernel(place_ref, own_ref, other_ref, main_ref, win_ref, wout_ref, proj_ref, blocks_ref,
-                *refs):
-    tiles = refs[:8]
-    next_ref, field_ref, extra_ref, edge_ref, merged, flux, total, table, index, sem = refs[8:]
+    copies = [
+        pltpu.make_async_copy(tile, ocean_ref.at[lat ^ k], sems.at[k])
+        for k, tile in enumerate(ocean_tiles)
+    ]
+    for copy in copies:
+        copy.start()
+
+    def emit(r, y):
+        base = (3 * (r + 1) + 1) * chans
+        out_ref[r] = (stack_ref[base : base + chans, :].astype(F32) + y).astype(BF)
+
+    main_block(stack_ref, turned(win_ref, 1), wout_ref[1], chans, chans, rows, width, emit)
+    for copy in copies:
+        copy.wait()
+
+
+def flux_kernel(place_ref, own_ref, other_ref, main_ref, win_ref, wout_ref, proj_ref, next_ref,
+                flux_ref, merged):
     lat, comp = place_ref[0], place_ref[1]
     rows, chans, width = main_ref.shape
-    fluxes = proj_ref.shape[0]
     per_row = width // 128
-    subs = 2 * per_row
-    slots = 2 * rows // 2
-
-    for i, tile in enumerate(tiles):
-        t = 2 * (lat ^ (i % 4)) + (comp if i < 4 else 1 - comp)
-        row = tile[0, 32:48, 0:128].astype(F32)[9:10]
-        table[pl.ds(t, 1), :] = row.astype(jnp.int32)
-    copy = pltpu.make_async_copy(table, index, sem)
-    copy.start()
-
     strip = jnp.concatenate(
         [
             with_neighbour(own_ref[q].astype(F32), other_ref[q].astype(F32))
@@ -350,7 +381,7 @@
         axis=1,
     )
     for layer in range(win_ref.shape[0]):
-        strip = strip + strip_block(strip, win_ref[layer], wout_ref[layer], chans)
+        strip = strip + strip_block(strip, turned(win_ref, layer), wout_ref[layer], chans)
         strip = strip.astype(BF).astype(F32)
 
     for r in range(rows):
@@ -359,13 +390,31 @@
         merged[r] = row
         f = jnp.dot(proj_ref[...], row, preferred_element_type=F32)
         for b in range(per_row):
-            flux[(r // 2) * subs + (r % 2) * per_row + b] = f[:, 128 * b : 128 * (b + 1)].astype(
-                BF
-            ).astype(F32)
+            flux_ref[r * per_row + b] = f[:, 128 * b : 128 * (b + 1)].astype(BF).astype(F32)
     base = 4 * lat + 2 * comp
     for r in range(2):
-        next_ref[r] = merged[base + r]
-
+        next_ref[:, r, :] = merged[base + r]
+
+
+def regrid_kernel(place_ref, flux_ref, blocks_ref, near_ref, far_ref, field_ref, extra_ref,
+                  edge_ref, table, total, index, sem):
+    comp = place_ref[1]
+    chips = near_ref.shape[0]
+    rows, chans, width = field_ref.shape
+    fluxes = flux_ref.shape[1]
+    outs = chans - fluxes
+    per_row = width // 128
+    subs = 2 * per_row
+    peers = 2 * chips
+    slots = rows
+
+    for chip in range(chips):
+        for near, tiles in ((0, near_ref), (1, far_ref)):
+            t = 2 * chip + jnp.where(comp == near, 0, 1)
+            row = tiles[chip, 0, 32:48, 0:128].astype(F32)[9:10]
+            table[pl.ds(t, 1), :] = row.astype(jnp.int32)
+    copy = pltpu.make_async_copy(table, index, sem)
+    copy.start()
     total[...] = jnp.zeros(total.shape, F32)
     copy.wait()
 
@@ -375,35 +424,31 @@
             live = source >= 0
             target = jnp.where(live, index[t, slots + slot], 6)
             block = blocks_ref[index[t, 2 * slots + slot]]
-            value = flux[t * subs + jnp.maximum(source, 0)].astype(BF)
+            value = flux_ref[t * subs + jnp.maximum(source, 0)].astype(BF)
             piece = jnp.dot(value, block, preferred_element_type=F32)
-            at = (slot // 2) * 8 + target
+            at = (slot % peers) * 8 + target
             total[at] = total[at] + piece.astype(BF).astype(F32)
         return carry
 
     lax.fori_loop(0, rows // 2, one_tile, 0)
 
-    for i, tile in enumerate(tiles):
-        t = 2 * (lat ^ (i % 4)) + (comp if i < 4 else 1 - comp)
-        ends = []
-        for r in range(2):
-            arrived = jnp.concatenate(
-                [total[8 * t + r * per_row + b] for b in range(per_row)], axis=1
-            )
-            state = tile[r].astype(F32)
-            outs = state.shape[0] - fluxes
-            row = jnp.concatenate([state[0:outs], arrived], axis=0)
-            field_ref[2 * t + r] = row.astype(BF)
-            extra_ref[2 * t + r] = state[outs:]
-            ends.append(jnp.concatenate([row, state[outs:]], axis=0))
-        both = edges_of(ends)
-        half = comp if i < 4 else 1 - comp
-        edge_ref_at = lat ^ (i % 4)
-        moved = pltpu.roll(both, 64 * half, 1)
-        if i < 4:
-            edge_ref[edge_ref_at] = moved.astype(BF)
-        else:
-            edge_ref[edge_ref_at] = (edge_ref[edge_ref_at].astype(F32) + moved).astype(BF)
+    for chip in range(chips):
+        both = jnp.zeros((chans + fluxes, 128), F32)
+        for near, tiles in ((0, near_ref), (1, far_ref)):
+            half = jnp.where(comp == near, 0, 1)
+            t = 2 * chip + half
+            ends = []
+            for r in range(2):
+                arrived = jnp.concatenate(
+                    [total[8 * t + r * per_row + b] for b in range(per_row)], axis=1
+                )
+                state = tiles[chip, r].astype(F32)
+                row = jnp.concatenate([state[0:outs], arrived], axis=0)
+                field_ref[2 * t + r] = row.astype(BF)
+                extra_ref[2 * t + r] = state[outs:]
+                ends.append(jnp.concatenate([row, state[outs:]], axis=0))
+            both = both + pltpu.roll(edges_of(ends), 64 * half, 1)
+        edge_ref[chip] = both.astype(BF)
 
 
 def ocean_kernel(field_ref, extra_ref, win_ref, wout_ref, out_ref, s0_ref, s1_ref):
@@ -429,14 +474,16 @@
                 row = jnp.concatenate([total.astype(BF).astype(F32), state[outs:]], axis=0)
                 store_row(stacks[(layer + 1) % 2], r + 1, row, chans)
 
-        main_block(source, win_ref[layer], wout_ref[layer], chans, outs, rows, width, emit)
-
-
-def finish_kernel(place_ref, slots_ref, own_ref, other_ref, main_ref, win_ref, wout_ref, blocks_ref,
-                  next_ref, temp_ref, surface, total):
+        main_block(source, turned(win_ref, layer), wout_ref[layer], chans, outs, rows, width, emit)
+
+
+def finish_kernel(place_ref, table_ref, own_ref, other_ref, main_ref, win_ref, wout_ref, blocks_ref,
+                  next_ref, temp_ref, surface, total, index, sem):
+    copy = pltpu.make_async_copy(table_ref, index, sem)
+    copy.start()
     lat, comp = place_ref[0], place_ref[1]
     rows, outs, width = main_ref.shape
-    chans = win_ref.shape[2] // 9
+    chans = win_ref.shape[1] // 9
     per_row = width // 128
     strip = jnp.concatenate(
         [
@@ -449,7 +496,7 @@
     state, fixed = strip[0:outs], strip[outs:chans]
     for layer in range(win_ref.shape[0]):
         source = jnp.concatenate([state, fixed], axis=0)
-        state = wet * (state + strip_block(source, win_ref[layer], wout_ref[layer], outs))
+        state = wet * (state + strip_block(source, turned(win_ref, layer), wout_ref[layer], outs))
         state = state.astype(BF).astype(F32)
 
     for r in range(rows):
@@ -464,15 +511,17 @@
         own = jnp.where(lat == q, state[:, 128 * q : 128 * (q + 1)], own)
     own = pltpu.roll(own, jnp.where(comp == 1, 64, 0), 1)
     for r in range(2):
-        next_ref[r] = mend_row(main_ref[base + r].astype(F32), own, r).astype(BF)
+        next_ref[:, r, :] = mend_row(main_ref[base + r].astype(F32), own, r).astype(BF)
 
     total[...] = jnp.zeros(total.shape, F32)
-    slots = slots_ref.shape[1]
+    copy.wait()
+    slots = rows
+    t = 2 * lat + comp
     for slot in range(slots):
-        source = slots_ref[0, slot]
-        target = slots_ref[1, slot]
-        block = blocks_ref[slots_ref[2, slot]]
-        value = surface[(slot // 2) * 8 + target].astype(BF)
+        source = index[t, slot]
+        target = index[t, slots + slot]
+        block = blocks_ref[index[t, 2 * slots + slot]]
+        value = surface[(slot % (rows // 2)) * 8 + target].astype(BF)
         piece = lax.dot_general(value, block, (((1,), (1,)), ((), ())), preferred_element_type=F32)
         at = jnp.where(source >= 0, source, 6)
         total[at] = total[at] + piece
@@ -482,11 +531,10 @@
         )
 
 
-def call(kernel, out_shape, operands, scratch=(), smem=1, flops=0):
-    specs = [
-        pl.BlockSpec(memory_space=pltpu.SMEM if i < smem else pltpu.VMEM)
-        for i in range(len(operands))
-    ]
+def call(kernel, out_shape, operands, scratch=(), smem=1, anywhere=0, flops=0):
+    held = len(operands) - smem - anywhere
+    spaces = [pltpu.SMEM] * smem + [pltpu.VMEM] * held + [pltpu.HBM] * anywhere
+    specs = [pl.BlockSpec(memory_space=space) for space in spaces]
     out_specs = jax.tree.map(lambda _: pl.BlockSpec(memory_space=pltpu.VMEM), out_shape)
     return pl.pallas_call(
         kernel,
@@ -529,33 +577,27 @@
     def swap(v, axis):
         return lax.ppermute(v, axis, [(0, 1), (1, 0)])
 
-    def column(mine):
-        near = [mine] + [far(mine, k) for k in range(1, lats)]
-        return near + [swap(v, "comp") for v in near]
-
-    atmos = column(jnp.transpose(atmos_state, (1, 0, 2)))
-
-    slots = jnp.stack(
-        [
-            v.reshape(-1)
-            for v in (regrid_source_block, regrid_target_block, regrid_weight_block)
-        ]
-    )
-    index_row = jnp.pad(slots.reshape(-1).astype(BF), (0, width - slots.size))
-    wet = ocean_mask.astype(BF)[:, None, :]
-    payload = jnp.concatenate(
-        [
-            jnp.transpose(ocean_state, (1, 0, 2)) * wet,
-            wet,
-            jnp.broadcast_to(index_row[None, None], (height, 1, width)),
-            jnp.zeros((height, 6, width), BF),
-        ],
-        axis=1,
-    )
-    ocean = column(payload)
+    def conv_flops(hidden, outs):
+        return 2 * layers * rows * width * 9 * hidden * (chans + outs)
+
+    tile = jax.ShapeDtypeStruct((height, chans, width), BF)
+    atmos_tile = call(pack_atmos_kernel, tile, [atmos_state], smem=0)
+    slots = (regrid_source_block, regrid_target_block, regrid_weight_block)
+    given = [*(jnp.transpose(v, (0, 1, 3, 2)) for v in slots), ocean_state, ocean_mask]
+    ocean_tile = call(
+        pack_ocean_kernel,
+        tile,
+        given,
+        [*(pltpu.VMEM(v.shape, v.dtype) for v in given), pltpu.SemaphoreType.DMA((len(given),))],
+        smem=0,
+        anywhere=len(given),
+    )
+    near = [atmos_tile] + [far(atmos_tile, k) for k in range(1, lats)]
+    column = near + [swap(v, "comp") for v in near]
+    ocean_near = [ocean_tile] + [far(ocean_tile, k) for k in range(1, lats)]
 
     def taps_in(w):
-        return jnp.transpose(w, (0, 2, 1, 3)).reshape(w.shape[0], w.shape[2], 9 * w.shape[3])
+        return jnp.transpose(w, (0, 1, 3, 2)).reshape(w.shape[0], 9 * w.shape[3], w.shape[2])
 
     def taps_out(w):
         return w.reshape(w.shape[0], 9 * w.shape[2], w.shape[3])
@@ -563,34 +605,56 @@
     win_a, wout_a = taps_in(atmos_in_w), taps_out(atmos_out_w)
     win_o, wout_o = taps_in(ocean_in_w), taps_out(ocean_out_w)
 
-    def conv_flops(hidden, outs):
-        return 2 * layers * rows * width * 9 * hidden * (chans + outs)
-
-    edges = call(edge_kernel, jax.ShapeDtypeStruct((lats, chans, 128), BF), [place, *atmos])
+    stack = (rows + 2) * 3 * chans
+    stack_shape = jax.ShapeDtypeStruct((stack, width), BF)
+    atmos_stack, edges = call(
+        stack_kernel,
+        (stack_shape, jax.ShapeDtypeStruct((lats, chans, 128), BF)),
+        [place, *column],
+        flops=conv_flops(hidden_a, chans),
+    )
     edges_other = swap(edges, "lon")
-    stack = (rows + 2) * 3 * chans
-    main = call(
-        atmos_kernel,
-        jax.ShapeDtypeStruct((rows, chans, width), BF),
-        [place, *atmos, win_a, wout_a],
-        [pltpu.VMEM((stack, width), BF), pltpu.VMEM((stack, width), BF)],
-        flops=conv_flops(hidden_a, chans),
-    )
+    atmos_stack = call(
+        first_kernel,
+        stack_shape,
+        [atmos_stack, win_a, wout_a],
+        smem=0,
+        flops=4 * conv_flops(hidden_a, chans),
+    )
+    main, ocean_near = call(
+        second_kernel,
+        (
+            jax.ShapeDtypeStruct((rows, chans, width), BF),
+            jax.ShapeDtypeStruct((lats, height, chans, width), BF),
+        ),
+        [place, atmos_stack, win_a, wout_a, *ocean_near],
+        [pltpu.SemaphoreType.DMA((lats,))],
+        flops=4 * conv_flops(hidden_a, chans),
+        anywhere=lats,
+    )
+    ocean_far = swap(ocean_near, "comp")
     subs = height * width // 128
-    atmos_next, field, extra, ocean_edges = call(
+    atmos_next, flux = call(
         flux_kernel,
         (
-            jax.ShapeDtypeStruct((height, chans, width), BF),
+            jax.ShapeDtypeStruct((chans, height, width), BF),
+            jax.ShapeDtypeStruct((tiles * subs, fluxes, 128), F32),
+        ),
+        [place, edges, edges_other, main, win_a, wout_a, flux_proj],
+        [pltpu.VMEM((rows, chans, width), BF)],
+        flops=4 * conv_flops(hidden_a, chans),
+    )
+    field, extra, ocean_edges, table = call(
+        regrid_kernel,
+        (
             jax.ShapeDtypeStruct((rows, chans, width), BF),
             jax.ShapeDtypeStruct((rows, fluxes, width), F32),
             jax.ShapeDtypeStruct((lats, chans + fluxes, 128), BF),
+            jax.ShapeDtypeStruct((tiles, 128), jnp.int32),
         ),
-        [place, edges, edges_other, main, win_a, wout_a, flux_proj, regrid_blocks, *ocean],
+        [place, flux, regrid_blocks, ocean_near, ocean_far],
         [
-            pltpu.VMEM((rows, chans, width), BF),
-            pltpu.VMEM((tiles * subs, fluxes, 128), F32),
             pltpu.VMEM((tiles * 8, fluxes, 128), F32),
-            pltpu.VMEM((tiles, 128), jnp.int32),
             pltpu.SMEM((tiles, 128), jnp.int32),
             pltpu.SemaphoreType.DMA,
         ],
@@ -602,23 +666,23 @@
         [field, extra, win_o, wout_o],
         [pltpu.VMEM((stack, width), BF), pltpu.VMEM((stack, width), BF)],
         smem=0,
-        flops=conv_flops(hidden_o, outs),
+        flops=4 * conv_flops(hidden_o, outs),
     )
     ocean_next, surface_temp = call(
         finish_kernel,
         (
-            jax.ShapeDtypeStruct((height, outs, width), BF),
+            jax.ShapeDtypeStruct((outs, height, width), BF),
             jax.ShapeDtypeStruct((height, width), F32),
         ),
-        [place, slots, ocean_edges, ocean_edges_other, ocean_main, win_o, wout_o, regrid_blocks],
-        [pltpu.VMEM((tiles * 8, 8, 128), F32), pltpu.VMEM((8, 8, 128), F32)],
-        smem=2,
-    )
-    return (
-        jnp.transpose(atmos_next, (1, 0, 2)),
-        jnp.transpose(ocean_next, (1, 0, 2)),
-        surface_temp,
-    )
+        [place, table, ocean_edges, ocean_edges_other, ocean_main, win_o, wout_o, regrid_blocks],
+        [
+            pltpu.VMEM((tiles * 8, 8, 128), F32),
+            pltpu.VMEM((8, 8, 128), F32),
+            pltpu.SMEM((tiles, 128), jnp.int32),
+            pltpu.SemaphoreType.DMA,
+        ],
+    )
+    return atmos_next, ocean_next, surface_temp
 
 
 def solution(mesh):

time: 56.6 us -> 49.8 us (0.88)
  waiting for transfers between devices: 5.46 us -> 0.41 us
  Pallas kernels: 26.7 us -> 30.2 us
  local copies, waits for them, and re-layouts: 7.3 us -> 4.45 us
  other arithmetic: 2.4 us -> 0.07 us
    ppermute x6, waiting for transfers between devices: 5.43 us -> 0.02 us  [far(): return lax.ppermute(v, 'lat', [(i, i ^ k) for i in range(lats)])]
    pallas_call x5 -> x9, Pallas kernels: 26.7 us -> 30.2 us  [call(): pl.pallas_call(kernel, out_shape=out_shape, in_specs=specs, out_specs=out...]
    reshape x2 -> x0, local copies, waits for them, and re-layouts: 2.29 us -> none  [taps_in(): jnp.transpose(w, (0, 2, 1, 3))]
    mul x1 -> x0, other arithmetic: 0.85 us -> none  [column_device(): jnp.transpose(ocean_state, (1, 0, 2)) * wet]
    convert_element_type x1 -> x0, other arithmetic: 0.69 us -> none  [column_device(): wet = ocean_mask.astype(BF)[:, None, :]]
    broadcast_in_dim x1 -> x0, other arithmetic: 0.69 us -> none  [column_device(): wet = ocean_mask.astype(BF)[:, None, :]]
    ppermute x10 -> x7, starting transfers between devices: 3.38 us -> 2.97 us  [swap(): return lax.ppermute(v, axis, [(0, 1), (1, 0)])]
    unnamed x14 -> x24, local copies, waits for them, and re-layouts: 4.59 us -> 4.45 us
  transfers between devices with their start and end apart: 16 -> 13, of which waited for: 2 -> 1; matrix products, arithmetic and copies ran while one was open for 14% -> 0% of each run, Pallas kernels for 31% -> 46%
where the time goes in v2:
time: 49.8 us; the launch traced here: 49.5 us
  Pallas kernels  30.2 us (61%)
  starting transfers between devices  13.3 us (27%)
  local copies, waits for them, and re-layouts  4.45 us (9%)
  between operations  0.97 us (2%)
    pallas_call x9, Pallas kernels, call(): pl.pallas_call(kernel, out_shape=out_shape, in_specs=specs, out_specs=out...  30.2 us
    ppermute x6, starting transfers between devices, far(): return lax.ppermute(v, 'lat', [(i, i ^ k) for i in range(lats)])  10.4 us
    unnamed x24, local copies, waits for them, and re-layouts  4.45 us
    ppermute x7, starting transfers between devices, swap(): return lax.ppermute(v, axis, [(0, 1), (1, 0)])  2.97 us
  transfers between devices with their start and end apart: 13, of which 1 were waited for; matrix products, arithmetic and copies ran while one was open for 0% of the time, Pallas kernels for 46%

profile of v2, /device:TPU:0, one launch (start us, length us, event | category | flops | bytes accessed | tf_op | source)
XLA Modules:
  0.0 49.5 jit_solution(4430827246165810556)
XLA Ops:
  0.6 0.9 %copy-done.3 = bf16[48,2,384]{2,1,0:T(2,128)(2,1)S(1)} copy-done((bf16[48,2,384]{2,1,0:T(2,128)(2,1)S(1)}, bf16[48,2,384]{2,1,0:T(2,128)(2,1)}, u32[]{:S(2)}) %copy-start.3) | copy-done | bytes 73752
  1.5 0.2 shard_map.139.refs_0_
  1.7 3.1 %collective-permute-start = (bf16[2,48,384]{2,1,0:T(8,128)(2,1)S(1)}, bf16[2,48,384]{2,1,0:T(8,128)(2,1)S(1)}, u32[]{:S(2)}, u32[]{:S(2)}) collective-permute-start(bf16[2,48,384]{2,1,0:T(8,128)(2,1)S(1)} %shard_map.139.refs_0_), channel_id=1, source_target_pairs={{0,4},{4,0},{8,12},{12,8},{1,5},{5,1},{9,13},{13,9},{2,6},{6,2},{1... | collective-permute-start | bytes 221192 | tf_op jit(solution)/shard_map/ppermute | solution.py:575
  4.8 2.6 %collective-permute-start.1 = (bf16[2,48,384]{2,1,0:T(8,128)(2,1)S(1)}, bf16[2,48,384]{2,1,0:T(8,128)(2,1)S(1)}, u32[]{:S(2)}, u32[]{:S(2)}) collective-permute-start(bf16[2,48,384]{2,1,0:T(8,128)(2,1)S(1)} %shard_map.139.refs_0_), channel_id=1, source_target_pairs={{0,8},{4,12},{8,0},{12,4},{1,9},{5,13},{9,1},{13,5},{2,10},{6,14},... | collective-permute-start | bytes 221192 | tf_op jit(solution)/shard_map/ppermute | solution.py:575
  7.4 0.0 collective-permute-start.2
  7.4 0.0 collective-permute-start.3
  7.4 0.8 %copy-done.4 = bf16[40,2,384]{2,1,0:T(2,128)(2,1)S(1)} copy-done((bf16[40,2,384]{2,1,0:T(2,128)(2,1)S(1)}, bf16[40,2,384]{2,1,0:T(2,128)(2,1)}, u32[]{:S(2)}) %copy-start.4) | copy-done | bytes 61464
  8.2 0.7 %copy-done.5 = s32[2,384]{1,0:T(2,128)S(1)} copy-done((s32[2,384]{1,0:T(2,128)S(1)}, s32[2,384]{1,0:T(2,128)}, u32[]{:S(2)}) %copy-start.5) | copy-done | bytes 3096
  8.9 0.7 %copy-done.6 = s32[1,1,8,2]{2,3,1,0:T(2,128)S(1)} copy-done((s32[1,1,8,2]{2,3,1,0:T(2,128)S(1)}, s32[1,1,8,2]{2,3,1,0:T(2,128)}, u32[]{:S(2)}) %copy-start.6) | copy-done | bytes 88
  9.6 0.7 %copy-done.7 = s32[1,1,8,2]{2,3,1,0:T(2,128)S(1)} copy-done((s32[1,1,8,2]{2,3,1,0:T(2,128)S(1)}, s32[1,1,8,2]{2,3,1,0:T(2,128)}, u32[]{:S(2)}) %copy-start.7) | copy-done | bytes 88
  10.3 0.7 %copy-done.8 = s32[1,1,8,2]{2,3,1,0:T(2,128)S(1)} copy-done((s32[1,1,8,2]{2,3,1,0:T(2,128)S(1)}, s32[1,1,8,2]{2,3,1,0:T(2,128)}, u32[]{:S(2)}) %copy-start.8) | copy-done | bytes 88
  10.9 0.2 shard_map.142.refs_0_
  11.1 3.9 %collective-permute-start.10 = (bf16[2,48,384]{2,1,0:T(8,128)(2,1)S(1)}, bf16[2,48,384]{2,1,0:T(8,128)(2,1)S(1)}, u32[]{:S(2)}, u32[]{:S(2)}) collective-permute-start(bf16[2,48,384]{2,1,0:T(8,128)(2,1)S(1)} %shard_map.142.refs_0_), channel_id=1, source_target_pairs={{0,12},{4,8},{8,4},{12,0},{1,13},{5,9},{9,5},{13,1},{2,14},{6,10},... | collective-permute-start | bytes 221192 | tf_op jit(solution)/shard_map/ppermute | solution.py:575
  15.0 0.2 collective-permute-start.4
  15.3 0.3 collective-permute-start.5
  15.5 0.2 collective-permute-start.6
  15.8 0.1 pad_add_fusion.place_ref
  15.9 0.1 collective-permute-start.8
  15.9 0.4 collective-permute-done.4.refs_5_
  16.3 0.8 %collective-permute-start.9 = (bf16[2,48,384]{2,1,0:T(8,128)(2,1)S(1)}, bf16[2,48,384]{2,1,0:T(8,128)(2,1)S(1)}, u32[]{:S(2)}, u32[]{:S(2)}) collective-permute-start(bf16[2,48,384]{2,1,0:T(8,128)(2,1)S(1)} %shard_map.142.refs_0_), channel_id=1, source_target_pairs={{0,8},{4,12},{8,0},{12,4},{1,9},{5,13},{9,1},{13,5},{2,10},{6,14},... | collective-permute-start | bytes 221192 | tf_op jit(solution)/shard_map/ppermute | solution.py:575
  17.1 1.6 %shard_map.140 = (bf16[2592,384]{1,0:T(8,128)(2,1)S(1)}, bf16[4,48,128]{2,1,0:T(8,128)(2,1)S(1)}) custom-call(s32[2]{0:T(128)S(1)} %pad_add_fusion.place_ref, bf16[2,48,384]{2,1,0:T(8,128)(2,1)S(1)} %shard_map.139.refs_0_, bf16[2,48,384]{2,1,0:T(8,128)(2,1)S(1)} %collective-permute-done.refs_1_, bf16[2,48,384]{2,1,0:T(8,128)(2,1)S(1)} %collective-permute-done.1.refs_2_, ...), custom_call_target="tpu_custom_call" | custom-call | flops 5435817984 | bytes 1048576 | tf_op jit(solution)/shard_map/pallas_call | solution.py:539
  18.6 1.6 %collective-permute-start.7 = (bf16[4,48,128]{2,1,0:T(8,128)(2,1)S(1)}, bf16[4,48,128]{2,1,0:T(8,128)(2,1)S(1)}, u32[]{:S(2)}, u32[]{:S(2)}) collective-permute-start(bf16[4,48,128]{2,1,0:T(8,128)(2,1)S(1)} %get-tuple-element.15.own_ref), channel_id=1, source_target_pairs={{0,2},{2,0},{1,3},{3,1},{4,6},{6,4},{5,7},{7,5},{8,10},{10,8},{9,1... | collective-permute-start | bytes 147464 | tf_op jit(solution)/shard_map/ppermute | solution.py:578
  20.2 5.0 %shard_map.141.stack_ref = bf16[2592,384]{1,0:T(8,128)(2,1)S(1)} custom-call(bf16[2592,384]{1,0:T(8,128)(2,1)S(1)} %get-tuple-element.16.stack_ref, bf16[2,432,256]{2,1,0:T(8,128)(2,1)S(1)} %bitcast.20, bf16[2,432,256]{2,1,0:T(8,128)(2,1)S(1)} %bitcast.23), custom_call_target="tpu_custom_call" | custom-call | flops 21743271936 | bytes 1048576 | tf_op jit(solution)/shard_map/pallas_call | solution.py:539
  25.2 0.0 copy-start.11
  25.2 5.9 %shard_map.143 = (bf16[16,48,384]{2,1,0:T(8,128)(2,1)S(1)}, bf16[4,2,48,384]{3,2,1,0:T(8,128)(2,1)S(1)}) custom-call(s32[2]{0:T(128)S(1)} %pad_add_fusion.place_ref, bf16[2592,384]{1,0:T(8,128)(2,1)S(1)} %shard_map.141.stack_ref, bf16[2,432,256]{2,1,0:T(8,128)(2,1)S(1)} %bitcast.21, bf16[2,432,256]{2,1,0:T(8,128)(2,1)S(1)} %bitcast.24, ...), custom_call_target="tpu_custom_call" | custom-call | flops 21743271936 | bytes 1048576 | tf_op jit(solution)/shard_map/pallas_call | solution.py:539
  31.1 0.1 collective-permute-start.11
  31.2 0.0 copy-start
  31.2 3.3 %shard_map.144 = (bf16[48,2,384]{2,1,0:T(2,128)(2,1)}, f32[48,8,128]{2,1,0:T(8,128)S(1)}) custom-call(s32[2]{0:T(128)S(1)} %pad_add_fusion.place_ref, bf16[4,48,128]{2,1,0:T(8,128)(2,1)S(1)} %get-tuple-element.15.own_ref, bf16[4,48,128]{2,1,0:T(8,128)(2,1)S(1)} %collective-permute-done.7.other_ref, bf16[16,48,384]{2,1,0:T(8,128)(2,1)S(1)} %get-tuple-element.17.main_ref, ...), custom_call_target="tpu_custom_call" | custom-call | flops 21743271936 | bytes 1048576 | tf_op jit(solution)/shard_map/pallas_call | solution.py:539
  34.6 4.0 %shard_map.145 = (bf16[16,48,384]{2,1,0:T(8,128)(2,1)S(1)}, f32[16,8,384]{2,1,0:T(8,128)S(1)}, bf16[4,56,128]{2,1,0:T(8,128)(2,1)S(1)}, s32[8,128]{1,0:T(8,128)S(1)}) custom-call(s32[2]{0:T(128)S(1)} %pad_add_fusion.place_ref, f32[48,8,128]{2,1,0:T(8,128)S(1)} %get-tuple-element.19.flux_ref, bf16[64,128,128]{2,1,0:T(8,128)(2,1)S(1)} %copy-done, ...), custom_call_target="tpu_custom_call" | custom-call | bytes 1048576 | tf_op jit(solution)/shard_map/pallas_call | solution.py:539
  38.6 0.6 %collective-permute-start.12 = (bf16[4,56,128]{2,1,0:T(8,128)(2,1)S(1)}, bf16[4,56,128]{2,1,0:T(8,128)(2,1)S(1)}, u32[]{:S(2)}, u32[]{:S(2)}) collective-permute-start(bf16[4,56,128]{2,1,0:T(8,128)(2,1)S(1)} %get-tuple-element.22.own_ref), channel_id=1, source_target_pairs={{0,2},{2,0},{1,3},{3,1},{4,6},{6,4},{5,7},{7,5},{8,10},{10,8},{9,1... | collective-permute-start | bytes 172040 | tf_op jit(solution)/shard_map/ppermute | solution.py:578
  39.2 6.7 %shard_map.146.main_ref = bf16[16,40,384]{2,1,0:T(8,128)(2,1)S(1)} custom-call(bf16[16,48,384]{2,1,0:T(8,128)(2,1)S(1)} %get-tuple-element.23.field_ref, f32[16,8,384]{2,1,0:T(8,128)S(1)} %get-tuple-element.24.extra_ref, bf16[2,432,128]{2,1,0:T(8,128)(2,1)S(1)} %bitcast.13, bf16[2,360,128]{2,1,0:T(8,128)(2,1)S(1)} %bitcast.15), custom_call_target="tpu_custom_call" | custom-call | flops 9965666304 | bytes 1048576 | tf_op jit(solution)/shard_map/pallas_call | solution.py:539
  45.9 3.4 %shard_map.147 = (bf16[40,2,384]{2,1,0:T(2,128)(2,1)}, f32[2,384]{1,0:T(2,128)}) custom-call(s32[2]{0:T(128)S(1)} %pad_add_fusion.place_ref, s32[8,128]{1,0:T(8,128)S(1)} %get-tuple-element.21.table_ref, bf16[4,56,128]{2,1,0:T(8,128)(2,1)S(1)} %get-tuple-element.22.own_ref, bf16[4,56,128]{2,1,0:T(8,128)(2,1)S(1)} %collective-permute-done.12.other_ref, ...), custom_call_target="tpu_custom_call" | custom-call | bytes 1048576 | tf_op jit(solution)/shard_map/pallas_call | solution.py:539
  (28 shorter events, 0.1 us)
Async XLA Ops:
  0.6 0.9 %copy-start.3 = (bf16[48,2,384]{2,1,0:T(2,128)(2,1)S(1)}, bf16[48,2,384]{2,1,0:T(2,128)(2,1)}, u32[]{:S(2)}) copy-start(bf16[48,2,384]{2,1,0:T(2,128)(2,1)} %atmos_ref.1) | copy-start | bytes 221188
  1.7 13.3 %collective-permute-start = (bf16[2,48,384]{2,1,0:T(8,128)(2,1)S(1)}, bf16[2,48,384]{2,1,0:T(8,128)(2,1)S(1)}, u32[]{:S(2)}, u32[]{:S(2)}) collective-permute-start(bf16[2,48,384]{2,1,0:T(8,128)(2,1)S(1)} %shard_map.139.refs_0_), channel_id=1, source_target_pairs={{0,4},{4,0},{8,12},{12,8},{1,5},{5,1},{9,13},{13,9},{2,6},{6,2},{1... | collective-permute-start | bytes 221192 | tf_op jit(solution)/shard_map/ppermute | solution.py:575
  4.8 10.5 %collective-permute-start.1 = (bf16[2,48,384]{2,1,0:T(8,128)(2,1)S(1)}, bf16[2,48,384]{2,1,0:T(8,128)(2,1)S(1)}, u32[]{:S(2)}, u32[]{:S(2)}) collective-permute-start(bf16[2,48,384]{2,1,0:T(8,128)(2,1)S(1)} %shard_map.139.refs_0_), channel_id=1, source_target_pairs={{0,8},{4,12},{8,0},{12,4},{1,9},{5,13},{9,1},{13,5},{2,10},{6,14},... | collective-permute-start | bytes 221192 | tf_op jit(solution)/shard_map/ppermute | solution.py:575
  7.4 8.2 %collective-permute-start.2 = (bf16[2,48,384]{2,1,0:T(8,128)(2,1)S(1)}, bf16[2,48,384]{2,1,0:T(8,128)(2,1)S(1)}, u32[]{:S(2)}, u32[]{:S(2)}) collective-permute-start(bf16[2,48,384]{2,1,0:T(8,128)(2,1)S(1)} %shard_map.139.refs_0_), channel_id=1, source_target_pairs={{0,12},{4,8},{8,4},{12,0},{1,13},{5,9},{9,5},{13,1},{2,14},{6,10},... | collective-permute-start | bytes 221192 | tf_op jit(solution)/shard_map/ppermute | solution.py:575
  7.4 8.5 %collective-permute-start.3 = (bf16[2,48,384]{2,1,0:T(8,128)(2,1)S(1)}, bf16[2,48,384]{2,1,0:T(8,128)(2,1)S(1)}, u32[]{:S(2)}, u32[]{:S(2)}) collective-permute-start(bf16[2,48,384]{2,1,0:T(8,128)(2,1)S(1)} %shard_map.139.refs_0_), channel_id=1, source_target_pairs={{0,1},{1,0},{2,3},{3,2},{4,5},{5,4},{6,7},{7,6},{8,9},{9,8},{10,11... | collective-permute-start | bytes 221192 | tf_op jit(solution)/shard_map/ppermute | solution.py:578
  7.4 0.8 %copy-start.4 = (bf16[40,2,384]{2,1,0:T(2,128)(2,1)S(1)}, bf16[40,2,384]{2,1,0:T(2,128)(2,1)}, u32[]{:S(2)}) copy-start(bf16[40,2,384]{2,1,0:T(2,128)(2,1)} %ocean_hbm.1) | copy-start | bytes 184324
  8.2 0.7 %copy-start.5 = (s32[2,384]{1,0:T(2,128)S(1)}, s32[2,384]{1,0:T(2,128)}, u32[]{:S(2)}) copy-start(s32[2,384]{1,0:T(2,128)} %mask_hbm.1) | copy-start | bytes 9220
  8.9 0.7 %copy-start.6 = (s32[1,1,8,2]{2,3,1,0:T(2,128)S(1)}, s32[1,1,8,2]{2,3,1,0:T(2,128)}, u32[]{:S(2)}) copy-start(s32[1,1,8,2]{2,3,1,0:T(2,128)} %param.21) | copy-start | bytes 196
  9.6 0.7 %copy-start.7 = (s32[1,1,8,2]{2,3,1,0:T(2,128)S(1)}, s32[1,1,8,2]{2,3,1,0:T(2,128)}, u32[]{:S(2)}) copy-start(s32[1,1,8,2]{2,3,1,0:T(2,128)} %param.22) | copy-start | bytes 196
  10.3 0.7 %copy-start.8 = (s32[1,1,8,2]{2,3,1,0:T(2,128)S(1)}, s32[1,1,8,2]{2,3,1,0:T(2,128)}, u32[]{:S(2)}) copy-start(s32[1,1,8,2]{2,3,1,0:T(2,128)} %param.23) | copy-start | bytes 196
  11.1 14.1 %collective-permute-start.10 = (bf16[2,48,384]{2,1,0:T(8,128)(2,1)S(1)}, bf16[2,48,384]{2,1,0:T(8,128)(2,1)S(1)}, u32[]{:S(2)}, u32[]{:S(2)}) collective-permute-start(bf16[2,48,384]{2,1,0:T(8,128)(2,1)S(1)} %shard_map.142.refs_0_), channel_id=1, source_target_pairs={{0,12},{4,8},{8,4},{12,0},{1,13},{5,9},{9,5},{13,1},{2,14},{6,10},... | collective-permute-start | bytes 221192 | tf_op jit(solution)/shard_map/ppermute | solution.py:575
  15.0 1.3 %collective-permute-start.4 = (bf16[2,48,384]{2,1,0:T(8,128)(2,1)S(1)}, bf16[2,48,384]{2,1,0:T(8,128)(2,1)S(1)}, u32[]{:S(2)}, u32[]{:S(2)}) collective-permute-start(bf16[2,48,384]{2,1,0:T(8,128)(2,1)S(1)} %collective-permute-done.refs_1_), channel_id=1, source_target_pairs={{0,1},{1,0},{2,3},{3,2},{4,5},{5,4},{6,7},{7,6},{8,9},{9,8},{10,11... | collective-permute-start | bytes 221192 | tf_op jit(solution)/shard_map/ppermute | solution.py:578
  15.3 1.8 %collective-permute-start.5 = (bf16[2,48,384]{2,1,0:T(8,128)(2,1)S(1)}, bf16[2,48,384]{2,1,0:T(8,128)(2,1)S(1)}, u32[]{:S(2)}, u32[]{:S(2)}) collective-permute-start(bf16[2,48,384]{2,1,0:T(8,128)(2,1)S(1)} %collective-permute-done.1.refs_2_), channel_id=1, source_target_pairs={{0,1},{1,0},{2,3},{3,2},{4,5},{5,4},{6,7},{7,6},{8,9},{9,8},{10,11... | collective-permute-start | bytes 221192 | tf_op jit(solution)/shard_map/ppermute | solution.py:578
  15.5 1.5 %collective-permute-start.6 = (bf16[2,48,384]{2,1,0:T(8,128)(2,1)S(1)}, bf16[2,48,384]{2,1,0:T(8,128)(2,1)S(1)}, u32[]{:S(2)}, u32[]{:S(2)}) collective-permute-start(bf16[2,48,384]{2,1,0:T(8,128)(2,1)S(1)} %collective-permute-done.2.refs_3_), channel_id=1, source_target_pairs={{0,1},{1,0},{2,3},{3,2},{4,5},{5,4},{6,7},{7,6},{8,9},{9,8},{10,11... | collective-permute-start | bytes 221192 | tf_op jit(solution)/shard_map/ppermute | solution.py:578
  15.8 4.3 %copy-start.9 = (bf16[2,9,256,48]{2,3,1,0:T(8,128)(2,1)S(1)}, bf16[2,9,256,48]{2,3,1,0:T(8,128)(2,1)}, u32[]{:S(2)}) copy-start(bf16[2,9,256,48]{2,3,1,0:T(8,128)(2,1)} %param.15) | copy-start | bytes 1327108
  15.8 4.3 %copy-start.10 = (bf16[2,9,48,256]{3,2,1,0:T(8,128)(2,1)S(1)}, bf16[2,9,48,256]{3,2,1,0:T(8,128)(2,1)}, u32[]{:S(2)}) copy-start(bf16[2,9,48,256]{3,2,1,0:T(8,128)(2,1)} %param.16) | copy-start | bytes 1327108
  15.9 9.4 %collective-permute-start.8 = (bf16[2,48,384]{2,1,0:T(8,128)(2,1)S(1)}, bf16[2,48,384]{2,1,0:T(8,128)(2,1)S(1)}, u32[]{:S(2)}, u32[]{:S(2)}) collective-permute-start(bf16[2,48,384]{2,1,0:T(8,128)(2,1)S(1)} %shard_map.142.refs_0_), channel_id=1, source_target_pairs={{0,4},{4,0},{8,12},{12,8},{1,5},{5,1},{9,13},{13,9},{2,6},{6,2},{1... | collective-permute-start | bytes 221192 | tf_op jit(solution)/shard_map/ppermute | solution.py:575
  16.3 8.9 %collective-permute-start.9 = (bf16[2,48,384]{2,1,0:T(8,128)(2,1)S(1)}, bf16[2,48,384]{2,1,0:T(8,128)(2,1)S(1)}, u32[]{:S(2)}, u32[]{:S(2)}) collective-permute-start(bf16[2,48,384]{2,1,0:T(8,128)(2,1)S(1)} %shard_map.142.refs_0_), channel_id=1, source_target_pairs={{0,8},{4,12},{8,0},{12,4},{1,9},{5,13},{9,1},{13,5},{2,10},{6,14},... | collective-permute-start | bytes 221192 | tf_op jit(solution)/shard_map/ppermute | solution.py:575
  18.6 12.6 %collective-permute-start.7 = (bf16[4,48,128]{2,1,0:T(8,128)(2,1)S(1)}, bf16[4,48,128]{2,1,0:T(8,128)(2,1)S(1)}, u32[]{:S(2)}, u32[]{:S(2)}) collective-permute-start(bf16[4,48,128]{2,1,0:T(8,128)(2,1)S(1)} %get-tuple-element.15.own_ref), channel_id=1, source_target_pairs={{0,2},{2,0},{1,3},{3,1},{4,6},{6,4},{5,7},{7,5},{8,10},{10,8},{9,1... | collective-permute-start | bytes 147464 | tf_op jit(solution)/shard_map/ppermute | solution.py:578
  25.2 6.0 %copy-start.11 = (bf16[8,48]{1,0:T(8,128)(2,1)S(1)}, bf16[8,48]{1,0:T(8,128)(2,1)}, u32[]{:S(2)}) copy-start(bf16[8,48]{1,0:T(8,128)(2,1)} %proj_ref.1) | copy-start | bytes 2308
  31.1 3.4 %collective-permute-start.11 = (bf16[4,2,48,384]{3,2,1,0:T(8,128)(2,1)S(1)}, bf16[4,2,48,384]{3,2,1,0:T(8,128)(2,1)S(1)}, u32[]{:S(2)}, u32[]{:S(2)}) collective-permute-start(bf16[4,2,48,384]{3,2,1,0:T(8,128)(2,1)S(1)} %get-tuple-element.20.near_ref), channel_id=1, source_target_pairs={{0,1},{1,0},{2,3},{3,2},{4,5},{5,4},{6,7},{7,6},{8,9},{9,8},{10,11... | collective-permute-start | bytes 884744 | tf_op jit(solution)/shard_map/ppermute | solution.py:578
  31.2 3.3 %copy-start = (bf16[64,128,128]{2,1,0:T(8,128)(2,1)S(1)}, bf16[64,128,128]{2,1,0:T(8,128)(2,1)}, u32[]{:S(2)}) copy-start(bf16[64,128,128]{2,1,0:T(8,128)(2,1)} %blocks_ref.3) | copy-start | bytes 6291460
  34.6 4.6 %copy-start.1 = (bf16[2,9,128,48]{2,3,1,0:T(8,128)(2,1)S(1)}, bf16[2,9,128,48]{2,3,1,0:T(8,128)(2,1)}, u32[]{:S(2)}) copy-start(bf16[2,9,128,48]{2,3,1,0:T(8,128)(2,1)} %param.17) | copy-start | bytes 663556
  34.6 4.6 %copy-start.2 = (bf16[2,9,40,128]{3,2,1,0:T(8,128)(2,1)S(1)}, bf16[2,9,40,128]{3,2,1,0:T(8,128)(2,1)}, u32[]{:S(2)}) copy-start(bf16[2,9,40,128]{3,2,1,0:T(8,128)(2,1)} %param.18) | copy-start | bytes 552964
  38.6 7.3 %collective-permute-start.12 = (bf16[4,56,128]{2,1,0:T(8,128)(2,1)S(1)}, bf16[4,56,128]{2,1,0:T(8,128)(2,1)S(1)}, u32[]{:S(2)}, u32[]{:S(2)}) collective-permute-start(bf16[4,56,128]{2,1,0:T(8,128)(2,1)S(1)} %get-tuple-element.22.own_ref), channel_id=1, source_target_pairs={{0,2},{2,0},{1,3},{3,1},{4,6},{6,4},{5,7},{7,5},{8,10},{10,8},{9,1... | collective-permute-start | bytes 172040 | tf_op jit(solution)/shard_map/ppermute | solution.py:578

commit v3 on v2

--- a/solution.py
+++ b/solution.py
@@ -197,33 +197,31 @@
     return z[outs : 2 * outs] + west(z[0:outs]) + east(z[2 * outs : 3 * outs])
 
 
-def main_block(s_ref, w_in, w_out, chans, outs, rows, width, emit):
+def main_block(s_ref, w_in, w_out, outs, rows, width, emit, shift=1, valid=None):
+    chans = w_in.shape[1] // 9
     span = 9 * chans
     ahead, behind = None, None
-    for pair in range(rows // 2):
-        r = 2 * pair
-        taps = jnp.concatenate(
-            [
-                s_ref[r * 3 * chans : r * 3 * chans + span, :],
-                s_ref[(r + 1) * 3 * chans : (r + 1) * 3 * chans + span, :],
-            ],
-            axis=1,
-        )
-        hidden = gelu(jnp.dot(w_in, taps, preferred_element_type=F32)).astype(BF)
-        z = jnp.dot(w_out, hidden, preferred_element_type=F32)
+    for r in rows[::2]:
+        at = [(r + q - 1 + shift) * 3 * chans for q in range(2)]
+        taps = jnp.concatenate([s_ref[i : i + span, :] for i in at], axis=1)
+        hidden = gelu(jnp.dot(w_in, taps, preferred_element_type=F32))
+        if valid is not None:
+            kept = [jnp.full((1, width), valid(r + q), F32) for q in range(2)]
+            hidden = hidden * jnp.concatenate(kept, axis=1)
+        z = jnp.dot(w_out, hidden.astype(BF), preferred_element_type=F32)
         part = [
             [z[a * 3 * outs : (a + 1) * 3 * outs, q * width : (q + 1) * width] for q in range(2)]
             for a in range(3)
         ]
-        if pair > 0:
+        if ahead is not None:
             emit(r - 1, column_sum(ahead + part[2][0], outs))
-            now = behind + part[1][0] + part[2][1]
-        else:
-            now = part[1][0] + part[2][1]
-        emit(r, column_sum(now, outs))
+            emit(r, column_sum(behind + part[1][0] + part[2][1], outs))
+        elif valid is None:
+            emit(r, column_sum(part[1][0] + part[2][1], outs))
         ahead = part[0][0] + part[1][1]
         behind = part[0][1]
-    emit(rows - 1, column_sum(ahead, outs))
+    if valid is None:
+        emit(rows[-1], column_sum(ahead, outs))
 
 
 def turned(w_ref, layer):
@@ -256,27 +254,30 @@
     return jnp.where(place < EDGE, left, jnp.where(place >= 3 * EDGE, right, own))
 
 
-def strip_shift(v, a, b):
+def strip_shift(v, a, b, poles):
     width = v.shape[1]
     moved = pltpu.roll(v, (-((a - 1) * STRIP + b - 1)) % width, 1) if (a, b) != (1, 1) else v
     lane = lanes_of(v.shape)
-    if a == 0:
+    if poles and a == 0:
         moved = jnp.where(lane < STRIP, 0.0, moved)
-    if a == 2:
+    if poles and a == 2:
         moved = jnp.where(lane >= width - STRIP, 0.0, moved)
     return moved
 
 
-def strip_block(source, w_in, w_out, outs):
+def strip_block(source, w_in, w_out, outs, kept=None):
+    poles = kept is None
     taps = jnp.concatenate(
-        [strip_shift(source, a, b) for a in range(3) for b in range(3)], axis=0
+        [strip_shift(source, a, b, poles) for a in range(3) for b in range(3)], axis=0
     ).astype(BF)
-    hidden = gelu(jnp.dot(w_in, taps, preferred_element_type=F32)).astype(BF)
-    z = jnp.dot(w_out, hidden, preferred_element_type=F32)
+    hidden = gelu(jnp.dot(w_in, taps, preferred_element_type=F32))
+    if not poles:
+        hidden = hidden * kept
+    z = jnp.dot(w_out, hidden.astype(BF), preferred_element_type=F32)
     total = z[4 * outs : 5 * outs]
     for tap in range(9):
         if tap != 4:
-            total = total + strip_shift(z[tap * outs : (tap + 1) * outs], tap // 3, tap % 3)
+            total = total + strip_shift(z[tap * outs : (tap + 1) * outs], tap // 3, tap % 3, poles)
     return total
 
 
@@ -318,210 +319,267 @@
         tile_ref[r] = jnp.concatenate([state, wet, listed, rest], axis=0).astype(BF)
 
 
-def stack_kernel(place_ref, *refs):
-    tiles, (stack_ref, edge_ref) = refs[:8], refs[8:]
+def stack_kernel(place_ref, own_ref, side_ref, cross_ref, even_ref, odd_ref, stack_ref, edge_ref):
     lat, comp = place_ref[0], place_ref[1]
-    chans, width = tiles[0].shape[1:]
-    chips = edge_ref.shape[0]
-    clear_ends(stack_ref, 4 * chips, chans)
-    for k in range(chips):
+    chans, width = own_ref.shape[1:]
+    low = lat % 2 == 0
+    places = (
+        (own_ref, 2),
+        (side_ref, 3 - 2 * comp),
+        (cross_ref, 1 + 2 * comp),
+        (even_ref, jnp.where(low, 4, 0)),
+        (odd_ref, jnp.where(low, 0, 4)),
+    )
+    for tile, at in places:
+        for r in range(2):
+            store_row(stack_ref, 2 * at + r, tile[r].astype(F32), chans)
+    for q in range(edge_ref.shape[0]):
         both = jnp.zeros((chans, 128), F32)
-        for half, tile in ((comp, tiles[k]), (1 - comp, tiles[chips + k])):
-            pair = [tile[r].astype(F32) for r in range(2)]
-            for r in range(2):
-                store_row(stack_ref, 4 * (lat ^ k) + 2 * half + r + 1, pair[r], chans)
-            both = both + pltpu.roll(edges_of(pair), 64 * half, 1)
-        edge_ref[lat ^ k] = both.astype(BF)
-
-
-def first_kernel(stack_ref, win_ref, wout_ref, next_ref):
-    chans = wout_ref.shape[1] // 9
-    width = stack_ref.shape[1]
-    rows = stack_ref.shape[0] // (3 * chans) - 2
-    clear_ends(next_ref, rows, chans)
-
-    def emit(r, y):
-        base = (3 * (r + 1) + 1) * chans
-        total = stack_ref[base : base + chans, :].astype(F32) + y
-        store_row(next_ref, r + 1, total.astype(BF).astype(F32), chans)
-
-    main_block(stack_ref, turned(win_ref, 0), wout_ref[0], chans, chans, rows, width, emit)
-
-
-def second_kernel(place_ref, stack_ref, win_ref, wout_ref, *refs):
-    ocean_tiles, (out_ref, ocean_ref, sems) = refs[:4], refs[4:]
-    lat = place_ref[0]
-    rows, chans, width = out_ref.shape
-    copies = [
-        pltpu.make_async_copy(tile, ocean_ref.at[lat ^ k], sems.at[k])
-        for k, tile in enumerate(ocean_tiles)
-    ]
-    for copy in copies:
-        copy.start()
-
-    def emit(r, y):
-        base = (3 * (r + 1) + 1) * chans
-        out_ref[r] = (stack_ref[base : base + chans, :].astype(F32) + y).astype(BF)
-
-    main_block(stack_ref, turned(win_ref, 1), wout_ref[1], chans, chans, rows, width, emit)
-    for copy in copies:
-        copy.wait()
-
-
-def flux_kernel(place_ref, own_ref, other_ref, main_ref, win_ref, wout_ref, proj_ref, next_ref,
-                flux_ref, merged):
+        for half in range(2):
+            r = 4 * q + 2 * half
+            if r < stack_ref.shape[0] // (3 * chans):
+                at = [(3 * (r + i) + 1) * chans for i in range(2)]
+                ends = edges_of([stack_ref[i : i + chans, :].astype(F32) for i in at])
+                both = both + pltpu.roll(ends, 64 * half, 1)
+        edge_ref[q] = both.astype(BF)
+
+
+def centre(ref, slot, chans):
+    at = (3 * slot + 1) * chans
+    if not isinstance(at, int):
+        at = pl.multiple_of(at, 16)
+    return ref[pl.ds(at, chans), :].astype(F32)
+
+
+def window_rule(place_ref):
+    first = 4 * place_ref[0] + 2 * place_ref[1] - 4
+    limit = place_ref[2]
+    return first, lambda r: jnp.where((first + r >= 0) & (first + r < limit), 1.0, 0.0)
+
+
+def strip_of(own_ref, other_ref):
+    tiles = range(own_ref.shape[0])
+    both = [with_neighbour(own_ref[q].astype(F32), other_ref[q].astype(F32)) for q in tiles]
+    return jnp.concatenate(both, axis=1)
+
+
+def first_kernel(place_ref, stack_ref, win_ref, wout_ref, next_ref):
+    chans, width = wout_ref.shape[1] // 9, stack_ref.shape[1]
+    valid = window_rule(place_ref)[1]
+
+    def keep(r, y):
+        total = (centre(stack_ref, r, chans) + y).astype(BF).astype(F32)
+        store_row(next_ref, r, total * valid(r), chans)
+
+    main_block(stack_ref, turned(win_ref, 0), wout_ref[0], chans, range(1, 9), width, keep, 0, valid)
+
+
+def second_kernel(place_ref, stack_ref, own_ref, other_ref, win_ref, wout_ref, proj_ref, ocean_ref,
+                  next_ref, sent_ref):
+    chans, width = wout_ref.shape[1] // 9, stack_ref.shape[1]
+    per_row = width // 128
+    first, valid = window_rule(place_ref)
+    w_in = [turned(win_ref, layer) for layer in range(2)]
+    main = {}
+
+    def finish(r, y):
+        main[r - 4] = (centre(stack_ref, r, chans) + y).astype(BF).astype(F32)
+
+    strip = strip_of(own_ref, other_ref)
+    lane = lanes_of((1, strip.shape[1]))
+    inside = (lane >= -first * STRIP) & (lane < (place_ref[2] - first) * STRIP)
+    kept = jnp.where(inside, 1.0, 0.0)
+    strip = strip + strip_block(strip, w_in[0], wout_ref[0], chans, kept)
+    strip = strip.astype(BF).astype(F32) * kept
+    main_block(stack_ref, w_in[1], wout_ref[1], chans, range(3, 7), width, finish, 0, valid)
+    strip = strip + strip_block(strip, w_in[1], wout_ref[1], chans, kept)
+
+    mended = [mend_row(main[r], strip[:, 128:256], r).astype(BF) for r in range(2)]
+    for r in range(2):
+        next_ref[:, r, :] = mended[r]
+    flux = jnp.dot(proj_ref[...], jnp.concatenate(mended, axis=1), preferred_element_type=F32)
+    blocks = [flux[:, 128 * b : 128 * (b + 1)] for b in range(2 * per_row)]
+    numbers = ocean_ref[0, 32:48, 0:128].astype(F32)[9:10]
+    rest = jnp.zeros((15, 128), F32)
+    head = jnp.concatenate([*blocks, numbers, rest], axis=0).astype(BF)
+    at = head.shape[0]
+    sent_ref[0:at, :] = head
+    for r in range(2):
+        for b in range(per_row):
+            sent_ref[at : at + chans, :] = ocean_ref[r, :, 128 * b : 128 * (b + 1)]
+            at = at + chans
+
+
+def regrid_kernel(place_ref, blocks_ref, atmos_ref, *refs):
+    sent, (stack_ref, wet_ref, edge_ref, table, next_hbm, flux_ref, total, index, sem, next_sem) = (
+        refs[:8],
+        refs[8:],
+    )
+    leaving = pltpu.make_async_copy(atmos_ref, next_hbm, next_sem)
+    leaving.start()
     lat, comp = place_ref[0], place_ref[1]
-    rows, chans, width = main_ref.shape
-    per_row = width // 128
-    strip = jnp.concatenate(
-        [
-            with_neighbour(own_ref[q].astype(F32), other_ref[q].astype(F32))
-            for q in range(own_ref.shape[0])
-        ],
-        axis=1,
-    )
-    for layer in range(win_ref.shape[0]):
-        strip = strip + strip_block(strip, turned(win_ref, layer), wout_ref[layer], chans)
-        strip = strip.astype(BF).astype(F32)
-
-    for r in range(rows):
-        q = r // 4
-        row = mend_row(main_ref[r].astype(F32), strip[:, 128 * q : 128 * (q + 1)], r).astype(BF)
-        merged[r] = row
-        f = jnp.dot(proj_ref[...], row, preferred_element_type=F32)
-        for b in range(per_row):
-            flux_ref[r * per_row + b] = f[:, 128 * b : 128 * (b + 1)].astype(BF).astype(F32)
-    base = 4 * lat + 2 * comp
-    for r in range(2):
-        next_ref[:, r, :] = merged[base + r]
-
-
-def regrid_kernel(place_ref, flux_ref, blocks_ref, near_ref, far_ref, field_ref, extra_ref,
-                  edge_ref, table, total, index, sem):
-    comp = place_ref[1]
-    chips = near_ref.shape[0]
-    rows, chans, width = field_ref.shape
+    peers = len(sent)
+    chips = peers // 2
     fluxes = flux_ref.shape[1]
+    subs = flux_ref.shape[0] // peers
+    per_row = subs // 2
+    rows = wet_ref.shape[0]
+    chans = stack_ref.shape[0] // (3 * (rows + 2))
     outs = chans - fluxes
-    per_row = width // 128
-    subs = 2 * per_row
-    peers = 2 * chips
-    slots = rows
-
-    for chip in range(chips):
-        for near, tiles in ((0, near_ref), (1, far_ref)):
-            t = 2 * chip + jnp.where(comp == near, 0, 1)
-            row = tiles[chip, 0, 32:48, 0:128].astype(F32)[9:10]
-            table[pl.ds(t, 1), :] = row.astype(jnp.int32)
+    slots = 2 * peers
+    places = [2 * (lat ^ (i % chips)) + (comp if i < chips else 1 - comp) for i in range(peers)]
+    head = subs * fluxes + 16
+    for t, ref in zip(places, sent):
+        row = ref[head - 16 : head, :].astype(F32)[0:1]
+        table[pl.ds(t, 1), :] = row.astype(jnp.int32)
     copy = pltpu.make_async_copy(table, index, sem)
     copy.start()
     total[...] = jnp.zeros(total.shape, F32)
+    for t, ref in zip(places, sent):
+        values = ref[0 : head - 16, :].astype(F32)
+        for b in range(subs):
+            flux_ref[t * subs + b] = values[b * fluxes : (b + 1) * fluxes]
+    clear_ends(stack_ref, rows, chans)
     copy.wait()
 
     def one_tile(t, carry):
+        pieces = []
         for slot in range(slots):
-            source = index[t, slot]
-            live = source >= 0
-            target = jnp.where(live, index[t, slots + slot], 6)
+            source = jnp.maximum(index[t, slot], 0)
             block = blocks_ref[index[t, 2 * slots + slot]]
-            value = flux_ref[t * subs + jnp.maximum(source, 0)].astype(BF)
+            value = flux_ref[t * subs + source].astype(BF)
             piece = jnp.dot(value, block, preferred_element_type=F32)
+            pieces.append(piece.astype(BF).astype(F32))
+        for slot in range(slots):
+            target = jnp.where(index[t, slot] >= 0, index[t, slots + slot], 6)
             at = (slot % peers) * 8 + target
-            total[at] = total[at] + piece.astype(BF).astype(F32)
+            total[at] = total[at] + pieces[slot]
         return carry
 
-    lax.fori_loop(0, rows // 2, one_tile, 0)
-
-    for chip in range(chips):
+    lax.fori_loop(0, peers, one_tile, 0, unroll=2)
+
+    def tile_row(ref, r):
+        at = [head + (r * per_row + b) * chans for b in range(per_row)]
+        return jnp.concatenate([ref[i : i + chans, :] for i in at], axis=1).astype(F32)
+
+    for k in range(chips):
         both = jnp.zeros((chans + fluxes, 128), F32)
-        for near, tiles in ((0, near_ref), (1, far_ref)):
-            half = jnp.where(comp == near, 0, 1)
-            t = 2 * chip + half
+        for i in (k, chips + k):
+            t = places[i]
             ends = []
             for r in range(2):
                 arrived = jnp.concatenate(
                     [total[8 * t + r * per_row + b] for b in range(per_row)], axis=1
                 )
-                state = tiles[chip, r].astype(F32)
-                row = jnp.concatenate([state[0:outs], arrived], axis=0)
-                field_ref[2 * t + r] = row.astype(BF)
-                extra_ref[2 * t + r] = state[outs:]
+                state = tile_row(sent[i], r)
+                row = jnp.concatenate([state[0:outs], arrived.astype(BF).astype(F32)], axis=0)
+                store_row(stack_ref, 2 * t + r + 1, row, chans)
+                wet_ref[2 * t + r] = state[outs:]
                 ends.append(jnp.concatenate([row, state[outs:]], axis=0))
-            both = both + pltpu.roll(edges_of(ends), 64 * half, 1)
-        edge_ref[chip] = both.astype(BF)
-
-
-def ocean_kernel(field_ref, extra_ref, win_ref, wout_ref, out_ref, s0_ref, s1_ref):
-    rows, chans, width = field_ref.shape
-    outs = out_ref.shape[1]
-    clear_ends(s0_ref, rows, chans)
-    clear_ends(s1_ref, rows, chans)
-    for r in range(rows):
-        store_row(s0_ref, r + 1, field_ref[r].astype(F32), chans)
-    stacks = (s0_ref, s1_ref)
-    layers = win_ref.shape[0]
-    for layer in range(layers):
-        source = stacks[layer % 2]
-
-        def emit(r, y):
-            base = (3 * (r + 1) + 1) * chans
-            state = source[base : base + chans, :].astype(F32)
-            wet = extra_ref[r, 0:1, :]
-            total = wet * (state[0:outs] + y)
-            if layer == layers - 1:
-                out_ref[r] = total.astype(BF)
-            else:
-                row = jnp.concatenate([total.astype(BF).astype(F32), state[outs:]], axis=0)
-                store_row(stacks[(layer + 1) % 2], r + 1, row, chans)
-
-        main_block(source, turned(win_ref, layer), wout_ref[layer], chans, outs, rows, width, emit)
-
-
-def finish_kernel(place_ref, table_ref, own_ref, other_ref, main_ref, win_ref, wout_ref, blocks_ref,
-                  next_ref, temp_ref, surface, total, index, sem):
+            both = both + pltpu.roll(edges_of(ends), 64 * (comp if i < chips else 1 - comp), 1)
+        edge_ref[lat ^ k] = both.astype(BF)
+    leaving.wait()
+
+
+def ocean_kernel(stack_ref, wet_ref, win_ref, wout_ref, next_ref):
+    chans, outs = win_ref.shape[1] // 9, wout_ref.shape[1] // 9
+    rows, width = wet_ref.shape[0], stack_ref.shape[1]
+    clear_ends(next_ref, rows, chans)
+
+    def emit(r, y):
+        state = centre(stack_ref, r + 1, chans)
+        total = (wet_ref[r, 0:1, :] * (state[0:outs] + y)).astype(BF).astype(F32)
+        store_row(next_ref, r + 1, jnp.concatenate([total, state[outs:]], axis=0), chans)
+
+    main_block(stack_ref, turned(win_ref, 0), wout_ref[0], outs, range(rows), width, emit)
+
+
+def finish_kernel(place_ref, table_ref, stack_ref, wet_ref, own_ref, other_ref, win_ref, wout_ref,
+                  blocks_ref, next_ref, temp_ref, hidden_ref, surface, total, index, sem):
     copy = pltpu.make_async_copy(table_ref, index, sem)
     copy.start()
     lat, comp = place_ref[0], place_ref[1]
-    rows, outs, width = main_ref.shape
-    chans = win_ref.shape[1] // 9
+    t = 2 * lat + comp
+    chans, outs = win_ref.shape[1] // 9, wout_ref.shape[1] // 9
+    hidden = win_ref.shape[2]
+    rows, width = wet_ref.shape[0], stack_ref.shape[1]
     per_row = width // 128
-    strip = jnp.concatenate(
-        [
-            with_neighbour(own_ref[q].astype(F32), other_ref[q].astype(F32))
-            for q in range(own_ref.shape[0])
-        ],
-        axis=1,
-    )
+    w_in = [turned(win_ref, layer) for layer in range(2)]
+    total[...] = jnp.zeros(total.shape, F32)
+
+    strip = strip_of(own_ref, other_ref)
     wet = strip[chans : chans + 1]
     state, fixed = strip[0:outs], strip[outs:chans]
-    for layer in range(win_ref.shape[0]):
-        source = jnp.concatenate([state, fixed], axis=0)
-        state = wet * (state + strip_block(source, turned(win_ref, layer), wout_ref[layer], outs))
-        state = state.astype(BF).astype(F32)
+    state = wet * (state + strip_block(strip[0:chans], w_in[0], wout_ref[0], outs))
+    state = state.astype(BF).astype(F32)
+
+    last = wout_ref[1].astype(F32)
+    none = jnp.zeros((5, hidden), F32)
+    w_temp = jnp.concatenate(
+        [v for a in range(3) for v in (*(last[(3 * a + b) * outs][None] for b in range(3)), none)]
+        + [jnp.zeros((8, hidden), F32)],
+        axis=0,
+    ).astype(BF)
+    ends = jnp.zeros((hidden, width), BF)
+    hidden_ref[0] = ends
+    hidden_ref[rows + 1] = ends
+    parts = {}
+    for r in range(0, rows, 2):
+        at = [(r + q) * 3 * chans for q in range(2)]
+        taps = jnp.concatenate([stack_ref[i : i + 9 * chans, :] for i in at], axis=1)
+        active = gelu(jnp.dot(w_in[1], taps, preferred_element_type=F32)).astype(BF)
+        for q in range(2):
+            hidden_ref[r + q + 1] = active[:, q * width : (q + 1) * width]
+        z = jnp.dot(w_temp, active, preferred_element_type=F32)
+        for a in range(3):
+            for q in range(2):
+                part = z[8 * a : 8 * a + 8, q * width : (q + 1) * width]
+                row = r + q - a + 1
+                parts[row] = parts[row] + part if row in parts else part
+
+    source = jnp.concatenate([state, fixed], axis=0)
+    state = wet * (state + strip_block(source, w_in[1], wout_ref[1], outs))
+    state = state.astype(BF).astype(F32)
 
     for r in range(rows):
+        y = parts[r]
+        y = y[1:2] + west(y)[0:1] + east(y)[2:3]
+        top = wet_ref[r, 0:1, :] * (centre(stack_ref, r + 1, chans)[0:8] + y)
         q = r // 4
-        top = mend_row(main_ref[r, 0:16, :].astype(F32)[0:8], state[0:8, 128 * q : 128 * (q + 1)], r)
+        top = mend_row(top, state[0:8, 128 * q : 128 * (q + 1)], r)
         for b in range(per_row):
             surface[(r // 2) * 8 + (r % 2) * per_row + b] = top[:, 128 * b : 128 * (b + 1)]
 
-    base = 4 * lat + 2 * comp
-    own = jnp.zeros((outs, 128), F32)
+    edge = jnp.zeros((outs, 128), F32)
     for q in range(own_ref.shape[0]):
-        own = jnp.where(lat == q, state[:, 128 * q : 128 * (q + 1)], own)
-    own = pltpu.roll(own, jnp.where(comp == 1, 64, 0), 1)
+        edge = jnp.where(lat == q, state[:, 128 * q : 128 * (q + 1)], edge)
+    edge = pltpu.roll(edge, jnp.where(comp == 1, 64, 0), 1)
+    z = [
+        jnp.dot(
+            wout_ref[1],
+            jnp.concatenate([hidden_ref[2 * t + 2 * p + q] for q in range(2)], axis=1),
+            preferred_element_type=F32,
+        )
+        for p in range(2)
+    ]
     for r in range(2):
-        next_ref[:, r, :] = mend_row(main_ref[base + r].astype(F32), own, r).astype(BF)
-
-    total[...] = jnp.zeros(total.shape, F32)
+        y = sum(
+            z[(r + a) // 2][
+                3 * a * outs : 3 * (a + 1) * outs, (r + a) % 2 * width : ((r + a) % 2 + 1) * width
+            ]
+            for a in range(3)
+        )
+        row = centre(stack_ref, 2 * t + r + 1, chans)[0:outs] + column_sum(y, outs)
+        next_ref[:, r, :] = mend_row(wet_ref[2 * t + r, 0:1, :] * row, edge, r).astype(BF)
+
     copy.wait()
-    slots = rows
-    t = 2 * lat + comp
+    peers = rows // 2
+    slots = 2 * peers
     for slot in range(slots):
         source = index[t, slot]
         target = index[t, slots + slot]
         block = blocks_ref[index[t, 2 * slots + slot]]
-        value = surface[(slot % (rows // 2)) * 8 + target].astype(BF)
+        value = surface[(slot % peers) * 8 + target].astype(BF)
         piece = lax.dot_general(value, block, (((1,), (1,)), ((), ())), preferred_element_type=F32)
         at = jnp.where(source >= 0, source, 6)
         total[at] = total[at] + piece
@@ -531,15 +589,17 @@
         )
 
 
-def call(kernel, out_shape, operands, scratch=(), smem=1, anywhere=0, flops=0):
+def call(kernel, out_shape, operands, scratch=(), smem=1, anywhere=0, flops=0, leaving=None):
     held = len(operands) - smem - anywhere
     spaces = [pltpu.SMEM] * smem + [pltpu.VMEM] * held + [pltpu.HBM] * anywhere
-    specs = [pl.BlockSpec(memory_space=space) for space in spaces]
     out_specs = jax.tree.map(lambda _: pl.BlockSpec(memory_space=pltpu.VMEM), out_shape)
+    if leaving is not None:
+        out_shape = (*out_shape, leaving)
+        out_specs = (*out_specs, pl.BlockSpec(memory_space=pl.ANY))
     return pl.pallas_call(
         kernel,
         out_shape=out_shape,
-        in_specs=specs,
+        in_specs=[pl.BlockSpec(memory_space=space) for space in spaces],
         out_specs=out_specs,
         scratch_shapes=list(scratch),
         compiler_params=pltpu.CompilerParams(vmem_limit_bytes=40 * 2**20),
@@ -569,7 +629,7 @@
     layers, _, hidden_a, _ = atmos_in_w.shape
     hidden_o = ocean_in_w.shape[2]
     fluxes = flux_proj.shape[0]
-    place = jnp.stack([lax.axis_index("lat"), lax.axis_index("comp")]).astype(jnp.int32)
+    place = jnp.stack([lax.axis_index("lat"), lax.axis_index("comp"), rows]).astype(jnp.int32)
 
     def far(v, k):
         return lax.ppermute(v, "lat", [(i, i ^ k) for i in range(lats)])
@@ -581,7 +641,9 @@
         return 2 * layers * rows * width * 9 * hidden * (chans + outs)
 
     tile = jax.ShapeDtypeStruct((height, chans, width), BF)
-    atmos_tile = call(pack_atmos_kernel, tile, [atmos_state], smem=0)
+    atmos_tile = call(
+        pack_atmos_kernel, tile, [atmos_state], smem=0, flops=conv_flops(hidden_a, chans)
+    )
     slots = (regrid_source_block, regrid_target_block, regrid_weight_block)
     given = [*(jnp.transpose(v, (0, 1, 3, 2)) for v in slots), ocean_state, ocean_mask]
     ocean_tile = call(
@@ -592,10 +654,19 @@
         smem=0,
         anywhere=len(given),
     )
-    near = [atmos_tile] + [far(atmos_tile, k) for k in range(1, lats)]
-    column = near + [swap(v, "comp") for v in near]
-    ocean_near = [ocean_tile] + [far(ocean_tile, k) for k in range(1, lats)]
-
+    cross = [(i, i + 1) for i in range(1, tiles - 1, 2)]
+    odd = [(i, i + 1) for i in range(1, lats - 1, 2)]
+
+    def both_ways(pairs):
+        return pairs + [(j, i) for i, j in pairs]
+
+    near = [
+        atmos_tile,
+        swap(atmos_tile, "comp"),
+        lax.ppermute(atmos_tile, ("lat", "comp"), both_ways(cross)),
+        far(atmos_tile, 1),
+        lax.ppermute(atmos_tile, "lat", both_ways(odd)),
+    ]
     def taps_in(w):
         return jnp.transpose(w, (0, 1, 3, 2)).reshape(w.shape[0], 9 * w.shape[3], w.shape[2])
 
@@ -605,66 +676,62 @@
     win_a, wout_a = taps_in(atmos_in_w), taps_out(atmos_out_w)
     win_o, wout_o = taps_in(ocean_in_w), taps_out(ocean_out_w)
 
-    stack = (rows + 2) * 3 * chans
-    stack_shape = jax.ShapeDtypeStruct((stack, width), BF)
+    window = height * len(near)
+    stack_shape = (window * 3 * chans, width)
     atmos_stack, edges = call(
         stack_kernel,
-        (stack_shape, jax.ShapeDtypeStruct((lats, chans, 128), BF)),
-        [place, *column],
+        (
+            jax.ShapeDtypeStruct(stack_shape, BF),
+            jax.ShapeDtypeStruct((pl.cdiv(window * STRIP, 128), chans, 128), BF),
+        ),
+        [place, *near],
         flops=conv_flops(hidden_a, chans),
     )
     edges_other = swap(edges, "lon")
     atmos_stack = call(
         first_kernel,
-        stack_shape,
-        [atmos_stack, win_a, wout_a],
-        smem=0,
+        jax.ShapeDtypeStruct(stack_shape, BF),
+        [place, atmos_stack, win_a, wout_a],
         flops=4 * conv_flops(hidden_a, chans),
     )
-    main, ocean_near = call(
+    subs = height * width // 128
+    atmos_next, sent = call(
         second_kernel,
         (
-            jax.ShapeDtypeStruct((rows, chans, width), BF),
-            jax.ShapeDtypeStruct((lats, height, chans, width), BF),
+            jax.ShapeDtypeStruct((chans, height, width), BF),
+            jax.ShapeDtypeStruct((subs * (fluxes + chans) + 16, 128), BF),
         ),
-        [place, atmos_stack, win_a, wout_a, *ocean_near],
-        [pltpu.SemaphoreType.DMA((lats,))],
+        [place, atmos_stack, edges, edges_other, win_a, wout_a, flux_proj, ocean_tile],
         flops=4 * conv_flops(hidden_a, chans),
-        anywhere=lats,
-    )
-    ocean_far = swap(ocean_near, "comp")
-    subs = height * width // 128
-    atmos_next, flux = call(
-        flux_kernel,
-        (
-            jax.ShapeDtypeStruct((chans, height, width), BF),
-            jax.ShapeDtypeStruct((tiles * subs, fluxes, 128), F32),
-        ),
-        [place, edges, edges_other, main, win_a, wout_a, flux_proj],
-        [pltpu.VMEM((rows, chans, width), BF)],
-        flops=4 * conv_flops(hidden_a, chans),
-    )
-    field, extra, ocean_edges, table = call(
+    )
+    others = {k: far(sent, k) for k in reversed(range(1, lats))}
+    sent = [sent] + [others[k] for k in range(1, lats)]
+    sent = sent + [swap(v, "comp") for v in sent]
+    stack_shape = ((rows + 2) * 3 * chans, width)
+    ocean_stack, wet, ocean_edges, table, atmos_next = call(
         regrid_kernel,
         (
-            jax.ShapeDtypeStruct((rows, chans, width), BF),
+            jax.ShapeDtypeStruct(stack_shape, BF),
             jax.ShapeDtypeStruct((rows, fluxes, width), F32),
             jax.ShapeDtypeStruct((lats, chans + fluxes, 128), BF),
             jax.ShapeDtypeStruct((tiles, 128), jnp.int32),
         ),
-        [place, flux, regrid_blocks, ocean_near, ocean_far],
+        [place, regrid_blocks, atmos_next, *sent],
         [
+            pltpu.VMEM((tiles * subs, fluxes, 128), F32),
             pltpu.VMEM((tiles * 8, fluxes, 128), F32),
             pltpu.SMEM((tiles, 128), jnp.int32),
             pltpu.SemaphoreType.DMA,
+            pltpu.SemaphoreType.DMA,
         ],
+        flops=conv_flops(hidden_o, outs),
+        leaving=jax.ShapeDtypeStruct((chans, height, width), BF),
     )
     ocean_edges_other = swap(ocean_edges, "lon")
-    ocean_main = call(
+    ocean_stack = call(
         ocean_kernel,
-        jax.ShapeDtypeStruct((rows, outs, width), BF),
-        [field, extra, win_o, wout_o],
-        [pltpu.VMEM((stack, width), BF), pltpu.VMEM((stack, width), BF)],
+        jax.ShapeDtypeStruct(stack_shape, BF),
+        [ocean_stack, wet, win_o, wout_o],
         smem=0,
         flops=4 * conv_flops(hidden_o, outs),
     )
@@ -674,8 +741,19 @@
             jax.ShapeDtypeStruct((outs, height, width), BF),
             jax.ShapeDtypeStruct((height, width), F32),
         ),
-        [place, table, ocean_edges, ocean_edges_other, ocean_main, win_o, wout_o, regrid_blocks],
         [
+            place,
+            table,
+            ocean_stack,
+            wet,
+            ocean_edges,
+            ocean_edges_other,
+            win_o,
+            wout_o,
+            regrid_blocks,
+        ],
+        [
+            pltpu.VMEM((rows + 2, hidden_o, width), BF),
             pltpu.VMEM((tiles * 8, 8, 128), F32),
             pltpu.VMEM((8, 8, 128), F32),
             pltpu.SMEM((tiles, 128), jnp.int32),

time: 49.8 us -> 47.8 us (0.960)
  Pallas kernels: 30.2 us -> 21.3 us
  waiting for transfers between devices: 0.41 us -> 9.14 us
  local copies, waits for them, and re-layouts: 4.45 us -> 0.97 us
  starting transfers between devices: 13.3 us -> 15.1 us
    pallas_call x9 -> x8, Pallas kernels: 30.2 us -> 21.3 us  [call(): pl.pallas_call(kernel, out_shape=out_shape, in_specs=[pl.BlockSpec(memory...]
    ppermute x6 -> x4, waiting for transfers between devices: 0.02 us -> 8.1 us  [far(): return lax.ppermute(v, 'lat', [(i, i ^ k) for i in range(lats)])]
    unnamed x24, local copies, waits for them, and re-layouts: 4.45 us -> 0.97 us
    ppermute x0 -> x2, starting transfers between devices: none -> 1.31 us  [the longest x1 0.65 us: column_device(): lax.ppermute(atmos_tile, ('lat', 'comp'), both_ways(cross))]
    ppermute x7, starting transfers between devices: 2.97 us -> 3.96 us  [swap(): return lax.ppermute(v, axis, [(0, 1), (1, 0)])]
    ppermute x7, waiting for transfers between devices: 0.39 us -> 1.04 us  [swap(): return lax.ppermute(v, axis, [(0, 1), (1, 0)])]
    ppermute x6 -> x4, starting transfers between devices: 10.4 us -> 9.85 us  [far(): return lax.ppermute(v, 'lat', [(i, i ^ k) for i in range(lats)])]
  transfers between devices with their start and end apart: 13 -> 13, of which waited for: 1 -> 6; matrix products, arithmetic and copies ran while one was open for 0% -> 0% of each run, Pallas kernels for 46% -> 15%
where the time goes in v3:
time: 47.8 us; the launch traced here: 47.6 us
  Pallas kernels  21.3 us (45%)
  starting transfers between devices  15.1 us (32%)
  waiting for transfers between devices  9.14 us (19%)
  between operations  1 us (2%)
  local copies, waits for them, and re-layouts  0.97 us (2%)
    pallas_call x8, Pallas kernels, call(): pl.pallas_call(kernel, out_shape=out_shape, in_specs=[pl.BlockSpec(memory...  21.3 us
    ppermute x4, starting transfers between devices, far(): return lax.ppermute(v, 'lat', [(i, i ^ k) for i in range(lats)])  9.85 us
    ppermute x4, waiting for transfers between devices, far(): return lax.ppermute(v, 'lat', [(i, i ^ k) for i in range(lats)])  8.1 us
    ppermute x7, starting transfers between devices, swap(): return lax.ppermute(v, axis, [(0, 1), (1, 0)])  3.96 us
    ppermute x7, waiting for transfers between devices, swap(): return lax.ppermute(v, axis, [(0, 1), (1, 0)])  1.04 us
    unnamed x24, local copies, waits for them, and re-layouts  0.97 us
  transfers between devices with their start and end apart: 13, of which 6 were waited for; matrix products, arithmetic and copies ran while one was open for 0% of the time, Pallas kernels for 15%

profile of v3, /device:TPU:0, one launch (start us, length us, event | category | flops | bytes accessed | tf_op | source)
XLA Modules:
  0.0 47.6 jit_solution(14685213902046708234)
XLA Ops:
  0.7 0.9 %copy-done.10 = bf16[48,2,384]{2,1,0:T(2,128)(2,1)S(1)} copy-done((bf16[48,2,384]{2,1,0:T(2,128)(2,1)S(1)}, bf16[48,2,384]{2,1,0:T(2,128)(2,1)}, u32[]{:S(2)}) %copy-start.10) | copy-done | bytes 73752
  1.6 0.2 shard_map.139.own_ref
  1.8 0.5 %collective-permute-start = (bf16[2,48,384]{2,1,0:T(8,128)(2,1)S(1)}, bf16[2,48,384]{2,1,0:T(8,128)(2,1)S(1)}, u32[]{:S(2)}, u32[]{:S(2)}) collective-permute-start(bf16[2,48,384]{2,1,0:T(8,128)(2,1)S(1)} %shard_map.139.own_ref), channel_id=1, source_target_pairs={{0,1},{1,0},{2,3},{3,2},{4,5},{5,4},{6,7},{7,6},{8,9},{9,8},{10,11... | collective-permute-start | bytes 221192 | tf_op jit(solution)/shard_map/ppermute | solution.py:638
  2.3 0.7 %collective-permute-start.1 = (bf16[2,48,384]{2,1,0:T(8,128)(2,1)S(1)}, bf16[2,48,384]{2,1,0:T(8,128)(2,1)S(1)}, u32[]{:S(2)}, u32[]{:S(2)}) collective-permute-start(bf16[2,48,384]{2,1,0:T(8,128)(2,1)S(1)} %shard_map.139.own_ref), channel_id=1, source_target_pairs={{1,4},{5,8},{9,12},{4,1},{8,5},{12,9},{3,6},{7,10},{11,14},{6,3},{... | collective-permute-start | bytes 221192 | tf_op jit(solution)/shard_map/ppermute | solution.py:666
  3.0 3.9 %collective-permute-start.2 = (bf16[2,48,384]{2,1,0:T(8,128)(2,1)S(1)}, bf16[2,48,384]{2,1,0:T(8,128)(2,1)S(1)}, u32[]{:S(2)}, u32[]{:S(2)}) collective-permute-start(bf16[2,48,384]{2,1,0:T(8,128)(2,1)S(1)} %shard_map.139.own_ref), channel_id=1, source_target_pairs={{0,4},{4,0},{8,12},{12,8},{1,5},{5,1},{9,13},{13,9},{2,6},{6,2},{1... | collective-permute-start | bytes 221192 | tf_op jit(solution)/shard_map/ppermute | solution.py:635
  6.9 0.7 %collective-permute-start.3 = (bf16[2,48,384]{2,1,0:T(8,128)(2,1)S(1)}, bf16[2,48,384]{2,1,0:T(8,128)(2,1)S(1)}, u32[]{:S(2)}, u32[]{:S(2)}) collective-permute-start(bf16[2,48,384]{2,1,0:T(8,128)(2,1)S(1)} %shard_map.139.own_ref), channel_id=1, source_target_pairs={{4,8},{8,4},{5,9},{9,5},{6,10},{10,6},{7,11},{11,7},{20,24},{24,20... | collective-permute-start | bytes 221192 | tf_op jit(solution)/shard_map/ppermute | solution.py:668
  7.6 0.2 shard_map.142.ocean_ref
  7.8 0.1 pad_add_fusion.place_ref
  7.9 0.0 collective-permute-done.side_ref
  7.9 0.0 collective-permute-done.1.cross_ref
  7.9 2.3 %collective-permute-done.2.even_ref = bf16[2,48,384]{2,1,0:T(8,128)(2,1)S(1)} collective-permute-done((bf16[2,48,384]{2,1,0:T(8,128)(2,1)S(1)}, bf16[2,48,384]{2,1,0:T(8,128)(2,1)S(1)}, u32[]{:S(2)}, u32[]{:S(2)}) %collective-permute-start.2) | collective-permute-done | bytes 73760 | tf_op jit(solution)/shard_map/ppermute | solution.py:635
  10.2 0.0 collective-permute-done.3.odd_ref
  10.2 1.0 %shard_map.140 = (bf16[1440,384]{1,0:T(8,128)(2,1)S(1)}, bf16[3,48,128]{2,1,0:T(8,128)(2,1)S(1)}) custom-call(s32[3]{0:T(128)S(1)} %pad_add_fusion.place_ref, bf16[2,48,384]{2,1,0:T(8,128)(2,1)S(1)} %shard_map.139.own_ref, bf16[2,48,384]{2,1,0:T(8,128)(2,1)S(1)} %collective-permute-done.side_ref, bf16[2,48,384]{2,1,0:T(8,128)(2,1)S(1)} %collective-permute-done.1.cross_ref, ...), custom_call_target="tpu_custom_call" | custom-call | flops 5435817984 | bytes 1048576 | tf_op jit(solution)/shard_map/pallas_call | solution.py:599
  11.2 2.6 %collective-permute-start.4 = (bf16[3,48,128]{2,1,0:T(8,128)(2,1)S(1)}, bf16[3,48,128]{2,1,0:T(8,128)(2,1)S(1)}, u32[]{:S(2)}, u32[]{:S(2)}) collective-permute-start(bf16[3,48,128]{2,1,0:T(8,128)(2,1)S(1)} %get-tuple-element.15.own_ref), channel_id=1, source_target_pairs={{0,2},{2,0},{1,3},{3,1},{4,6},{6,4},{5,7},{7,5},{8,10},{10,8},{9,1... | collective-permute-start | bytes 110600 | tf_op jit(solution)/shard_map/ppermute | solution.py:638
  13.8 3.3 %shard_map.141.stack_ref = bf16[1440,384]{1,0:T(8,128)(2,1)S(1)} custom-call(s32[3]{0:T(128)S(1)} %pad_add_fusion.place_ref, bf16[1440,384]{1,0:T(8,128)(2,1)S(1)} %get-tuple-element.14.stack_ref, bf16[2,432,256]{2,1,0:T(8,128)(2,1)S(1)} %bitcast.20, bf16[2,432,256]{2,1,0:T(8,128)(2,1)S(1)} %bitcast.22), custom_call_target="tpu_custom_call" | custom-call | flops 21743271936 | bytes 1048576 | tf_op jit(solution)/shard_map/pallas_call | solution.py:599
  17.2 0.0 copy-start
  17.2 0.0 collective-permute-done.4.other_ref
  17.2 3.3 %shard_map.143 = (bf16[48,2,384]{2,1,0:T(2,128)(2,1)S(1)}, bf16[352,128]{1,0:T(8,128)(2,1)S(1)}) custom-call(s32[3]{0:T(128)S(1)} %pad_add_fusion.place_ref, bf16[1440,384]{1,0:T(8,128)(2,1)S(1)} %shard_map.141.stack_ref, bf16[3,48,128]{2,1,0:T(8,128)(2,1)S(1)} %get-tuple-element.15.own_ref, bf16[3,48,128]{2,1,0:T(8,128)(2,1)S(1)} %collective-permute-done.4.other_ref, ...), custom_call_target="tpu_custom_call" | custom-call | flops 21743271936 | bytes 1048576 | tf_op jit(solution)/shard_map/pallas_call | solution.py:599
  20.4 5.0 %collective-permute-start.6 = (bf16[352,128]{1,0:T(8,128)(2,1)S(1)}, bf16[352,128]{1,0:T(8,128)(2,1)S(1)}, u32[]{:S(2)}, u32[]{:S(2)}) collective-permute-start(bf16[352,128]{1,0:T(8,128)(2,1)S(1)} %get-tuple-element.17.refs_0_), channel_id=1, source_target_pairs={{0,8},{4,12},{8,0},{12,4},{1,9},{5,13},{9,1},{13,5},{2,10},{6,14},... | collective-permute-start | bytes 270344 | tf_op jit(solution)/shard_map/ppermute | solution.py:635
  25.5 0.9 %collective-permute-start.7 = (bf16[352,128]{1,0:T(8,128)(2,1)S(1)}, bf16[352,128]{1,0:T(8,128)(2,1)S(1)}, u32[]{:S(2)}, u32[]{:S(2)}) collective-permute-start(bf16[352,128]{1,0:T(8,128)(2,1)S(1)} %get-tuple-element.17.refs_0_), channel_id=1, source_target_pairs={{0,12},{4,8},{8,4},{12,0},{1,13},{5,9},{9,5},{13,1},{2,14},{6,10},... | collective-permute-start | bytes 270344 | tf_op jit(solution)/shard_map/ppermute | solution.py:635
  26.4 0.0 collective-permute-start.5
  26.4 0.0 collective-permute-start.8
  26.4 3.9 %collective-permute-done.6.refs_2_ = bf16[352,128]{1,0:T(8,128)(2,1)S(1)} collective-permute-done((bf16[352,128]{1,0:T(8,128)(2,1)S(1)}, bf16[352,128]{1,0:T(8,128)(2,1)S(1)}, u32[]{:S(2)}, u32[]{:S(2)}) %collective-permute-start.6) | collective-permute-done | bytes 90144 | tf_op jit(solution)/shard_map/ppermute | solution.py:635
  30.3 1.6 %collective-permute-done.7.refs_3_ = bf16[352,128]{1,0:T(8,128)(2,1)S(1)} collective-permute-done((bf16[352,128]{1,0:T(8,128)(2,1)S(1)}, bf16[352,128]{1,0:T(8,128)(2,1)S(1)}, u32[]{:S(2)}, u32[]{:S(2)}) %collective-permute-start.7) | collective-permute-done | bytes 90144 | tf_op jit(solution)/shard_map/ppermute | solution.py:635
  32.0 0.3 collective-permute-done.5.refs_1_
  32.2 0.3 collective-permute-start.9
  32.5 0.8 %collective-permute-done.11.refs_7_ = bf16[352,128]{1,0:T(8,128)(2,1)S(1)} collective-permute-done((bf16[352,128]{1,0:T(8,128)(2,1)S(1)}, bf16[352,128]{1,0:T(8,128)(2,1)S(1)}, u32[]{:S(2)}, u32[]{:S(2)}) %collective-permute-start.11) | collective-permute-done | bytes 90144 | tf_op jit(solution)/shard_map/ppermute | solution.py:638
  33.2 0.3 collective-permute-done.9.refs_5_
  33.5 4.0 %shard_map.144 = (bf16[2592,384]{1,0:T(8,128)(2,1)S(1)}, f32[16,8,384]{2,1,0:T(8,128)S(1)}, bf16[4,56,128]{2,1,0:T(8,128)(2,1)S(1)}, s32[8,128]{1,0:T(8,128)S(1)}, bf16[48,2,384]{2,1,0:T(2,128)(2,1)}) custom-call(s32[3]{0:T(128)S(1)} %pad_add_fusion.place_ref, bf16[64,128,128]{2,1,0:T(8,128)(2,1)S(1)} %copy-done, ...), custom_call_target="tpu_custom_call" | custom-call | flops 2491416576 | bytes 1048576 | tf_op jit(solution)/shard_map/pallas_call | solution.py:599
  37.5 0.6 %collective-permute-start.12 = (bf16[4,56,128]{2,1,0:T(8,128)(2,1)S(1)}, bf16[4,56,128]{2,1,0:T(8,128)(2,1)S(1)}, u32[]{:S(2)}, u32[]{:S(2)}) collective-permute-start(bf16[4,56,128]{2,1,0:T(8,128)(2,1)S(1)} %get-tuple-element.22.own_ref), channel_id=1, source_target_pairs={{0,2},{2,0},{1,3},{3,1},{4,6},{6,4},{5,7},{7,5},{8,10},{10,8},{9,1... | collective-permute-start | bytes 172040 | tf_op jit(solution)/shard_map/ppermute | solution.py:638
  38.1 3.7 %shard_map.145.stack_ref = bf16[2592,384]{1,0:T(8,128)(2,1)S(1)} custom-call(bf16[2592,384]{1,0:T(8,128)(2,1)S(1)} %get-tuple-element.20.stack_ref, f32[16,8,384]{2,1,0:T(8,128)S(1)} %get-tuple-element.21.wet_ref, bf16[2,432,128]{2,1,0:T(8,128)(2,1)S(1)} %bitcast.13, bf16[2,360,128]{2,1,0:T(8,128)(2,1)S(1)} %bitcast.15), custom_call_target="tpu_custom_call" | custom-call | flops 9965666304 | bytes 1048576 | tf_op jit(solution)/shard_map/pallas_call | solution.py:599
  41.8 5.6 %shard_map.146 = (bf16[40,2,384]{2,1,0:T(2,128)(2,1)}, f32[2,384]{1,0:T(2,128)}) custom-call(s32[3]{0:T(128)S(1)} %pad_add_fusion.place_ref, s32[8,128]{1,0:T(8,128)S(1)} %get-tuple-element.19.table_ref, bf16[2592,384]{1,0:T(8,128)(2,1)S(1)} %shard_map.145.stack_ref, f32[16,8,384]{2,1,0:T(8,128)S(1)} %get-tuple-element.21.wet_ref, ...), custom_call_target="tpu_custom_call" | custom-call | bytes 1048576 | tf_op jit(solution)/shard_map/pallas_call | solution.py:599
  (27 shorter events, 0.1 us)
Async XLA Ops:
  0.6 6.9 %copy-start.5 = (s32[1,1,8,2]{2,3,1,0:T(2,128)S(1)}, s32[1,1,8,2]{2,3,1,0:T(2,128)}, u32[]{:S(2)}) copy-start(s32[1,1,8,2]{2,3,1,0:T(2,128)} %param.21) | copy-start | bytes 196
  0.6 6.9 %copy-start.6 = (s32[1,1,8,2]{2,3,1,0:T(2,128)S(1)}, s32[1,1,8,2]{2,3,1,0:T(2,128)}, u32[]{:S(2)}) copy-start(s32[1,1,8,2]{2,3,1,0:T(2,128)} %param.22) | copy-start | bytes 196
  0.7 6.9 %copy-start.7 = (s32[1,1,8,2]{2,3,1,0:T(2,128)S(1)}, s32[1,1,8,2]{2,3,1,0:T(2,128)}, u32[]{:S(2)}) copy-start(s32[1,1,8,2]{2,3,1,0:T(2,128)} %param.23) | copy-start | bytes 196
  0.7 6.9 %copy-start.3 = (bf16[40,2,384]{2,1,0:T(2,128)(2,1)S(1)}, bf16[40,2,384]{2,1,0:T(2,128)(2,1)}, u32[]{:S(2)}) copy-start(bf16[40,2,384]{2,1,0:T(2,128)(2,1)} %ocean_hbm.1) | copy-start | bytes 184324
  0.7 6.9 %copy-start.4 = (s32[2,384]{1,0:T(2,128)S(1)}, s32[2,384]{1,0:T(2,128)}, u32[]{:S(2)}) copy-start(s32[2,384]{1,0:T(2,128)} %mask_hbm.1) | copy-start | bytes 9220
  0.7 0.9 %copy-start.10 = (bf16[48,2,384]{2,1,0:T(2,128)(2,1)S(1)}, bf16[48,2,384]{2,1,0:T(2,128)(2,1)}, u32[]{:S(2)}) copy-start(bf16[48,2,384]{2,1,0:T(2,128)(2,1)} %atmos_ref.1) | copy-start | bytes 221188
  1.8 6.1 %collective-permute-start = (bf16[2,48,384]{2,1,0:T(8,128)(2,1)S(1)}, bf16[2,48,384]{2,1,0:T(8,128)(2,1)S(1)}, u32[]{:S(2)}, u32[]{:S(2)}) collective-permute-start(bf16[2,48,384]{2,1,0:T(8,128)(2,1)S(1)} %shard_map.139.own_ref), channel_id=1, source_target_pairs={{0,1},{1,0},{2,3},{3,2},{4,5},{5,4},{6,7},{7,6},{8,9},{9,8},{10,11... | collective-permute-start | bytes 221192 | tf_op jit(solution)/shard_map/ppermute | solution.py:638
  2.3 5.6 %collective-permute-start.1 = (bf16[2,48,384]{2,1,0:T(8,128)(2,1)S(1)}, bf16[2,48,384]{2,1,0:T(8,128)(2,1)S(1)}, u32[]{:S(2)}, u32[]{:S(2)}) collective-permute-start(bf16[2,48,384]{2,1,0:T(8,128)(2,1)S(1)} %shard_map.139.own_ref), channel_id=1, source_target_pairs={{1,4},{5,8},{9,12},{4,1},{8,5},{12,9},{3,6},{7,10},{11,14},{6,3},{... | collective-permute-start | bytes 221192 | tf_op jit(solution)/shard_map/ppermute | solution.py:666
  3.0 7.2 %collective-permute-start.2 = (bf16[2,48,384]{2,1,0:T(8,128)(2,1)S(1)}, bf16[2,48,384]{2,1,0:T(8,128)(2,1)S(1)}, u32[]{:S(2)}, u32[]{:S(2)}) collective-permute-start(bf16[2,48,384]{2,1,0:T(8,128)(2,1)S(1)} %shard_map.139.own_ref), channel_id=1, source_target_pairs={{0,4},{4,0},{8,12},{12,8},{1,5},{5,1},{9,13},{13,9},{2,6},{6,2},{1... | collective-permute-start | bytes 221192 | tf_op jit(solution)/shard_map/ppermute | solution.py:635
  6.9 3.3 %collective-permute-start.3 = (bf16[2,48,384]{2,1,0:T(8,128)(2,1)S(1)}, bf16[2,48,384]{2,1,0:T(8,128)(2,1)S(1)}, u32[]{:S(2)}, u32[]{:S(2)}) collective-permute-start(bf16[2,48,384]{2,1,0:T(8,128)(2,1)S(1)} %shard_map.139.own_ref), channel_id=1, source_target_pairs={{4,8},{8,4},{5,9},{9,5},{6,10},{10,6},{7,11},{11,7},{20,24},{24,20... | collective-permute-start | bytes 221192 | tf_op jit(solution)/shard_map/ppermute | solution.py:668
  7.9 5.9 %copy-start.8 = (bf16[2,9,256,48]{2,3,1,0:T(8,128)(2,1)S(1)}, bf16[2,9,256,48]{2,3,1,0:T(8,128)(2,1)}, u32[]{:S(2)}) copy-start(bf16[2,9,256,48]{2,3,1,0:T(8,128)(2,1)} %param.15) | copy-start | bytes 1327108
  7.9 5.9 %copy-start.9 = (bf16[2,9,48,256]{3,2,1,0:T(8,128)(2,1)S(1)}, bf16[2,9,48,256]{3,2,1,0:T(8,128)(2,1)}, u32[]{:S(2)}) copy-start(bf16[2,9,48,256]{3,2,1,0:T(8,128)(2,1)} %param.16) | copy-start | bytes 1327108
  11.2 5.9 %collective-permute-start.4 = (bf16[3,48,128]{2,1,0:T(8,128)(2,1)S(1)}, bf16[3,48,128]{2,1,0:T(8,128)(2,1)S(1)}, u32[]{:S(2)}, u32[]{:S(2)}) collective-permute-start(bf16[3,48,128]{2,1,0:T(8,128)(2,1)S(1)} %get-tuple-element.15.own_ref), channel_id=1, source_target_pairs={{0,2},{2,0},{1,3},{3,1},{4,6},{6,4},{5,7},{7,5},{8,10},{10,8},{9,1... | collective-permute-start | bytes 110600 | tf_op jit(solution)/shard_map/ppermute | solution.py:638
  13.8 3.4 %copy-start.11 = (bf16[8,48]{1,0:T(8,128)(2,1)S(1)}, bf16[8,48]{1,0:T(8,128)(2,1)}, u32[]{:S(2)}) copy-start(bf16[8,48]{1,0:T(8,128)(2,1)} %proj_ref.1) | copy-start | bytes 2308
  17.2 16.4 %copy-start = (bf16[64,128,128]{2,1,0:T(8,128)(2,1)S(1)}, bf16[64,128,128]{2,1,0:T(8,128)(2,1)}, u32[]{:S(2)}) copy-start(bf16[64,128,128]{2,1,0:T(8,128)(2,1)} %blocks_ref.3) | copy-start | bytes 6291460
  20.4 9.9 %collective-permute-start.6 = (bf16[352,128]{1,0:T(8,128)(2,1)S(1)}, bf16[352,128]{1,0:T(8,128)(2,1)S(1)}, u32[]{:S(2)}, u32[]{:S(2)}) collective-permute-start(bf16[352,128]{1,0:T(8,128)(2,1)S(1)} %get-tuple-element.17.refs_0_), channel_id=1, source_target_pairs={{0,8},{4,12},{8,0},{12,4},{1,9},{5,13},{9,1},{13,5},{2,10},{6,14},... | collective-permute-start | bytes 270344 | tf_op jit(solution)/shard_map/ppermute | solution.py:635
  25.5 6.5 %collective-permute-start.7 = (bf16[352,128]{1,0:T(8,128)(2,1)S(1)}, bf16[352,128]{1,0:T(8,128)(2,1)S(1)}, u32[]{:S(2)}, u32[]{:S(2)}) collective-permute-start(bf16[352,128]{1,0:T(8,128)(2,1)S(1)} %get-tuple-element.17.refs_0_), channel_id=1, source_target_pairs={{0,12},{4,8},{8,4},{12,0},{1,13},{5,9},{9,5},{13,1},{2,14},{6,10},... | collective-permute-start | bytes 270344 | tf_op jit(solution)/shard_map/ppermute | solution.py:635
  26.4 5.8 %collective-permute-start.5 = (bf16[352,128]{1,0:T(8,128)(2,1)S(1)}, bf16[352,128]{1,0:T(8,128)(2,1)S(1)}, u32[]{:S(2)}, u32[]{:S(2)}) collective-permute-start(bf16[352,128]{1,0:T(8,128)(2,1)S(1)} %get-tuple-element.17.refs_0_), channel_id=1, source_target_pairs={{0,4},{4,0},{8,12},{12,8},{1,5},{5,1},{9,13},{13,9},{2,6},{6,2},{1... | collective-permute-start | bytes 270344 | tf_op jit(solution)/shard_map/ppermute | solution.py:635
  26.4 6.1 %collective-permute-start.8 = (bf16[352,128]{1,0:T(8,128)(2,1)S(1)}, bf16[352,128]{1,0:T(8,128)(2,1)S(1)}, u32[]{:S(2)}, u32[]{:S(2)}) collective-permute-start(bf16[352,128]{1,0:T(8,128)(2,1)S(1)} %get-tuple-element.17.refs_0_), channel_id=1, source_target_pairs={{0,1},{1,0},{2,3},{3,2},{4,5},{5,4},{6,7},{7,6},{8,9},{9,8},{10,11... | collective-permute-start | bytes 270344 | tf_op jit(solution)/shard_map/ppermute | solution.py:638
  30.3 2.2 %collective-permute-start.10 = (bf16[352,128]{1,0:T(8,128)(2,1)S(1)}, bf16[352,128]{1,0:T(8,128)(2,1)S(1)}, u32[]{:S(2)}, u32[]{:S(2)}) collective-permute-start(bf16[352,128]{1,0:T(8,128)(2,1)S(1)} %collective-permute-done.6.refs_2_), channel_id=1, source_target_pairs={{0,1},{1,0},{2,3},{3,2},{4,5},{5,4},{6,7},{7,6},{8,9},{9,8},{10,11... | collective-permute-start | bytes 270344 | tf_op jit(solution)/shard_map/ppermute | solution.py:638
  32.0 1.3 %collective-permute-start.11 = (bf16[352,128]{1,0:T(8,128)(2,1)S(1)}, bf16[352,128]{1,0:T(8,128)(2,1)S(1)}, u32[]{:S(2)}, u32[]{:S(2)}) collective-permute-start(bf16[352,128]{1,0:T(8,128)(2,1)S(1)} %collective-permute-done.7.refs_3_), channel_id=1, source_target_pairs={{0,1},{1,0},{2,3},{3,2},{4,5},{5,4},{6,7},{7,6},{8,9},{9,8},{10,11... | collective-permute-start | bytes 270344 | tf_op jit(solution)/shard_map/ppermute | solution.py:638
  32.2 1.3 %collective-permute-start.9 = (bf16[352,128]{1,0:T(8,128)(2,1)S(1)}, bf16[352,128]{1,0:T(8,128)(2,1)S(1)}, u32[]{:S(2)}, u32[]{:S(2)}) collective-permute-start(bf16[352,128]{1,0:T(8,128)(2,1)S(1)} %collective-permute-done.5.refs_1_), channel_id=1, source_target_pairs={{0,1},{1,0},{2,3},{3,2},{4,5},{5,4},{6,7},{7,6},{8,9},{9,8},{10,11... | collective-permute-start | bytes 270344 | tf_op jit(solution)/shard_map/ppermute | solution.py:638
  33.5 4.6 %copy-start.1 = (bf16[2,9,128,48]{2,3,1,0:T(8,128)(2,1)S(1)}, bf16[2,9,128,48]{2,3,1,0:T(8,128)(2,1)}, u32[]{:S(2)}) copy-start(bf16[2,9,128,48]{2,3,1,0:T(8,128)(2,1)} %param.17) | copy-start | bytes 663556
  33.5 4.6 %copy-start.2 = (bf16[2,9,40,128]{3,2,1,0:T(8,128)(2,1)S(1)}, bf16[2,9,40,128]{3,2,1,0:T(8,128)(2,1)}, u32[]{:S(2)}) copy-start(bf16[2,9,40,128]{3,2,1,0:T(8,128)(2,1)} %param.18) | copy-start | bytes 552964
  37.5 4.3 %collective-permute-start.12 = (bf16[4,56,128]{2,1,0:T(8,128)(2,1)S(1)}, bf16[4,56,128]{2,1,0:T(8,128)(2,1)S(1)}, u32[]{:S(2)}, u32[]{:S(2)}) collective-permute-start(bf16[4,56,128]{2,1,0:T(8,128)(2,1)S(1)} %get-tuple-element.22.own_ref), channel_id=1, source_target_pairs={{0,2},{2,0},{1,3},{3,1},{4,6},{6,4},{5,7},{7,5},{8,10},{10,8},{9,1... | collective-permute-start | bytes 172040 | tf_op jit(solution)/shard_map/ppermute | solution.py:638

commit v4 on v3

--- a/solution.py
+++ b/solution.py
@@ -322,6 +322,7 @@
 def stack_kernel(place_ref, own_ref, side_ref, cross_ref, even_ref, odd_ref, stack_ref, edge_ref):
     lat, comp = place_ref[0], place_ref[1]
     chans, width = own_ref.shape[1:]
+    valid = window_rule(place_ref)[1]
     low = lat % 2 == 0
     places = (
         (own_ref, 2),
@@ -332,7 +333,8 @@
     )
     for tile, at in places:
         for r in range(2):
-            store_row(stack_ref, 2 * at + r, tile[r].astype(F32), chans)
+            row = 2 * at + r
+            store_row(stack_ref, row, tile[r].astype(F32) * valid(row), chans)
     for q in range(edge_ref.shape[0]):
         both = jnp.zeros((chans, 128), F32)
         for half in range(2):
@@ -400,14 +402,13 @@
     flux = jnp.dot(proj_ref[...], jnp.concatenate(mended, axis=1), preferred_element_type=F32)
     blocks = [flux[:, 128 * b : 128 * (b + 1)] for b in range(2 * per_row)]
     numbers = ocean_ref[0, 32:48, 0:128].astype(F32)[9:10]
-    rest = jnp.zeros((15, 128), F32)
-    head = jnp.concatenate([*blocks, numbers, rest], axis=0).astype(BF)
-    at = head.shape[0]
-    sent_ref[0:at, :] = head
-    for r in range(2):
-        for b in range(per_row):
-            sent_ref[at : at + chans, :] = ocean_ref[r, :, 128 * b : 128 * (b + 1)]
-            at = at + chans
+    state = [ocean_ref[r].astype(F32) for r in range(2)]
+    outs = chans - 8
+    lanes = [(r, slice(128 * b, 128 * (b + 1))) for r in range(2) for b in range(per_row)]
+    wet = [state[r][outs : outs + 1, at] for r, at in lanes]
+    rest = jnp.zeros((16 - 1 - len(wet), 128), F32)
+    ocean = [state[r][0:outs, at] for r, at in lanes]
+    sent_ref[...] = jnp.concatenate([*blocks, numbers, *wet, rest, *ocean], axis=0).astype(BF)
 
 
 def regrid_kernel(place_ref, blocks_ref, atmos_ref, *refs):
@@ -456,11 +457,18 @@
             total[at] = total[at] + pieces[slot]
         return carry
 
-    lax.fori_loop(0, peers, one_tile, 0, unroll=2)
+    lax.fori_loop(0, peers, one_tile, 0, unroll=8)
 
     def tile_row(ref, r):
-        at = [head + (r * per_row + b) * chans for b in range(per_row)]
-        return jnp.concatenate([ref[i : i + chans, :] for i in at], axis=1).astype(F32)
+        state = []
+        for b in range(per_row):
+            at = head + (r * per_row + b) * outs
+            shift = at % 16
+            rows16 = ref[at - shift : at - shift + chans, :].astype(F32)
+            state.append(rows16[shift : shift + outs])
+        marks = ref[head - 16 : head, :].astype(F32)[1 + r * per_row : 1 + (r + 1) * per_row]
+        wet = jnp.concatenate([marks[b : b + 1] for b in range(per_row)], axis=1)
+        return jnp.concatenate(state, axis=1), wet
 
     for k in range(chips):
         both = jnp.zeros((chans + fluxes, 128), F32)
@@ -471,11 +479,12 @@
                 arrived = jnp.concatenate(
                     [total[8 * t + r * per_row + b] for b in range(per_row)], axis=1
                 )
-                state = tile_row(sent[i], r)
-                row = jnp.concatenate([state[0:outs], arrived.astype(BF).astype(F32)], axis=0)
+                state, wet = tile_row(sent[i], r)
+                wet = jnp.concatenate([wet, jnp.zeros((fluxes - 1, wet.shape[1]), F32)], axis=0)
+                row = jnp.concatenate([state, arrived.astype(BF).astype(F32)], axis=0)
                 store_row(stack_ref, 2 * t + r + 1, row, chans)
-                wet_ref[2 * t + r] = state[outs:]
-                ends.append(jnp.concatenate([row, state[outs:]], axis=0))
+                wet_ref[2 * t + r] = wet
+                ends.append(jnp.concatenate([row, wet], axis=0))
             both = both + pltpu.roll(edges_of(ends), 64 * (comp if i < chips else 1 - comp), 1)
         edge_ref[lat ^ k] = both.astype(BF)
     leaving.wait()
@@ -506,6 +515,7 @@
     per_row = width // 128
     w_in = [turned(win_ref, layer) for layer in range(2)]
     total[...] = jnp.zeros(total.shape, F32)
+    copy.wait()
 
     strip = strip_of(own_ref, other_ref)
     wet = strip[chans : chans + 1]
@@ -572,7 +582,6 @@
         row = centre(stack_ref, 2 * t + r + 1, chans)[0:outs] + column_sum(y, outs)
         next_ref[:, r, :] = mend_row(wet_ref[2 * t + r, 0:1, :] * row, edge, r).astype(BF)
 
-    copy.wait()
     peers = rows // 2
     slots = 2 * peers
     for slot in range(slots):
@@ -660,6 +669,9 @@
     def both_ways(pairs):
         return pairs + [(j, i) for i, j in pairs]
 
+    cross.append((0, tiles - 1))
+    odd.append((0, lats - 1))
+
     near = [
         atmos_tile,
         swap(atmos_tile, "comp"),
@@ -699,7 +711,7 @@
         second_kernel,
         (
             jax.ShapeDtypeStruct((chans, height, width), BF),
-            jax.ShapeDtypeStruct((subs * (fluxes + chans) + 16, 128), BF),
+            jax.ShapeDtypeStruct((subs * (fluxes + outs) + 16, 128), BF),
         ),
         [place, atmos_stack, edges, edges_other, win_a, wout_a, flux_proj, ocean_tile],
         flops=4 * conv_flops(hidden_a, chans),

time: 47.8 us -> 46.1 us (0.964)
  starting transfers between devices: 15.1 us -> 12.3 us
  waiting for transfers between devices: 9.14 us -> 10.7 us
    ppermute x4, starting transfers between devices: 9.85 us -> 3.52 us  [far(): return lax.ppermute(v, 'lat', [(i, i ^ k) for i in range(lats)])]
    ppermute x1, starting transfers between devices: 0.65 us -> 4.71 us  [column_device(): lax.ppermute(atmos_tile, ('lat', 'comp'), both_ways(cross))]
    ppermute x1, waiting for transfers between devices: 0.01 us -> 1.72 us  [column_device(): lax.ppermute(atmos_tile, 'lat', both_ways(odd))]
    ppermute x4, waiting for transfers between devices: 8.1 us -> 6.8 us  [far(): return lax.ppermute(v, 'lat', [(i, i ^ k) for i in range(lats)])]
    ppermute x1, waiting for transfers between devices: 0.01 us -> 0.96 us  [column_device(): lax.ppermute(atmos_tile, ('lat', 'comp'), both_ways(cross))]
    ppermute x7, starting transfers between devices: 3.96 us -> 3.21 us  [swap(): return lax.ppermute(v, axis, [(0, 1), (1, 0)])]
  transfers between devices with their start and end apart: 13 -> 13, of which waited for: 6 -> 8; matrix products, arithmetic and copies ran while one was open for 0% -> 0% of each run, Pallas kernels for 15% -> 16%
where the time goes in v4:
time: 46.1 us; the launch traced here: 46 us
  Pallas kernels  20.9 us (45%)
  starting transfers between devices  12.3 us (27%)
  waiting for transfers between devices  10.7 us (23%)
  local copies, waits for them, and re-layouts  0.97 us (2%)
  between operations  0.95 us (2%)
    pallas_call x8, Pallas kernels, call(): pl.pallas_call(kernel, out_shape=out_shape, in_specs=[pl.BlockSpec(memory...  20.9 us
    ppermute x4, waiting for transfers between devices, far(): return lax.ppermute(v, 'lat', [(i, i ^ k) for i in range(lats)])  6.8 us
    ppermute x1, starting transfers between devices, column_device(): lax.ppermute(atmos_tile, ('lat', 'comp'), both_ways(cross))  4.71 us
    ppermute x4, starting transfers between devices, far(): return lax.ppermute(v, 'lat', [(i, i ^ k) for i in range(lats)])  3.52 us
    ppermute x7, starting transfers between devices, swap(): return lax.ppermute(v, axis, [(0, 1), (1, 0)])  3.21 us
    ppermute x1, waiting for transfers between devices, column_device(): lax.ppermute(atmos_tile, 'lat', both_ways(odd))  1.72 us
    ppermute x7, waiting for transfers between devices, swap(): return lax.ppermute(v, axis, [(0, 1), (1, 0)])  1.28 us
    unnamed x24, local copies, waits for them, and re-layouts  0.97 us
  transfers between devices with their start and end apart: 13, of which 8 were waited for; matrix products, arithmetic and copies ran while one was open for 0% of the time, Pallas kernels for 16%

profile of v4, /device:TPU:0, one launch (start us, length us, event | category | flops | bytes accessed | tf_op | source)
XLA Modules:
  0.0 46.0 jit_solution(3032527520054103538)
XLA Ops:
  0.7 0.9 %copy-done.10 = bf16[48,2,384]{2,1,0:T(2,128)(2,1)S(1)} copy-done((bf16[48,2,384]{2,1,0:T(2,128)(2,1)S(1)}, bf16[48,2,384]{2,1,0:T(2,128)(2,1)}, u32[]{:S(2)}) %copy-start.10) | copy-done | bytes 73752
  1.6 0.2 shard_map.139.own_ref
  1.8 0.5 %collective-permute-start = (bf16[2,48,384]{2,1,0:T(8,128)(2,1)S(1)}, bf16[2,48,384]{2,1,0:T(8,128)(2,1)S(1)}, u32[]{:S(2)}, u32[]{:S(2)}) collective-permute-start(bf16[2,48,384]{2,1,0:T(8,128)(2,1)S(1)} %shard_map.139.own_ref), channel_id=1, source_target_pairs={{0,1},{1,0},{2,3},{3,2},{4,5},{5,4},{6,7},{7,6},{8,9},{9,8},{10,11... | collective-permute-start | bytes 221192 | tf_op jit(solution)/shard_map/ppermute | solution.py:647
  2.3 4.7 %collective-permute-start.1 = (bf16[2,48,384]{2,1,0:T(8,128)(2,1)S(1)}, bf16[2,48,384]{2,1,0:T(8,128)(2,1)S(1)}, u32[]{:S(2)}, u32[]{:S(2)}) collective-permute-start(bf16[2,48,384]{2,1,0:T(8,128)(2,1)S(1)} %shard_map.139.own_ref), channel_id=1, source_target_pairs={{1,4},{5,8},{9,12},{0,13},{4,1},{8,5},{12,9},{13,0},{3,6},{7,10},{... | collective-permute-start | bytes 221192 | tf_op jit(solution)/shard_map/ppermute | solution.py:678
  7.0 0.0 collective-permute-start.2
  7.0 0.9 %collective-permute-start.3 = (bf16[2,48,384]{2,1,0:T(8,128)(2,1)S(1)}, bf16[2,48,384]{2,1,0:T(8,128)(2,1)S(1)}, u32[]{:S(2)}, u32[]{:S(2)}) collective-permute-start(bf16[2,48,384]{2,1,0:T(8,128)(2,1)S(1)} %shard_map.139.own_ref), channel_id=1, source_target_pairs={{4,8},{0,12},{8,4},{12,0},{5,9},{1,13},{9,5},{13,1},{6,10},{2,14},... | collective-permute-start | bytes 221192 | tf_op jit(solution)/shard_map/ppermute | solution.py:680
  7.9 0.2 shard_map.142.ocean_ref
  8.2 0.1 pad_add_fusion.place_ref
  8.2 0.0 collective-permute-done.side_ref
  8.3 1.0 %collective-permute-done.1.cross_ref = bf16[2,48,384]{2,1,0:T(8,128)(2,1)S(1)} collective-permute-done((bf16[2,48,384]{2,1,0:T(8,128)(2,1)S(1)}, bf16[2,48,384]{2,1,0:T(8,128)(2,1)S(1)}, u32[]{:S(2)}, u32[]{:S(2)}) %collective-permute-start.1) | collective-permute-done | bytes 73760 | tf_op jit(solution)/shard_map/ppermute | solution.py:678
  9.2 2.3 %collective-permute-done.2.even_ref = bf16[2,48,384]{2,1,0:T(8,128)(2,1)S(1)} collective-permute-done((bf16[2,48,384]{2,1,0:T(8,128)(2,1)S(1)}, bf16[2,48,384]{2,1,0:T(8,128)(2,1)S(1)}, u32[]{:S(2)}, u32[]{:S(2)}) %collective-permute-start.2) | collective-permute-done | bytes 73760 | tf_op jit(solution)/shard_map/ppermute | solution.py:644
  11.5 1.7 %collective-permute-done.3.odd_ref = bf16[2,48,384]{2,1,0:T(8,128)(2,1)S(1)} collective-permute-done((bf16[2,48,384]{2,1,0:T(8,128)(2,1)S(1)}, bf16[2,48,384]{2,1,0:T(8,128)(2,1)S(1)}, u32[]{:S(2)}, u32[]{:S(2)}) %collective-permute-start.3) | collective-permute-done | bytes 73760 | tf_op jit(solution)/shard_map/ppermute | solution.py:680
  13.2 1.0 %shard_map.140 = (bf16[1440,384]{1,0:T(8,128)(2,1)S(1)}, bf16[3,48,128]{2,1,0:T(8,128)(2,1)S(1)}) custom-call(s32[3]{0:T(128)S(1)} %pad_add_fusion.place_ref, bf16[2,48,384]{2,1,0:T(8,128)(2,1)S(1)} %shard_map.139.own_ref, bf16[2,48,384]{2,1,0:T(8,128)(2,1)S(1)} %collective-permute-done.side_ref, bf16[2,48,384]{2,1,0:T(8,128)(2,1)S(1)} %collective-permute-done.1.cross_ref, ...), custom_call_target="tpu_custom_call" | custom-call | flops 5435817984 | bytes 1048576 | tf_op jit(solution)/shard_map/pallas_call | solution.py:608
  14.3 1.6 %collective-permute-start.4 = (bf16[3,48,128]{2,1,0:T(8,128)(2,1)S(1)}, bf16[3,48,128]{2,1,0:T(8,128)(2,1)S(1)}, u32[]{:S(2)}, u32[]{:S(2)}) collective-permute-start(bf16[3,48,128]{2,1,0:T(8,128)(2,1)S(1)} %get-tuple-element.15.own_ref), channel_id=1, source_target_pairs={{0,2},{2,0},{1,3},{3,1},{4,6},{6,4},{5,7},{7,5},{8,10},{10,8},{9,1... | collective-permute-start | bytes 110600 | tf_op jit(solution)/shard_map/ppermute | solution.py:647
  15.8 3.3 %shard_map.141.stack_ref = bf16[1440,384]{1,0:T(8,128)(2,1)S(1)} custom-call(s32[3]{0:T(128)S(1)} %pad_add_fusion.place_ref, bf16[1440,384]{1,0:T(8,128)(2,1)S(1)} %get-tuple-element.14.stack_ref, bf16[2,432,256]{2,1,0:T(8,128)(2,1)S(1)} %bitcast.20, bf16[2,432,256]{2,1,0:T(8,128)(2,1)S(1)} %bitcast.22), custom_call_target="tpu_custom_call" | custom-call | flops 21743271936 | bytes 1048576 | tf_op jit(solution)/shard_map/pallas_call | solution.py:608
  19.2 0.0 copy-start
  19.2 0.0 collective-permute-done.4.other_ref
  19.2 3.3 %shard_map.143 = (bf16[48,2,384]{2,1,0:T(2,128)(2,1)S(1)}, bf16[304,128]{1,0:T(8,128)(2,1)S(1)}) custom-call(s32[3]{0:T(128)S(1)} %pad_add_fusion.place_ref, bf16[1440,384]{1,0:T(8,128)(2,1)S(1)} %shard_map.141.stack_ref, bf16[3,48,128]{2,1,0:T(8,128)(2,1)S(1)} %get-tuple-element.15.own_ref, bf16[3,48,128]{2,1,0:T(8,128)(2,1)S(1)} %collective-permute-done.4.other_ref, ...), custom_call_target="tpu_custom_call" | custom-call | flops 21743271936 | bytes 1048576 | tf_op jit(solution)/shard_map/pallas_call | solution.py:608
  22.4 0.6 %collective-permute-start.6 = (bf16[304,128]{1,0:T(8,128)(2,1)S(1)}, bf16[304,128]{1,0:T(8,128)(2,1)S(1)}, u32[]{:S(2)}, u32[]{:S(2)}) collective-permute-start(bf16[304,128]{1,0:T(8,128)(2,1)S(1)} %get-tuple-element.17.refs_0_), channel_id=1, source_target_pairs={{0,8},{4,12},{8,0},{12,4},{1,9},{5,13},{9,1},{13,5},{2,10},{6,14},... | collective-permute-start | bytes 233480 | tf_op jit(solution)/shard_map/ppermute | solution.py:644
  23.1 2.9 %collective-permute-start.7 = (bf16[304,128]{1,0:T(8,128)(2,1)S(1)}, bf16[304,128]{1,0:T(8,128)(2,1)S(1)}, u32[]{:S(2)}, u32[]{:S(2)}) collective-permute-start(bf16[304,128]{1,0:T(8,128)(2,1)S(1)} %get-tuple-element.17.refs_0_), channel_id=1, source_target_pairs={{0,12},{4,8},{8,4},{12,0},{1,13},{5,9},{9,5},{13,1},{2,14},{6,10},... | collective-permute-start | bytes 233480 | tf_op jit(solution)/shard_map/ppermute | solution.py:644
  26.0 0.0 collective-permute-start.5
  26.0 0.0 collective-permute-start.8
  26.0 4.4 %collective-permute-done.6.refs_2_ = bf16[304,128]{1,0:T(8,128)(2,1)S(1)} collective-permute-done((bf16[304,128]{1,0:T(8,128)(2,1)S(1)}, bf16[304,128]{1,0:T(8,128)(2,1)S(1)}, u32[]{:S(2)}, u32[]{:S(2)}) %collective-permute-start.6) | collective-permute-done | bytes 77856 | tf_op jit(solution)/shard_map/ppermute | solution.py:644
  30.3 0.5 %collective-permute-start.11 = (bf16[304,128]{1,0:T(8,128)(2,1)S(1)}, bf16[304,128]{1,0:T(8,128)(2,1)S(1)}, u32[]{:S(2)}, u32[]{:S(2)}) collective-permute-start(bf16[304,128]{1,0:T(8,128)(2,1)S(1)} %collective-permute-done.7.refs_3_), channel_id=1, source_target_pairs={{0,1},{1,0},{2,3},{3,2},{4,5},{5,4},{6,7},{7,6},{8,9},{9,8},{10,11... | collective-permute-start | bytes 233480 | tf_op jit(solution)/shard_map/ppermute | solution.py:647
  30.8 0.1 collective-permute-done.5.refs_1_
  31.0 0.6 %collective-permute-done.10.refs_6_ = bf16[304,128]{1,0:T(8,128)(2,1)S(1)} collective-permute-done((bf16[304,128]{1,0:T(8,128)(2,1)S(1)}, bf16[304,128]{1,0:T(8,128)(2,1)S(1)}, u32[]{:S(2)}, u32[]{:S(2)}) %collective-permute-start.10) | collective-permute-done | bytes 77856 | tf_op jit(solution)/shard_map/ppermute | solution.py:647
  31.6 0.2 collective-permute-done.11.refs_7_
  31.8 0.5 %collective-permute-done.9.refs_5_ = bf16[304,128]{1,0:T(8,128)(2,1)S(1)} collective-permute-done((bf16[304,128]{1,0:T(8,128)(2,1)S(1)}, bf16[304,128]{1,0:T(8,128)(2,1)S(1)}, u32[]{:S(2)}, u32[]{:S(2)}) %collective-permute-start.9) | collective-permute-done | bytes 77856 | tf_op jit(solution)/shard_map/ppermute | solution.py:647
  32.3 3.6 %shard_map.144 = (bf16[2592,384]{1,0:T(8,128)(2,1)S(1)}, f32[16,8,384]{2,1,0:T(8,128)S(1)}, bf16[4,56,128]{2,1,0:T(8,128)(2,1)S(1)}, s32[8,128]{1,0:T(8,128)S(1)}, bf16[48,2,384]{2,1,0:T(2,128)(2,1)}) custom-call(s32[3]{0:T(128)S(1)} %pad_add_fusion.place_ref, bf16[64,128,128]{2,1,0:T(8,128)(2,1)S(1)} %copy-done, ...), custom_call_target="tpu_custom_call" | custom-call | flops 2491416576 | bytes 1048576 | tf_op jit(solution)/shard_map/pallas_call | solution.py:608
  35.9 0.6 %collective-permute-start.12 = (bf16[4,56,128]{2,1,0:T(8,128)(2,1)S(1)}, bf16[4,56,128]{2,1,0:T(8,128)(2,1)S(1)}, u32[]{:S(2)}, u32[]{:S(2)}) collective-permute-start(bf16[4,56,128]{2,1,0:T(8,128)(2,1)S(1)} %get-tuple-element.22.own_ref), channel_id=1, source_target_pairs={{0,2},{2,0},{1,3},{3,1},{4,6},{6,4},{5,7},{7,5},{8,10},{10,8},{9,1... | collective-permute-start | bytes 172040 | tf_op jit(solution)/shard_map/ppermute | solution.py:647
  36.5 3.6 %shard_map.145.stack_ref = bf16[2592,384]{1,0:T(8,128)(2,1)S(1)} custom-call(bf16[2592,384]{1,0:T(8,128)(2,1)S(1)} %get-tuple-element.20.stack_ref, f32[16,8,384]{2,1,0:T(8,128)S(1)} %get-tuple-element.21.wet_ref, bf16[2,432,128]{2,1,0:T(8,128)(2,1)S(1)} %bitcast.13, bf16[2,360,128]{2,1,0:T(8,128)(2,1)S(1)} %bitcast.15), custom_call_target="tpu_custom_call" | custom-call | flops 9965666304 | bytes 1048576 | tf_op jit(solution)/shard_map/pallas_call | solution.py:608
  40.1 5.7 %shard_map.146 = (bf16[40,2,384]{2,1,0:T(2,128)(2,1)}, f32[2,384]{1,0:T(2,128)}) custom-call(s32[3]{0:T(128)S(1)} %pad_add_fusion.place_ref, s32[8,128]{1,0:T(8,128)S(1)} %get-tuple-element.19.table_ref, bf16[2592,384]{1,0:T(8,128)(2,1)S(1)} %shard_map.145.stack_ref, f32[16,8,384]{2,1,0:T(8,128)S(1)} %get-tuple-element.21.wet_ref, ...), custom_call_target="tpu_custom_call" | custom-call | bytes 1048576 | tf_op jit(solution)/shard_map/pallas_call | solution.py:608
  (27 shorter events, 0.1 us)
Async XLA Ops:
  0.6 7.3 %copy-start.5 = (s32[1,1,8,2]{2,3,1,0:T(2,128)S(1)}, s32[1,1,8,2]{2,3,1,0:T(2,128)}, u32[]{:S(2)}) copy-start(s32[1,1,8,2]{2,3,1,0:T(2,128)} %param.21) | copy-start | bytes 196
  0.6 7.3 %copy-start.6 = (s32[1,1,8,2]{2,3,1,0:T(2,128)S(1)}, s32[1,1,8,2]{2,3,1,0:T(2,128)}, u32[]{:S(2)}) copy-start(s32[1,1,8,2]{2,3,1,0:T(2,128)} %param.22) | copy-start | bytes 196
  0.7 7.3 %copy-start.7 = (s32[1,1,8,2]{2,3,1,0:T(2,128)S(1)}, s32[1,1,8,2]{2,3,1,0:T(2,128)}, u32[]{:S(2)}) copy-start(s32[1,1,8,2]{2,3,1,0:T(2,128)} %param.23) | copy-start | bytes 196
  0.7 7.3 %copy-start.3 = (bf16[40,2,384]{2,1,0:T(2,128)(2,1)S(1)}, bf16[40,2,384]{2,1,0:T(2,128)(2,1)}, u32[]{:S(2)}) copy-start(bf16[40,2,384]{2,1,0:T(2,128)(2,1)} %ocean_hbm.1) | copy-start | bytes 184324
  0.7 7.3 %copy-start.4 = (s32[2,384]{1,0:T(2,128)S(1)}, s32[2,384]{1,0:T(2,128)}, u32[]{:S(2)}) copy-start(s32[2,384]{1,0:T(2,128)} %mask_hbm.1) | copy-start | bytes 9220
  0.7 0.9 %copy-start.10 = (bf16[48,2,384]{2,1,0:T(2,128)(2,1)S(1)}, bf16[48,2,384]{2,1,0:T(2,128)(2,1)}, u32[]{:S(2)}) copy-start(bf16[48,2,384]{2,1,0:T(2,128)(2,1)} %atmos_ref.1) | copy-start | bytes 221188
  1.8 6.5 %collective-permute-start = (bf16[2,48,384]{2,1,0:T(8,128)(2,1)S(1)}, bf16[2,48,384]{2,1,0:T(8,128)(2,1)S(1)}, u32[]{:S(2)}, u32[]{:S(2)}) collective-permute-start(bf16[2,48,384]{2,1,0:T(8,128)(2,1)S(1)} %shard_map.139.own_ref), channel_id=1, source_target_pairs={{0,1},{1,0},{2,3},{3,2},{4,5},{5,4},{6,7},{7,6},{8,9},{9,8},{10,11... | collective-permute-start | bytes 221192 | tf_op jit(solution)/shard_map/ppermute | solution.py:647
  2.3 6.9 %collective-permute-start.1 = (bf16[2,48,384]{2,1,0:T(8,128)(2,1)S(1)}, bf16[2,48,384]{2,1,0:T(8,128)(2,1)S(1)}, u32[]{:S(2)}, u32[]{:S(2)}) collective-permute-start(bf16[2,48,384]{2,1,0:T(8,128)(2,1)S(1)} %shard_map.139.own_ref), channel_id=1, source_target_pairs={{1,4},{5,8},{9,12},{0,13},{4,1},{8,5},{12,9},{13,0},{3,6},{7,10},{... | collective-permute-start | bytes 221192 | tf_op jit(solution)/shard_map/ppermute | solution.py:678
  7.0 4.5 %collective-permute-start.2 = (bf16[2,48,384]{2,1,0:T(8,128)(2,1)S(1)}, bf16[2,48,384]{2,1,0:T(8,128)(2,1)S(1)}, u32[]{:S(2)}, u32[]{:S(2)}) collective-permute-start(bf16[2,48,384]{2,1,0:T(8,128)(2,1)S(1)} %shard_map.139.own_ref), channel_id=1, source_target_pairs={{0,4},{4,0},{8,12},{12,8},{1,5},{5,1},{9,13},{13,9},{2,6},{6,2},{1... | collective-permute-start | bytes 221192 | tf_op jit(solution)/shard_map/ppermute | solution.py:644
  7.0 6.2 %collective-permute-start.3 = (bf16[2,48,384]{2,1,0:T(8,128)(2,1)S(1)}, bf16[2,48,384]{2,1,0:T(8,128)(2,1)S(1)}, u32[]{:S(2)}, u32[]{:S(2)}) collective-permute-start(bf16[2,48,384]{2,1,0:T(8,128)(2,1)S(1)} %shard_map.139.own_ref), channel_id=1, source_target_pairs={{4,8},{0,12},{8,4},{12,0},{5,9},{1,13},{9,5},{13,1},{6,10},{2,14},... | collective-permute-start | bytes 221192 | tf_op jit(solution)/shard_map/ppermute | solution.py:680
  8.2 7.6 %copy-start.8 = (bf16[2,9,256,48]{2,3,1,0:T(8,128)(2,1)S(1)}, bf16[2,9,256,48]{2,3,1,0:T(8,128)(2,1)}, u32[]{:S(2)}) copy-start(bf16[2,9,256,48]{2,3,1,0:T(8,128)(2,1)} %param.15) | copy-start | bytes 1327108
  8.2 7.6 %copy-start.9 = (bf16[2,9,48,256]{3,2,1,0:T(8,128)(2,1)S(1)}, bf16[2,9,48,256]{3,2,1,0:T(8,128)(2,1)}, u32[]{:S(2)}) copy-start(bf16[2,9,48,256]{3,2,1,0:T(8,128)(2,1)} %param.16) | copy-start | bytes 1327108
  14.3 4.9 %collective-permute-start.4 = (bf16[3,48,128]{2,1,0:T(8,128)(2,1)S(1)}, bf16[3,48,128]{2,1,0:T(8,128)(2,1)S(1)}, u32[]{:S(2)}, u32[]{:S(2)}) collective-permute-start(bf16[3,48,128]{2,1,0:T(8,128)(2,1)S(1)} %get-tuple-element.15.own_ref), channel_id=1, source_target_pairs={{0,2},{2,0},{1,3},{3,1},{4,6},{6,4},{5,7},{7,5},{8,10},{10,8},{9,1... | collective-permute-start | bytes 110600 | tf_op jit(solution)/shard_map/ppermute | solution.py:647
  15.8 3.4 %copy-start.11 = (bf16[8,48]{1,0:T(8,128)(2,1)S(1)}, bf16[8,48]{1,0:T(8,128)(2,1)}, u32[]{:S(2)}) copy-start(bf16[8,48]{1,0:T(8,128)(2,1)} %proj_ref.1) | copy-start | bytes 2308
  19.2 13.1 %copy-start = (bf16[64,128,128]{2,1,0:T(8,128)(2,1)S(1)}, bf16[64,128,128]{2,1,0:T(8,128)(2,1)}, u32[]{:S(2)}) copy-start(bf16[64,128,128]{2,1,0:T(8,128)(2,1)} %blocks_ref.3) | copy-start | bytes 6291460
  22.4 7.9 %collective-permute-start.6 = (bf16[304,128]{1,0:T(8,128)(2,1)S(1)}, bf16[304,128]{1,0:T(8,128)(2,1)S(1)}, u32[]{:S(2)}, u32[]{:S(2)}) collective-permute-start(bf16[304,128]{1,0:T(8,128)(2,1)S(1)} %get-tuple-element.17.refs_0_), channel_id=1, source_target_pairs={{0,8},{4,12},{8,0},{12,4},{1,9},{5,13},{9,1},{13,5},{2,10},{6,14},... | collective-permute-start | bytes 233480 | tf_op jit(solution)/shard_map/ppermute | solution.py:644
  23.1 7.3 %collective-permute-start.7 = (bf16[304,128]{1,0:T(8,128)(2,1)S(1)}, bf16[304,128]{1,0:T(8,128)(2,1)S(1)}, u32[]{:S(2)}, u32[]{:S(2)}) collective-permute-start(bf16[304,128]{1,0:T(8,128)(2,1)S(1)} %get-tuple-element.17.refs_0_), channel_id=1, source_target_pairs={{0,12},{4,8},{8,4},{12,0},{1,13},{5,9},{9,5},{13,1},{2,14},{6,10},... | collective-permute-start | bytes 233480 | tf_op jit(solution)/shard_map/ppermute | solution.py:644
  26.0 5.0 %collective-permute-start.5 = (bf16[304,128]{1,0:T(8,128)(2,1)S(1)}, bf16[304,128]{1,0:T(8,128)(2,1)S(1)}, u32[]{:S(2)}, u32[]{:S(2)}) collective-permute-start(bf16[304,128]{1,0:T(8,128)(2,1)S(1)} %get-tuple-element.17.refs_0_), channel_id=1, source_target_pairs={{0,4},{4,0},{8,12},{12,8},{1,5},{5,1},{9,13},{13,9},{2,6},{6,2},{1... | collective-permute-start | bytes 233480 | tf_op jit(solution)/shard_map/ppermute | solution.py:644
  26.0 5.0 %collective-permute-start.8 = (bf16[304,128]{1,0:T(8,128)(2,1)S(1)}, bf16[304,128]{1,0:T(8,128)(2,1)S(1)}, u32[]{:S(2)}, u32[]{:S(2)}) collective-permute-start(bf16[304,128]{1,0:T(8,128)(2,1)S(1)} %get-tuple-element.17.refs_0_), channel_id=1, source_target_pairs={{0,1},{1,0},{2,3},{3,2},{4,5},{5,4},{6,7},{7,6},{8,9},{9,8},{10,11... | collective-permute-start | bytes 233480 | tf_op jit(solution)/shard_map/ppermute | solution.py:647
  30.3 1.3 %collective-permute-start.10 = (bf16[304,128]{1,0:T(8,128)(2,1)S(1)}, bf16[304,128]{1,0:T(8,128)(2,1)S(1)}, u32[]{:S(2)}, u32[]{:S(2)}) collective-permute-start(bf16[304,128]{1,0:T(8,128)(2,1)S(1)} %collective-permute-done.6.refs_2_), channel_id=1, source_target_pairs={{0,1},{1,0},{2,3},{3,2},{4,5},{5,4},{6,7},{7,6},{8,9},{9,8},{10,11... | collective-permute-start | bytes 233480 | tf_op jit(solution)/shard_map/ppermute | solution.py:647
  30.3 1.4 %collective-permute-start.11 = (bf16[304,128]{1,0:T(8,128)(2,1)S(1)}, bf16[304,128]{1,0:T(8,128)(2,1)S(1)}, u32[]{:S(2)}, u32[]{:S(2)}) collective-permute-start(bf16[304,128]{1,0:T(8,128)(2,1)S(1)} %collective-permute-done.7.refs_3_), channel_id=1, source_target_pairs={{0,1},{1,0},{2,3},{3,2},{4,5},{5,4},{6,7},{7,6},{8,9},{9,8},{10,11... | collective-permute-start | bytes 233480 | tf_op jit(solution)/shard_map/ppermute | solution.py:647
  31.0 1.3 %collective-permute-start.9 = (bf16[304,128]{1,0:T(8,128)(2,1)S(1)}, bf16[304,128]{1,0:T(8,128)(2,1)S(1)}, u32[]{:S(2)}, u32[]{:S(2)}) collective-permute-start(bf16[304,128]{1,0:T(8,128)(2,1)S(1)} %collective-permute-done.5.refs_1_), channel_id=1, source_target_pairs={{0,1},{1,0},{2,3},{3,2},{4,5},{5,4},{6,7},{7,6},{8,9},{9,8},{10,11... | collective-permute-start | bytes 233480 | tf_op jit(solution)/shard_map/ppermute | solution.py:647
  32.3 4.2 %copy-start.1 = (bf16[2,9,128,48]{2,3,1,0:T(8,128)(2,1)S(1)}, bf16[2,9,128,48]{2,3,1,0:T(8,128)(2,1)}, u32[]{:S(2)}) copy-start(bf16[2,9,128,48]{2,3,1,0:T(8,128)(2,1)} %param.17) | copy-start | bytes 663556
  32.3 4.2 %copy-start.2 = (bf16[2,9,40,128]{3,2,1,0:T(8,128)(2,1)S(1)}, bf16[2,9,40,128]{3,2,1,0:T(8,128)(2,1)}, u32[]{:S(2)}) copy-start(bf16[2,9,40,128]{3,2,1,0:T(8,128)(2,1)} %param.18) | copy-start | bytes 552964
  35.9 4.3 %collective-permute-start.12 = (bf16[4,56,128]{2,1,0:T(8,128)(2,1)S(1)}, bf16[4,56,128]{2,1,0:T(8,128)(2,1)S(1)}, u32[]{:S(2)}, u32[]{:S(2)}) collective-permute-start(bf16[4,56,128]{2,1,0:T(8,128)(2,1)S(1)} %get-tuple-element.22.own_ref), channel_id=1, source_target_pairs={{0,2},{2,0},{1,3},{3,1},{4,6},{6,4},{5,7},{7,5},{8,10},{10,8},{9,1... | collective-permute-start | bytes 172040 | tf_op jit(solution)/shard_map/ppermute | solution.py:647

commit v5 on v4

--- a/solution.py
+++ b/solution.py
@@ -292,11 +292,6 @@
     return jnp.concatenate([head, row[:, 128 : width - 128], tail], axis=1)
 
 
-def pack_atmos_kernel(atmos_ref, tile_ref):
-    for r in range(tile_ref.shape[0]):
-        tile_ref[r] = atmos_ref[:, r, :]
-
-
 def pack_ocean_kernel(source_hbm, target_hbm, weight_hbm, ocean_hbm, mask_hbm, tile_ref, source_ref,
                       target_ref, weight_ref, ocean_ref, mask_ref, sems):
     given = (source_hbm, target_hbm, weight_hbm, ocean_hbm, mask_hbm)
@@ -321,7 +316,7 @@
 
 def stack_kernel(place_ref, own_ref, side_ref, cross_ref, even_ref, odd_ref, stack_ref, edge_ref):
     lat, comp = place_ref[0], place_ref[1]
-    chans, width = own_ref.shape[1:]
+    chans, _, width = own_ref.shape
     valid = window_rule(place_ref)[1]
     low = lat % 2 == 0
     places = (
@@ -334,7 +329,7 @@
     for tile, at in places:
         for r in range(2):
             row = 2 * at + r
-            store_row(stack_ref, row, tile[r].astype(F32) * valid(row), chans)
+            store_row(stack_ref, row, tile[:, r, :].astype(F32) * valid(row), chans)
     for q in range(edge_ref.shape[0]):
         both = jnp.zeros((chans, 128), F32)
         for half in range(2):
@@ -650,9 +645,6 @@
         return 2 * layers * rows * width * 9 * hidden * (chans + outs)
 
     tile = jax.ShapeDtypeStruct((height, chans, width), BF)
-    atmos_tile = call(
-        pack_atmos_kernel, tile, [atmos_state], smem=0, flops=conv_flops(hidden_a, chans)
-    )
     slots = (regrid_source_block, regrid_target_block, regrid_weight_block)
     given = [*(jnp.transpose(v, (0, 1, 3, 2)) for v in slots), ocean_state, ocean_mask]
     ocean_tile = call(
@@ -662,6 +654,7 @@
         [*(pltpu.VMEM(v.shape, v.dtype) for v in given), pltpu.SemaphoreType.DMA((len(given),))],
         smem=0,
         anywhere=len(given),
+        flops=conv_flops(hidden_a, chans),
     )
     cross = [(i, i + 1) for i in range(1, tiles - 1, 2)]
     odd = [(i, i + 1) for i in range(1, lats - 1, 2)]
@@ -673,11 +666,11 @@
     odd.append((0, lats - 1))
 
     near = [
-        atmos_tile,
-        swap(atmos_tile, "comp"),
-        lax.ppermute(atmos_tile, ("lat", "comp"), both_ways(cross)),
-        far(atmos_tile, 1),
-        lax.ppermute(atmos_tile, "lat", both_ways(odd)),
+        atmos_state,
+        swap(atmos_state, "comp"),
+        lax.ppermute(atmos_state, ("lat", "comp"), both_ways(cross)),
+        far(atmos_state, 1),
+        lax.ppermute(atmos_state, "lat", both_ways(odd)),
     ]
     def taps_in(w):
         return jnp.transpose(w, (0, 1, 3, 2)).reshape(w.shape[0], 9 * w.shape[3], w.shape[2])

time: 46.1 us -> 45.6 us (0.989)
  waiting for transfers between devices: 10.7 us -> 7.64 us
  local copies, waits for them, and re-layouts: 0.97 us -> 3.58 us
    unnamed x24, local copies, waits for them, and re-layouts: 0.97 us -> 3.58 us
    ppermute x4, waiting for transfers between devices: 6.8 us -> 4.72 us  [far(): return lax.ppermute(v, 'lat', [(i, i ^ k) for i in range(lats)])]
    ppermute x2, waiting for transfers between devices: 2.68 us -> 1.64 us  [the longest x1 1.64 us: column_device(): lax.ppermute(atmos_state, 'lat', both_ways(odd))]
    pallas_call x8 -> x7, Pallas kernels: 20.9 us -> 20.8 us  [call(): pl.pallas_call(kernel, out_shape=out_shape, in_specs=[pl.BlockSpec(memory...]
  transfers between devices with their start and end apart: 13 -> 13, of which waited for: 8 -> 6; matrix products, arithmetic and copies ran while one was open for 0% -> 0% of each run, Pallas kernels for 16% -> 16%
where the time goes in v5:
time: 45.6 us; the launch traced here: 45.3 us
  Pallas kernels  20.8 us (46%)
  starting transfers between devices  12.4 us (27%)
  waiting for transfers between devices  7.64 us (17%)
  local copies, waits for them, and re-layouts  3.58 us (8%)
  between operations  0.91 us (2%)
    pallas_call x7, Pallas kernels, call(): pl.pallas_call(kernel, out_shape=out_shape, in_specs=[pl.BlockSpec(memory...  20.8 us
    ppermute x4, waiting for transfers between devices, far(): return lax.ppermute(v, 'lat', [(i, i ^ k) for i in range(lats)])  4.72 us
    ppermute x1, starting transfers between devices, column_device(): lax.ppermute(atmos_state, ('lat', 'comp'), both_ways(cross))  4.71 us
    unnamed x24, local copies, waits for them, and re-layouts  3.58 us
    ppermute x4, starting transfers between devices, far(): return lax.ppermute(v, 'lat', [(i, i ^ k) for i in range(lats)])  3.52 us
    ppermute x7, starting transfers between devices, swap(): return lax.ppermute(v, axis, [(0, 1), (1, 0)])  3.24 us
    ppermute x1, waiting for transfers between devices, column_device(): lax.ppermute(atmos_state, 'lat', both_ways(odd))  1.64 us
    ppermute x7, waiting for transfers between devices, swap(): return lax.ppermute(v, axis, [(0, 1), (1, 0)])  1.28 us
  transfers between devices with their start and end apart: 13, of which 6 were waited for; matrix products, arithmetic and copies ran while one was open for 0% of the time, Pallas kernels for 16%

profile of v5, /device:TPU:0, one launch (start us, length us, event | category | flops | bytes accessed | tf_op | source)
XLA Modules:
  0.0 45.3 jit_solution(4383450918453213412)
XLA Ops:
  0.6 0.5 %collective-permute-start = (bf16[48,2,384]{2,1,0:T(2,128)(2,1)}, bf16[48,2,384]{2,1,0:T(2,128)(2,1)S(1)}, u32[]{:S(2)}, u32[]{:S(2)}) collective-permute-start(bf16[48,2,384]{2,1,0:T(2,128)(2,1)} %own_ref.1), channel_id=1, source_target_pairs={{0,1},{1,0},{2,3},{3,2},{4,5},{5,4},{6,7},{7,6},{8,9},{9,8},{10,11... | collective-permute-start | bytes 221192 | tf_op jit(solution)/shard_map/ppermute | solution.py:642
  1.1 4.7 %collective-permute-start.1 = (bf16[48,2,384]{2,1,0:T(2,128)(2,1)}, bf16[48,2,384]{2,1,0:T(2,128)(2,1)S(1)}, u32[]{:S(2)}, u32[]{:S(2)}) collective-permute-start(bf16[48,2,384]{2,1,0:T(2,128)(2,1)} %own_ref.1), channel_id=1, source_target_pairs={{1,4},{5,8},{9,12},{0,13},{4,1},{8,5},{12,9},{13,0},{3,6},{7,10},{... | collective-permute-start | bytes 221192 | tf_op jit(solution)/shard_map/ppermute | solution.py:671
  5.9 0.9 %collective-permute-start.3 = (bf16[48,2,384]{2,1,0:T(2,128)(2,1)}, bf16[48,2,384]{2,1,0:T(2,128)(2,1)S(1)}, u32[]{:S(2)}, u32[]{:S(2)}) collective-permute-start(bf16[48,2,384]{2,1,0:T(2,128)(2,1)} %own_ref.1), channel_id=1, source_target_pairs={{4,8},{0,12},{8,4},{12,0},{5,9},{1,13},{9,5},{13,1},{6,10},{2,14},... | collective-permute-start | bytes 221192 | tf_op jit(solution)/shard_map/ppermute | solution.py:673
  6.8 0.8 %copy-done.6 = bf16[40,2,384]{2,1,0:T(2,128)(2,1)S(1)} copy-done((bf16[40,2,384]{2,1,0:T(2,128)(2,1)S(1)}, bf16[40,2,384]{2,1,0:T(2,128)(2,1)}, u32[]{:S(2)}) %copy-start.6) | copy-done | bytes 61464
  7.6 0.7 %copy-done.7 = s32[2,384]{1,0:T(2,128)S(1)} copy-done((s32[2,384]{1,0:T(2,128)S(1)}, s32[2,384]{1,0:T(2,128)}, u32[]{:S(2)}) %copy-start.7) | copy-done | bytes 3096
  8.3 0.7 %copy-done.9 = s32[1,1,8,2]{2,3,1,0:T(2,128)S(1)} copy-done((s32[1,1,8,2]{2,3,1,0:T(2,128)S(1)}, s32[1,1,8,2]{2,3,1,0:T(2,128)}, u32[]{:S(2)}) %copy-start.9) | copy-done | bytes 88
  9.0 0.7 %copy-done.10 = s32[1,1,8,2]{2,3,1,0:T(2,128)S(1)} copy-done((s32[1,1,8,2]{2,3,1,0:T(2,128)S(1)}, s32[1,1,8,2]{2,3,1,0:T(2,128)}, u32[]{:S(2)}) %copy-start.10) | copy-done | bytes 88
  9.6 0.7 %copy-done.11 = s32[1,1,8,2]{2,3,1,0:T(2,128)S(1)} copy-done((s32[1,1,8,2]{2,3,1,0:T(2,128)S(1)}, s32[1,1,8,2]{2,3,1,0:T(2,128)}, u32[]{:S(2)}) %copy-start.11) | copy-done | bytes 88
  10.3 0.2 shard_map.141.ocean_ref
  10.5 0.1 pad_add_fusion.place_ref
  10.6 0.0 collective-permute-done.side_ref
  10.6 0.0 collective-permute-done.1.cross_ref
  10.6 0.0 collective-permute-done.2.even_ref
  10.6 1.6 %collective-permute-done.3.odd_ref = bf16[48,2,384]{2,1,0:T(2,128)(2,1)S(1)} collective-permute-done((bf16[48,2,384]{2,1,0:T(2,128)(2,1)}, bf16[48,2,384]{2,1,0:T(2,128)(2,1)S(1)}, u32[]{:S(2)}, u32[]{:S(2)}) %collective-permute-start.3) | collective-permute-done | bytes 73760 | tf_op jit(solution)/shard_map/ppermute | solution.py:673
  12.3 1.3 %shard_map.139 = (bf16[1440,384]{1,0:T(8,128)(2,1)S(1)}, bf16[3,48,128]{2,1,0:T(8,128)(2,1)S(1)}) custom-call(s32[3]{0:T(128)S(1)} %pad_add_fusion.place_ref, bf16[48,2,384]{2,1,0:T(2,128)(2,1)S(1)} %copy-done.5, bf16[48,2,384]{2,1,0:T(2,128)(2,1)S(1)} %collective-permute-done.side_ref, bf16[48,2,384]{2,1,0:T(2,128)(2,1)S(1)} %collective-permute-done.1.cross_ref, ...), custom_call_target="tpu_custom_call" | custom-call | flops 5435817984 | bytes 1048576 | tf_op jit(solution)/shard_map/pallas_call | solution.py:603
  13.6 1.6 %collective-permute-start.4 = (bf16[3,48,128]{2,1,0:T(8,128)(2,1)S(1)}, bf16[3,48,128]{2,1,0:T(8,128)(2,1)S(1)}, u32[]{:S(2)}, u32[]{:S(2)}) collective-permute-start(bf16[3,48,128]{2,1,0:T(8,128)(2,1)S(1)} %get-tuple-element.15.own_ref), channel_id=1, source_target_pairs={{0,2},{2,0},{1,3},{3,1},{4,6},{6,4},{5,7},{7,5},{8,10},{10,8},{9,1... | collective-permute-start | bytes 110600 | tf_op jit(solution)/shard_map/ppermute | solution.py:642
  15.2 3.3 %shard_map.140.stack_ref = bf16[1440,384]{1,0:T(8,128)(2,1)S(1)} custom-call(s32[3]{0:T(128)S(1)} %pad_add_fusion.place_ref, bf16[1440,384]{1,0:T(8,128)(2,1)S(1)} %get-tuple-element.14.stack_ref, bf16[2,432,256]{2,1,0:T(8,128)(2,1)S(1)} %bitcast.17, bf16[2,432,256]{2,1,0:T(8,128)(2,1)S(1)} %bitcast.19), custom_call_target="tpu_custom_call" | custom-call | flops 21743271936 | bytes 1048576 | tf_op jit(solution)/shard_map/pallas_call | solution.py:603
  18.5 0.0 copy-start
  18.5 3.3 %shard_map.142 = (bf16[48,2,384]{2,1,0:T(2,128)(2,1)S(1)}, bf16[304,128]{1,0:T(8,128)(2,1)S(1)}) custom-call(s32[3]{0:T(128)S(1)} %pad_add_fusion.place_ref, bf16[1440,384]{1,0:T(8,128)(2,1)S(1)} %shard_map.140.stack_ref, bf16[3,48,128]{2,1,0:T(8,128)(2,1)S(1)} %get-tuple-element.15.own_ref, bf16[3,48,128]{2,1,0:T(8,128)(2,1)S(1)} %collective-permute-done.4.other_ref, ...), custom_call_target="tpu_custom_call" | custom-call | flops 21743271936 | bytes 1048576 | tf_op jit(solution)/shard_map/pallas_call | solution.py:603
  21.8 1.5 %collective-permute-start.6 = (bf16[304,128]{1,0:T(8,128)(2,1)S(1)}, bf16[304,128]{1,0:T(8,128)(2,1)S(1)}, u32[]{:S(2)}, u32[]{:S(2)}) collective-permute-start(bf16[304,128]{1,0:T(8,128)(2,1)S(1)} %get-tuple-element.17.refs_0_), channel_id=1, source_target_pairs={{0,8},{4,12},{8,0},{12,4},{1,9},{5,13},{9,1},{13,5},{2,10},{6,14},... | collective-permute-start | bytes 233480 | tf_op jit(solution)/shard_map/ppermute | solution.py:639
  23.3 2.0 %collective-permute-start.7 = (bf16[304,128]{1,0:T(8,128)(2,1)S(1)}, bf16[304,128]{1,0:T(8,128)(2,1)S(1)}, u32[]{:S(2)}, u32[]{:S(2)}) collective-permute-start(bf16[304,128]{1,0:T(8,128)(2,1)S(1)} %get-tuple-element.17.refs_0_), channel_id=1, source_target_pairs={{0,12},{4,8},{8,4},{12,0},{1,13},{5,9},{9,5},{13,1},{2,14},{6,10},... | collective-permute-start | bytes 233480 | tf_op jit(solution)/shard_map/ppermute | solution.py:639
  25.3 0.0 collective-permute-start.8
  25.3 4.6 %collective-permute-done.6.refs_2_ = bf16[304,128]{1,0:T(8,128)(2,1)S(1)} collective-permute-done((bf16[304,128]{1,0:T(8,128)(2,1)S(1)}, bf16[304,128]{1,0:T(8,128)(2,1)S(1)}, u32[]{:S(2)}, u32[]{:S(2)}) %collective-permute-start.6) | collective-permute-done | bytes 77856 | tf_op jit(solution)/shard_map/ppermute | solution.py:639
  29.9 0.5 %collective-permute-start.11 = (bf16[304,128]{1,0:T(8,128)(2,1)S(1)}, bf16[304,128]{1,0:T(8,128)(2,1)S(1)}, u32[]{:S(2)}, u32[]{:S(2)}) collective-permute-start(bf16[304,128]{1,0:T(8,128)(2,1)S(1)} %collective-permute-done.7.refs_3_), channel_id=1, source_target_pairs={{0,1},{1,0},{2,3},{3,2},{4,5},{5,4},{6,7},{7,6},{8,9},{9,8},{10,11... | collective-permute-start | bytes 233480 | tf_op jit(solution)/shard_map/ppermute | solution.py:642
  30.4 0.1 collective-permute-done.5.refs_1_
  30.5 0.6 %collective-permute-done.10.refs_6_ = bf16[304,128]{1,0:T(8,128)(2,1)S(1)} collective-permute-done((bf16[304,128]{1,0:T(8,128)(2,1)S(1)}, bf16[304,128]{1,0:T(8,128)(2,1)S(1)}, u32[]{:S(2)}, u32[]{:S(2)}) %collective-permute-start.10) | collective-permute-done | bytes 77856 | tf_op jit(solution)/shard_map/ppermute | solution.py:642
  31.1 0.2 collective-permute-done.11.refs_7_
  31.3 0.5 %collective-permute-done.9.refs_5_ = bf16[304,128]{1,0:T(8,128)(2,1)S(1)} collective-permute-done((bf16[304,128]{1,0:T(8,128)(2,1)S(1)}, bf16[304,128]{1,0:T(8,128)(2,1)S(1)}, u32[]{:S(2)}, u32[]{:S(2)}) %collective-permute-start.9) | collective-permute-done | bytes 77856 | tf_op jit(solution)/shard_map/ppermute | solution.py:642
  31.8 3.6 %shard_map.143 = (bf16[2592,384]{1,0:T(8,128)(2,1)S(1)}, f32[16,8,384]{2,1,0:T(8,128)S(1)}, bf16[4,56,128]{2,1,0:T(8,128)(2,1)S(1)}, s32[8,128]{1,0:T(8,128)S(1)}, bf16[48,2,384]{2,1,0:T(2,128)(2,1)}) custom-call(s32[3]{0:T(128)S(1)} %pad_add_fusion.place_ref, bf16[64,128,128]{2,1,0:T(8,128)(2,1)S(1)} %copy-done, ...), custom_call_target="tpu_custom_call" | custom-call | flops 2491416576 | bytes 1048576 | tf_op jit(solution)/shard_map/pallas_call | solution.py:603
  35.4 0.6 %collective-permute-start.12 = (bf16[4,56,128]{2,1,0:T(8,128)(2,1)S(1)}, bf16[4,56,128]{2,1,0:T(8,128)(2,1)S(1)}, u32[]{:S(2)}, u32[]{:S(2)}) collective-permute-start(bf16[4,56,128]{2,1,0:T(8,128)(2,1)S(1)} %get-tuple-element.22.own_ref), channel_id=1, source_target_pairs={{0,2},{2,0},{1,3},{3,1},{4,6},{6,4},{5,7},{7,5},{8,10},{10,8},{9,1... | collective-permute-start | bytes 172040 | tf_op jit(solution)/shard_map/ppermute | solution.py:642
  36.0 3.6 %shard_map.144.stack_ref = bf16[2592,384]{1,0:T(8,128)(2,1)S(1)} custom-call(bf16[2592,384]{1,0:T(8,128)(2,1)S(1)} %get-tuple-element.20.stack_ref, f32[16,8,384]{2,1,0:T(8,128)S(1)} %get-tuple-element.21.wet_ref, bf16[2,432,128]{2,1,0:T(8,128)(2,1)S(1)} %bitcast.13, bf16[2,360,128]{2,1,0:T(8,128)(2,1)S(1)} %bitcast.15), custom_call_target="tpu_custom_call" | custom-call | flops 9965666304 | bytes 1048576 | tf_op jit(solution)/shard_map/pallas_call | solution.py:603
  39.7 5.5 %shard_map.145 = (bf16[40,2,384]{2,1,0:T(2,128)(2,1)}, f32[2,384]{1,0:T(2,128)}) custom-call(s32[3]{0:T(128)S(1)} %pad_add_fusion.place_ref, s32[8,128]{1,0:T(8,128)S(1)} %get-tuple-element.19.table_ref, bf16[2592,384]{1,0:T(8,128)(2,1)S(1)} %shard_map.144.stack_ref, f32[16,8,384]{2,1,0:T(8,128)S(1)} %get-tuple-element.21.wet_ref, ...), custom_call_target="tpu_custom_call" | custom-call | bytes 1048576 | tf_op jit(solution)/shard_map/pallas_call | solution.py:603
  (26 shorter events, 0.1 us)
Async XLA Ops:
  0.6 10.0 %collective-permute-start = (bf16[48,2,384]{2,1,0:T(2,128)(2,1)}, bf16[48,2,384]{2,1,0:T(2,128)(2,1)S(1)}, u32[]{:S(2)}, u32[]{:S(2)}) collective-permute-start(bf16[48,2,384]{2,1,0:T(2,128)(2,1)} %own_ref.1), channel_id=1, source_target_pairs={{0,1},{1,0},{2,3},{3,2},{4,5},{5,4},{6,7},{7,6},{8,9},{9,8},{10,11... | collective-permute-start | bytes 221192 | tf_op jit(solution)/shard_map/ppermute | solution.py:642
  1.1 9.5 %collective-permute-start.1 = (bf16[48,2,384]{2,1,0:T(2,128)(2,1)}, bf16[48,2,384]{2,1,0:T(2,128)(2,1)S(1)}, u32[]{:S(2)}, u32[]{:S(2)}) collective-permute-start(bf16[48,2,384]{2,1,0:T(2,128)(2,1)} %own_ref.1), channel_id=1, source_target_pairs={{1,4},{5,8},{9,12},{0,13},{4,1},{8,5},{12,9},{13,0},{3,6},{7,10},{... | collective-permute-start | bytes 221192 | tf_op jit(solution)/shard_map/ppermute | solution.py:671
  5.9 4.8 %collective-permute-start.2 = (bf16[48,2,384]{2,1,0:T(2,128)(2,1)}, bf16[48,2,384]{2,1,0:T(2,128)(2,1)S(1)}, u32[]{:S(2)}, u32[]{:S(2)}) collective-permute-start(bf16[48,2,384]{2,1,0:T(2,128)(2,1)} %own_ref.1), channel_id=1, source_target_pairs={{0,4},{4,0},{8,12},{12,8},{1,5},{5,1},{9,13},{13,9},{2,6},{6,2},{1... | collective-permute-start | bytes 221192 | tf_op jit(solution)/shard_map/ppermute | solution.py:639
  5.9 6.4 %collective-permute-start.3 = (bf16[48,2,384]{2,1,0:T(2,128)(2,1)}, bf16[48,2,384]{2,1,0:T(2,128)(2,1)S(1)}, u32[]{:S(2)}, u32[]{:S(2)}) collective-permute-start(bf16[48,2,384]{2,1,0:T(2,128)(2,1)} %own_ref.1), channel_id=1, source_target_pairs={{4,8},{0,12},{8,4},{12,0},{5,9},{1,13},{9,5},{13,1},{6,10},{2,14},... | collective-permute-start | bytes 221192 | tf_op jit(solution)/shard_map/ppermute | solution.py:673
  6.8 0.8 %copy-start.6 = (bf16[40,2,384]{2,1,0:T(2,128)(2,1)S(1)}, bf16[40,2,384]{2,1,0:T(2,128)(2,1)}, u32[]{:S(2)}) copy-start(bf16[40,2,384]{2,1,0:T(2,128)(2,1)} %ocean_hbm.1) | copy-start | bytes 184324
  7.6 0.7 %copy-start.7 = (s32[2,384]{1,0:T(2,128)S(1)}, s32[2,384]{1,0:T(2,128)}, u32[]{:S(2)}) copy-start(s32[2,384]{1,0:T(2,128)} %mask_hbm.1) | copy-start | bytes 9220
  8.3 0.7 %copy-start.9 = (s32[1,1,8,2]{2,3,1,0:T(2,128)S(1)}, s32[1,1,8,2]{2,3,1,0:T(2,128)}, u32[]{:S(2)}) copy-start(s32[1,1,8,2]{2,3,1,0:T(2,128)} %param.21) | copy-start | bytes 196
  9.0 0.7 %copy-start.10 = (s32[1,1,8,2]{2,3,1,0:T(2,128)S(1)}, s32[1,1,8,2]{2,3,1,0:T(2,128)}, u32[]{:S(2)}) copy-start(s32[1,1,8,2]{2,3,1,0:T(2,128)} %param.22) | copy-start | bytes 196
  9.6 0.7 %copy-start.11 = (s32[1,1,8,2]{2,3,1,0:T(2,128)S(1)}, s32[1,1,8,2]{2,3,1,0:T(2,128)}, u32[]{:S(2)}) copy-start(s32[1,1,8,2]{2,3,1,0:T(2,128)} %param.23) | copy-start | bytes 196
  10.3 2.0 %copy-start.5 = (bf16[48,2,384]{2,1,0:T(2,128)(2,1)S(1)}, bf16[48,2,384]{2,1,0:T(2,128)(2,1)}, u32[]{:S(2)}) copy-start(bf16[48,2,384]{2,1,0:T(2,128)(2,1)} %own_ref.1) | copy-start | bytes 221188
  10.6 4.6 %copy-start.3 = (bf16[2,9,256,48]{2,3,1,0:T(8,128)(2,1)S(1)}, bf16[2,9,256,48]{2,3,1,0:T(8,128)(2,1)}, u32[]{:S(2)}) copy-start(bf16[2,9,256,48]{2,3,1,0:T(8,128)(2,1)} %param.15) | copy-start | bytes 1327108
  10.6 4.6 %copy-start.4 = (bf16[2,9,48,256]{3,2,1,0:T(8,128)(2,1)S(1)}, bf16[2,9,48,256]{3,2,1,0:T(8,128)(2,1)}, u32[]{:S(2)}) copy-start(bf16[2,9,48,256]{3,2,1,0:T(8,128)(2,1)} %param.16) | copy-start | bytes 1327108
  13.6 4.9 %collective-permute-start.4 = (bf16[3,48,128]{2,1,0:T(8,128)(2,1)S(1)}, bf16[3,48,128]{2,1,0:T(8,128)(2,1)S(1)}, u32[]{:S(2)}, u32[]{:S(2)}) collective-permute-start(bf16[3,48,128]{2,1,0:T(8,128)(2,1)S(1)} %get-tuple-element.15.own_ref), channel_id=1, source_target_pairs={{0,2},{2,0},{1,3},{3,1},{4,6},{6,4},{5,7},{7,5},{8,10},{10,8},{9,1... | collective-permute-start | bytes 110600 | tf_op jit(solution)/shard_map/ppermute | solution.py:642
  15.2 3.3 %copy-start.8 = (bf16[8,48]{1,0:T(8,128)(2,1)S(1)}, bf16[8,48]{1,0:T(8,128)(2,1)}, u32[]{:S(2)}) copy-start(bf16[8,48]{1,0:T(8,128)(2,1)} %proj_ref.1) | copy-start | bytes 2308
  18.5 13.3 %copy-start = (bf16[64,128,128]{2,1,0:T(8,128)(2,1)S(1)}, bf16[64,128,128]{2,1,0:T(8,128)(2,1)}, u32[]{:S(2)}) copy-start(bf16[64,128,128]{2,1,0:T(8,128)(2,1)} %blocks_ref.3) | copy-start | bytes 6291460
  21.8 8.1 %collective-permute-start.6 = (bf16[304,128]{1,0:T(8,128)(2,1)S(1)}, bf16[304,128]{1,0:T(8,128)(2,1)S(1)}, u32[]{:S(2)}, u32[]{:S(2)}) collective-permute-start(bf16[304,128]{1,0:T(8,128)(2,1)S(1)} %get-tuple-element.17.refs_0_), channel_id=1, source_target_pairs={{0,8},{4,12},{8,0},{12,4},{1,9},{5,13},{9,1},{13,5},{2,10},{6,14},... | collective-permute-start | bytes 233480 | tf_op jit(solution)/shard_map/ppermute | solution.py:639
  23.3 6.6 %collective-permute-start.7 = (bf16[304,128]{1,0:T(8,128)(2,1)S(1)}, bf16[304,128]{1,0:T(8,128)(2,1)S(1)}, u32[]{:S(2)}, u32[]{:S(2)}) collective-permute-start(bf16[304,128]{1,0:T(8,128)(2,1)S(1)} %get-tuple-element.17.refs_0_), channel_id=1, source_target_pairs={{0,12},{4,8},{8,4},{12,0},{1,13},{5,9},{9,5},{13,1},{2,14},{6,10},... | collective-permute-start | bytes 233480 | tf_op jit(solution)/shard_map/ppermute | solution.py:639
  25.3 5.2 %collective-permute-start.5 = (bf16[304,128]{1,0:T(8,128)(2,1)S(1)}, bf16[304,128]{1,0:T(8,128)(2,1)S(1)}, u32[]{:S(2)}, u32[]{:S(2)}) collective-permute-start(bf16[304,128]{1,0:T(8,128)(2,1)S(1)} %get-tuple-element.17.refs_0_), channel_id=1, source_target_pairs={{0,4},{4,0},{8,12},{12,8},{1,5},{5,1},{9,13},{13,9},{2,6},{6,2},{1... | collective-permute-start | bytes 233480 | tf_op jit(solution)/shard_map/ppermute | solution.py:639
  25.3 5.2 %collective-permute-start.8 = (bf16[304,128]{1,0:T(8,128)(2,1)S(1)}, bf16[304,128]{1,0:T(8,128)(2,1)S(1)}, u32[]{:S(2)}, u32[]{:S(2)}) collective-permute-start(bf16[304,128]{1,0:T(8,128)(2,1)S(1)} %get-tuple-element.17.refs_0_), channel_id=1, source_target_pairs={{0,1},{1,0},{2,3},{3,2},{4,5},{5,4},{6,7},{7,6},{8,9},{9,8},{10,11... | collective-permute-start | bytes 233480 | tf_op jit(solution)/shard_map/ppermute | solution.py:642
  29.9 1.3 %collective-permute-start.10 = (bf16[304,128]{1,0:T(8,128)(2,1)S(1)}, bf16[304,128]{1,0:T(8,128)(2,1)S(1)}, u32[]{:S(2)}, u32[]{:S(2)}) collective-permute-start(bf16[304,128]{1,0:T(8,128)(2,1)S(1)} %collective-permute-done.6.refs_2_), channel_id=1, source_target_pairs={{0,1},{1,0},{2,3},{3,2},{4,5},{5,4},{6,7},{7,6},{8,9},{9,8},{10,11... | collective-permute-start | bytes 233480 | tf_op jit(solution)/shard_map/ppermute | solution.py:642
  29.9 1.4 %collective-permute-start.11 = (bf16[304,128]{1,0:T(8,128)(2,1)S(1)}, bf16[304,128]{1,0:T(8,128)(2,1)S(1)}, u32[]{:S(2)}, u32[]{:S(2)}) collective-permute-start(bf16[304,128]{1,0:T(8,128)(2,1)S(1)} %collective-permute-done.7.refs_3_), channel_id=1, source_target_pairs={{0,1},{1,0},{2,3},{3,2},{4,5},{5,4},{6,7},{7,6},{8,9},{9,8},{10,11... | collective-permute-start | bytes 233480 | tf_op jit(solution)/shard_map/ppermute | solution.py:642
  30.5 1.3 %collective-permute-start.9 = (bf16[304,128]{1,0:T(8,128)(2,1)S(1)}, bf16[304,128]{1,0:T(8,128)(2,1)S(1)}, u32[]{:S(2)}, u32[]{:S(2)}) collective-permute-start(bf16[304,128]{1,0:T(8,128)(2,1)S(1)} %collective-permute-done.5.refs_1_), channel_id=1, source_target_pairs={{0,1},{1,0},{2,3},{3,2},{4,5},{5,4},{6,7},{7,6},{8,9},{9,8},{10,11... | collective-permute-start | bytes 233480 | tf_op jit(solution)/shard_map/ppermute | solution.py:642
  31.8 4.2 %copy-start.1 = (bf16[2,9,128,48]{2,3,1,0:T(8,128)(2,1)S(1)}, bf16[2,9,128,48]{2,3,1,0:T(8,128)(2,1)}, u32[]{:S(2)}) copy-start(bf16[2,9,128,48]{2,3,1,0:T(8,128)(2,1)} %param.17) | copy-start | bytes 663556
  31.8 4.2 %copy-start.2 = (bf16[2,9,40,128]{3,2,1,0:T(8,128)(2,1)S(1)}, bf16[2,9,40,128]{3,2,1,0:T(8,128)(2,1)}, u32[]{:S(2)}) copy-start(bf16[2,9,40,128]{3,2,1,0:T(8,128)(2,1)} %param.18) | copy-start | bytes 552964
  35.4 4.3 %collective-permute-start.12 = (bf16[4,56,128]{2,1,0:T(8,128)(2,1)S(1)}, bf16[4,56,128]{2,1,0:T(8,128)(2,1)S(1)}, u32[]{:S(2)}, u32[]{:S(2)}) collective-permute-start(bf16[4,56,128]{2,1,0:T(8,128)(2,1)S(1)} %get-tuple-element.22.own_ref), channel_id=1, source_target_pairs={{0,2},{2,0},{1,3},{3,1},{4,6},{6,4},{5,7},{7,5},{8,10},{10,8},{9,1... | collective-permute-start | bytes 172040 | tf_op jit(solution)/shard_map/ppermute | solution.py:642

commit v6 on v5

--- a/solution.py
+++ b/solution.py
@@ -167,8 +167,7 @@
 
 def gelu(v):
     u = v * (0.7978845608 + 0.0356774081 * (v * v))
-    half = 0.5 * v
-    return half + half * jnp.tanh(u)
+    return v + v * jnp.tanh(u)
 
 
 def west(v):
@@ -194,7 +193,7 @@
 
 
 def column_sum(z, outs):
-    return z[outs : 2 * outs] + west(z[0:outs]) + east(z[2 * outs : 3 * outs])
+    return 0.5 * (z[outs : 2 * outs] + west(z[0:outs]) + east(z[2 * outs : 3 * outs]))
 
 
 def main_block(s_ref, w_in, w_out, outs, rows, width, emit, shift=1, valid=None):
@@ -278,7 +277,7 @@
     for tap in range(9):
         if tap != 4:
             total = total + strip_shift(z[tap * outs : (tap + 1) * outs], tap // 3, tap % 3, poles)
-    return total
+    return 0.5 * total
 
 
 def mend_row(row, strip, r):
@@ -314,7 +313,7 @@
         tile_ref[r] = jnp.concatenate([state, wet, listed, rest], axis=0).astype(BF)
 
 
-def stack_kernel(place_ref, own_ref, side_ref, cross_ref, even_ref, odd_ref, stack_ref, edge_ref):
+def stack_kernel(place_ref, own_ref, side_ref, odd_ref, cross_ref, even_ref, stack_ref, edge_ref):
     lat, comp = place_ref[0], place_ref[1]
     chans, _, width = own_ref.shape
     valid = window_rule(place_ref)[1]
@@ -548,7 +547,7 @@
 
     for r in range(rows):
         y = parts[r]
-        y = y[1:2] + west(y)[0:1] + east(y)[2:3]
+        y = 0.5 * (y[1:2] + west(y)[0:1] + east(y)[2:3])
         top = wet_ref[r, 0:1, :] * (centre(stack_ref, r + 1, chans)[0:8] + y)
         q = r // 4
         top = mend_row(top, state[0:8, 128 * q : 128 * (q + 1)], r)
@@ -657,20 +656,20 @@
         flops=conv_flops(hidden_a, chans),
     )
     cross = [(i, i + 1) for i in range(1, tiles - 1, 2)]
-    odd = [(i, i + 1) for i in range(1, lats - 1, 2)]
+    odd = [(t, t + 2) for z in range(1, lats - 1, 2) for t in (2 * z, 2 * z + 1)]
 
     def both_ways(pairs):
         return pairs + [(j, i) for i, j in pairs]
 
     cross.append((0, tiles - 1))
-    odd.append((0, lats - 1))
+    odd += [(0, 1), (tiles - 2, tiles - 1)]
 
     near = [
         atmos_state,
         swap(atmos_state, "comp"),
+        lax.ppermute(atmos_state, ("lat", "comp"), both_ways(odd)),
         lax.ppermute(atmos_state, ("lat", "comp"), both_ways(cross)),
         far(atmos_state, 1),
-        lax.ppermute(atmos_state, "lat", both_ways(odd)),
     ]
     def taps_in(w):
         return jnp.transpose(w, (0, 1, 3, 2)).reshape(w.shape[0], 9 * w.shape[3], w.shape[2])

time: 45.6 us -> 44.3 us (0.971)
  waiting for transfers between devices: 7.64 us -> 6.54 us
    ppermute x1, waiting for transfers between devices: 1.64 us -> 0.01 us  [column_device(): lax.ppermute(atmos_state, ('lat', 'comp'), both_ways(odd))]
    ppermute x1, starting transfers between devices: 0.9 us -> 0.08 us  [column_device(): lax.ppermute(atmos_state, ('lat', 'comp'), both_ways(odd))]
    ppermute x4, starting transfers between devices: 3.52 us -> 4.29 us  [far(): return lax.ppermute(v, 'lat', [(i, i ^ k) for i in range(lats)])]
    ppermute x4, waiting for transfers between devices: 4.72 us -> 5.24 us  [far(): return lax.ppermute(v, 'lat', [(i, i ^ k) for i in range(lats)])]
where the time goes in v6:
time: 44.3 us; the launch traced here: 44 us
  Pallas kernels  20.6 us (47%)
  starting transfers between devices  12.3 us (28%)
  waiting for transfers between devices  6.54 us (15%)
  local copies, waits for them, and re-layouts  3.58 us (8%)
  between operations  0.9 us (2%)
    pallas_call x7, Pallas kernels, call(): pl.pallas_call(kernel, out_shape=out_shape, in_specs=[pl.BlockSpec(memory...  20.6 us
    ppermute x4, waiting for transfers between devices, far(): return lax.ppermute(v, 'lat', [(i, i ^ k) for i in range(lats)])  5.24 us
    ppermute x1, starting transfers between devices, column_device(): lax.ppermute(atmos_state, ('lat', 'comp'), both_ways(cross))  4.71 us
    ppermute x4, starting transfers between devices, far(): return lax.ppermute(v, 'lat', [(i, i ^ k) for i in range(lats)])  4.29 us
    unnamed x24, local copies, waits for them, and re-layouts  3.58 us
    ppermute x7, starting transfers between devices, swap(): return lax.ppermute(v, axis, [(0, 1), (1, 0)])  3.26 us
    ppermute x7, waiting for transfers between devices, swap(): return lax.ppermute(v, axis, [(0, 1), (1, 0)])  1.29 us
  transfers between devices with their start and end apart: 13, of which 6 were waited for; matrix products, arithmetic and copies ran while one was open for 0% of the time, Pallas kernels for 16%

profile of v6, /device:TPU:0, one launch (start us, length us, event | category | flops | bytes accessed | tf_op | source)
XLA Modules:
  0.0 44.0 jit_solution(3590654224190086649)
XLA Ops:
  0.6 0.5 %collective-permute-start = (bf16[48,2,384]{2,1,0:T(2,128)(2,1)}, bf16[48,2,384]{2,1,0:T(2,128)(2,1)S(1)}, u32[]{:S(2)}, u32[]{:S(2)}) collective-permute-start(bf16[48,2,384]{2,1,0:T(2,128)(2,1)} %own_ref.1), channel_id=1, source_target_pairs={{0,1},{1,0},{2,3},{3,2},{4,5},{5,4},{6,7},{7,6},{8,9},{9,8},{10,11... | collective-permute-start | bytes 221192 | tf_op jit(solution)/shard_map/ppermute | solution.py:641
  1.1 0.1 collective-permute-start.1
  1.2 4.7 %collective-permute-start.2 = (bf16[48,2,384]{2,1,0:T(2,128)(2,1)}, bf16[48,2,384]{2,1,0:T(2,128)(2,1)S(1)}, u32[]{:S(2)}, u32[]{:S(2)}) collective-permute-start(bf16[48,2,384]{2,1,0:T(2,128)(2,1)} %own_ref.1), channel_id=1, source_target_pairs={{1,4},{5,8},{9,12},{0,13},{4,1},{8,5},{12,9},{13,0},{3,6},{7,10},{... | collective-permute-start | bytes 221192 | tf_op jit(solution)/shard_map/ppermute | solution.py:671
  5.9 0.0 collective-permute-start.3
  5.9 0.8 %copy-done.6 = bf16[40,2,384]{2,1,0:T(2,128)(2,1)S(1)} copy-done((bf16[40,2,384]{2,1,0:T(2,128)(2,1)S(1)}, bf16[40,2,384]{2,1,0:T(2,128)(2,1)}, u32[]{:S(2)}) %copy-start.6) | copy-done | bytes 61464
  6.8 0.7 %copy-done.7 = s32[2,384]{1,0:T(2,128)S(1)} copy-done((s32[2,384]{1,0:T(2,128)S(1)}, s32[2,384]{1,0:T(2,128)}, u32[]{:S(2)}) %copy-start.7) | copy-done | bytes 3096
  7.5 0.7 %copy-done.9 = s32[1,1,8,2]{2,3,1,0:T(2,128)S(1)} copy-done((s32[1,1,8,2]{2,3,1,0:T(2,128)S(1)}, s32[1,1,8,2]{2,3,1,0:T(2,128)}, u32[]{:S(2)}) %copy-start.9) | copy-done | bytes 88
  8.1 0.7 %copy-done.10 = s32[1,1,8,2]{2,3,1,0:T(2,128)S(1)} copy-done((s32[1,1,8,2]{2,3,1,0:T(2,128)S(1)}, s32[1,1,8,2]{2,3,1,0:T(2,128)}, u32[]{:S(2)}) %copy-start.10) | copy-done | bytes 88
  8.8 0.7 %copy-done.11 = s32[1,1,8,2]{2,3,1,0:T(2,128)S(1)} copy-done((s32[1,1,8,2]{2,3,1,0:T(2,128)S(1)}, s32[1,1,8,2]{2,3,1,0:T(2,128)}, u32[]{:S(2)}) %copy-start.11) | copy-done | bytes 88
  9.5 0.2 shard_map.141.ocean_ref
  9.7 0.1 pad_add_fusion.place_ref
  9.8 0.0 collective-permute-done.side_ref
  9.8 0.0 collective-permute-done.2.cross_ref
  9.8 0.7 %collective-permute-done.3.even_ref = bf16[48,2,384]{2,1,0:T(2,128)(2,1)S(1)} collective-permute-done((bf16[48,2,384]{2,1,0:T(2,128)(2,1)}, bf16[48,2,384]{2,1,0:T(2,128)(2,1)S(1)}, u32[]{:S(2)}, u32[]{:S(2)}) %collective-permute-start.3) | collective-permute-done | bytes 73760 | tf_op jit(solution)/shard_map/ppermute | solution.py:638
  10.5 1.3 %shard_map.139 = (bf16[1440,384]{1,0:T(8,128)(2,1)S(1)}, bf16[3,48,128]{2,1,0:T(8,128)(2,1)S(1)}) custom-call(s32[3]{0:T(128)S(1)} %pad_add_fusion.place_ref, bf16[48,2,384]{2,1,0:T(2,128)(2,1)S(1)} %copy-done.5, bf16[48,2,384]{2,1,0:T(2,128)(2,1)S(1)} %collective-permute-done.side_ref, bf16[48,2,384]{2,1,0:T(2,128)(2,1)S(1)} %collective-permute-done.1.odd_ref, ...), custom_call_target="tpu_custom_call" | custom-call | flops 5435817984 | bytes 1048576 | tf_op jit(solution)/shard_map/pallas_call | solution.py:602
  11.8 1.6 %collective-permute-start.4 = (bf16[3,48,128]{2,1,0:T(8,128)(2,1)S(1)}, bf16[3,48,128]{2,1,0:T(8,128)(2,1)S(1)}, u32[]{:S(2)}, u32[]{:S(2)}) collective-permute-start(bf16[3,48,128]{2,1,0:T(8,128)(2,1)S(1)} %get-tuple-element.15.own_ref), channel_id=1, source_target_pairs={{0,2},{2,0},{1,3},{3,1},{4,6},{6,4},{5,7},{7,5},{8,10},{10,8},{9,1... | collective-permute-start | bytes 110600 | tf_op jit(solution)/shard_map/ppermute | solution.py:641
  13.4 3.2 %shard_map.140.stack_ref = bf16[1440,384]{1,0:T(8,128)(2,1)S(1)} custom-call(s32[3]{0:T(128)S(1)} %pad_add_fusion.place_ref, bf16[1440,384]{1,0:T(8,128)(2,1)S(1)} %get-tuple-element.14.stack_ref, bf16[2,432,256]{2,1,0:T(8,128)(2,1)S(1)} %bitcast.17, bf16[2,432,256]{2,1,0:T(8,128)(2,1)S(1)} %bitcast.19), custom_call_target="tpu_custom_call" | custom-call | flops 21743271936 | bytes 1048576 | tf_op jit(solution)/shard_map/pallas_call | solution.py:602
  16.6 0.0 copy-start
  16.6 3.2 %shard_map.142 = (bf16[48,2,384]{2,1,0:T(2,128)(2,1)S(1)}, bf16[304,128]{1,0:T(8,128)(2,1)S(1)}) custom-call(s32[3]{0:T(128)S(1)} %pad_add_fusion.place_ref, bf16[1440,384]{1,0:T(8,128)(2,1)S(1)} %shard_map.140.stack_ref, bf16[3,48,128]{2,1,0:T(8,128)(2,1)S(1)} %get-tuple-element.15.own_ref, bf16[3,48,128]{2,1,0:T(8,128)(2,1)S(1)} %collective-permute-done.4.other_ref, ...), custom_call_target="tpu_custom_call" | custom-call | flops 21743271936 | bytes 1048576 | tf_op jit(solution)/shard_map/pallas_call | solution.py:602
  19.8 1.0 %collective-permute-start.6 = (bf16[304,128]{1,0:T(8,128)(2,1)S(1)}, bf16[304,128]{1,0:T(8,128)(2,1)S(1)}, u32[]{:S(2)}, u32[]{:S(2)}) collective-permute-start(bf16[304,128]{1,0:T(8,128)(2,1)S(1)} %get-tuple-element.17.refs_0_), channel_id=1, source_target_pairs={{0,8},{4,12},{8,0},{12,4},{1,9},{5,13},{9,1},{13,5},{2,10},{6,14},... | collective-permute-start | bytes 233480 | tf_op jit(solution)/shard_map/ppermute | solution.py:638
  20.8 3.3 %collective-permute-start.7 = (bf16[304,128]{1,0:T(8,128)(2,1)S(1)}, bf16[304,128]{1,0:T(8,128)(2,1)S(1)}, u32[]{:S(2)}, u32[]{:S(2)}) collective-permute-start(bf16[304,128]{1,0:T(8,128)(2,1)S(1)} %get-tuple-element.17.refs_0_), channel_id=1, source_target_pairs={{0,12},{4,8},{8,4},{12,0},{1,13},{5,9},{9,5},{13,1},{2,14},{6,10},... | collective-permute-start | bytes 233480 | tf_op jit(solution)/shard_map/ppermute | solution.py:638
  24.1 4.6 %collective-permute-done.6.refs_2_ = bf16[304,128]{1,0:T(8,128)(2,1)S(1)} collective-permute-done((bf16[304,128]{1,0:T(8,128)(2,1)S(1)}, bf16[304,128]{1,0:T(8,128)(2,1)S(1)}, u32[]{:S(2)}, u32[]{:S(2)}) %collective-permute-start.6) | collective-permute-done | bytes 77856 | tf_op jit(solution)/shard_map/ppermute | solution.py:638
  28.6 0.5 %collective-permute-start.11 = (bf16[304,128]{1,0:T(8,128)(2,1)S(1)}, bf16[304,128]{1,0:T(8,128)(2,1)S(1)}, u32[]{:S(2)}, u32[]{:S(2)}) collective-permute-start(bf16[304,128]{1,0:T(8,128)(2,1)S(1)} %collective-permute-done.7.refs_3_), channel_id=1, source_target_pairs={{0,1},{1,0},{2,3},{3,2},{4,5},{5,4},{6,7},{7,6},{8,9},{9,8},{10,11... | collective-permute-start | bytes 233480 | tf_op jit(solution)/shard_map/ppermute | solution.py:641
  29.1 0.1 collective-permute-start.9
  29.2 0.7 %collective-permute-done.10.refs_6_ = bf16[304,128]{1,0:T(8,128)(2,1)S(1)} collective-permute-done((bf16[304,128]{1,0:T(8,128)(2,1)S(1)}, bf16[304,128]{1,0:T(8,128)(2,1)S(1)}, u32[]{:S(2)}, u32[]{:S(2)}) %collective-permute-start.10) | collective-permute-done | bytes 77856 | tf_op jit(solution)/shard_map/ppermute | solution.py:641
  29.9 0.2 collective-permute-done.11.refs_7_
  30.0 0.4 collective-permute-done.9.refs_5_
  30.4 3.6 %shard_map.143 = (bf16[2592,384]{1,0:T(8,128)(2,1)S(1)}, f32[16,8,384]{2,1,0:T(8,128)S(1)}, bf16[4,56,128]{2,1,0:T(8,128)(2,1)S(1)}, s32[8,128]{1,0:T(8,128)S(1)}, bf16[48,2,384]{2,1,0:T(2,128)(2,1)}) custom-call(s32[3]{0:T(128)S(1)} %pad_add_fusion.place_ref, bf16[64,128,128]{2,1,0:T(8,128)(2,1)S(1)} %copy-done, ...), custom_call_target="tpu_custom_call" | custom-call | flops 2491416576 | bytes 1048576 | tf_op jit(solution)/shard_map/pallas_call | solution.py:602
  34.0 0.6 %collective-permute-start.12 = (bf16[4,56,128]{2,1,0:T(8,128)(2,1)S(1)}, bf16[4,56,128]{2,1,0:T(8,128)(2,1)S(1)}, u32[]{:S(2)}, u32[]{:S(2)}) collective-permute-start(bf16[4,56,128]{2,1,0:T(8,128)(2,1)S(1)} %get-tuple-element.22.own_ref), channel_id=1, source_target_pairs={{0,2},{2,0},{1,3},{3,1},{4,6},{6,4},{5,7},{7,5},{8,10},{10,8},{9,1... | collective-permute-start | bytes 172040 | tf_op jit(solution)/shard_map/ppermute | solution.py:641
  34.6 3.6 %shard_map.144.stack_ref = bf16[2592,384]{1,0:T(8,128)(2,1)S(1)} custom-call(bf16[2592,384]{1,0:T(8,128)(2,1)S(1)} %get-tuple-element.20.stack_ref, f32[16,8,384]{2,1,0:T(8,128)S(1)} %get-tuple-element.21.wet_ref, bf16[2,432,128]{2,1,0:T(8,128)(2,1)S(1)} %bitcast.13, bf16[2,360,128]{2,1,0:T(8,128)(2,1)S(1)} %bitcast.15), custom_call_target="tpu_custom_call" | custom-call | flops 9965666304 | bytes 1048576 | tf_op jit(solution)/shard_map/pallas_call | solution.py:602
  38.2 0.1 collective-permute-done.12.other_ref
  38.2 5.6 %shard_map.145 = (bf16[40,2,384]{2,1,0:T(2,128)(2,1)}, f32[2,384]{1,0:T(2,128)}) custom-call(s32[3]{0:T(128)S(1)} %pad_add_fusion.place_ref, s32[8,128]{1,0:T(8,128)S(1)} %get-tuple-element.19.table_ref, bf16[2592,384]{1,0:T(8,128)(2,1)S(1)} %shard_map.144.stack_ref, f32[16,8,384]{2,1,0:T(8,128)S(1)} %get-tuple-element.21.wet_ref, ...), custom_call_target="tpu_custom_call" | custom-call | bytes 1048576 | tf_op jit(solution)/shard_map/pallas_call | solution.py:602
  (26 shorter events, 0.1 us)
Async XLA Ops:
  0.6 9.2 %collective-permute-start = (bf16[48,2,384]{2,1,0:T(2,128)(2,1)}, bf16[48,2,384]{2,1,0:T(2,128)(2,1)S(1)}, u32[]{:S(2)}, u32[]{:S(2)}) collective-permute-start(bf16[48,2,384]{2,1,0:T(2,128)(2,1)} %own_ref.1), channel_id=1, source_target_pairs={{0,1},{1,0},{2,3},{3,2},{4,5},{5,4},{6,7},{7,6},{8,9},{9,8},{10,11... | collective-permute-start | bytes 221192 | tf_op jit(solution)/shard_map/ppermute | solution.py:641
  1.1 8.7 %collective-permute-start.1 = (bf16[48,2,384]{2,1,0:T(2,128)(2,1)}, bf16[48,2,384]{2,1,0:T(2,128)(2,1)S(1)}, u32[]{:S(2)}, u32[]{:S(2)}) collective-permute-start(bf16[48,2,384]{2,1,0:T(2,128)(2,1)} %own_ref.1), channel_id=1, source_target_pairs={{4,8},{5,9},{0,1},{12,13},{8,4},{9,5},{1,0},{13,12},{6,10},{7,11},... | collective-permute-start | bytes 221192 | tf_op jit(solution)/shard_map/ppermute | solution.py:670
  1.2 8.6 %collective-permute-start.2 = (bf16[48,2,384]{2,1,0:T(2,128)(2,1)}, bf16[48,2,384]{2,1,0:T(2,128)(2,1)S(1)}, u32[]{:S(2)}, u32[]{:S(2)}) collective-permute-start(bf16[48,2,384]{2,1,0:T(2,128)(2,1)} %own_ref.1), channel_id=1, source_target_pairs={{1,4},{5,8},{9,12},{0,13},{4,1},{8,5},{12,9},{13,0},{3,6},{7,10},{... | collective-permute-start | bytes 221192 | tf_op jit(solution)/shard_map/ppermute | solution.py:671
  5.9 4.6 %collective-permute-start.3 = (bf16[48,2,384]{2,1,0:T(2,128)(2,1)}, bf16[48,2,384]{2,1,0:T(2,128)(2,1)S(1)}, u32[]{:S(2)}, u32[]{:S(2)}) collective-permute-start(bf16[48,2,384]{2,1,0:T(2,128)(2,1)} %own_ref.1), channel_id=1, source_target_pairs={{0,4},{4,0},{8,12},{12,8},{1,5},{5,1},{9,13},{13,9},{2,6},{6,2},{1... | collective-permute-start | bytes 221192 | tf_op jit(solution)/shard_map/ppermute | solution.py:638
  5.9 0.8 %copy-start.6 = (bf16[40,2,384]{2,1,0:T(2,128)(2,1)S(1)}, bf16[40,2,384]{2,1,0:T(2,128)(2,1)}, u32[]{:S(2)}) copy-start(bf16[40,2,384]{2,1,0:T(2,128)(2,1)} %ocean_hbm.1) | copy-start | bytes 184324
  6.8 0.7 %copy-start.7 = (s32[2,384]{1,0:T(2,128)S(1)}, s32[2,384]{1,0:T(2,128)}, u32[]{:S(2)}) copy-start(s32[2,384]{1,0:T(2,128)} %mask_hbm.1) | copy-start | bytes 9220
  7.5 0.7 %copy-start.9 = (s32[1,1,8,2]{2,3,1,0:T(2,128)S(1)}, s32[1,1,8,2]{2,3,1,0:T(2,128)}, u32[]{:S(2)}) copy-start(s32[1,1,8,2]{2,3,1,0:T(2,128)} %param.21) | copy-start | bytes 196
  8.1 0.7 %copy-start.10 = (s32[1,1,8,2]{2,3,1,0:T(2,128)S(1)}, s32[1,1,8,2]{2,3,1,0:T(2,128)}, u32[]{:S(2)}) copy-start(s32[1,1,8,2]{2,3,1,0:T(2,128)} %param.22) | copy-start | bytes 196
  8.8 0.7 %copy-start.11 = (s32[1,1,8,2]{2,3,1,0:T(2,128)S(1)}, s32[1,1,8,2]{2,3,1,0:T(2,128)}, u32[]{:S(2)}) copy-start(s32[1,1,8,2]{2,3,1,0:T(2,128)} %param.23) | copy-start | bytes 196
  9.5 1.0 %copy-start.5 = (bf16[48,2,384]{2,1,0:T(2,128)(2,1)S(1)}, bf16[48,2,384]{2,1,0:T(2,128)(2,1)}, u32[]{:S(2)}) copy-start(bf16[48,2,384]{2,1,0:T(2,128)(2,1)} %own_ref.1) | copy-start | bytes 221188
  9.8 3.6 %copy-start.3 = (bf16[2,9,256,48]{2,3,1,0:T(8,128)(2,1)S(1)}, bf16[2,9,256,48]{2,3,1,0:T(8,128)(2,1)}, u32[]{:S(2)}) copy-start(bf16[2,9,256,48]{2,3,1,0:T(8,128)(2,1)} %param.15) | copy-start | bytes 1327108
  9.8 3.6 %copy-start.4 = (bf16[2,9,48,256]{3,2,1,0:T(8,128)(2,1)S(1)}, bf16[2,9,48,256]{3,2,1,0:T(8,128)(2,1)}, u32[]{:S(2)}) copy-start(bf16[2,9,48,256]{3,2,1,0:T(8,128)(2,1)} %param.16) | copy-start | bytes 1327108
  11.8 4.7 %collective-permute-start.4 = (bf16[3,48,128]{2,1,0:T(8,128)(2,1)S(1)}, bf16[3,48,128]{2,1,0:T(8,128)(2,1)S(1)}, u32[]{:S(2)}, u32[]{:S(2)}) collective-permute-start(bf16[3,48,128]{2,1,0:T(8,128)(2,1)S(1)} %get-tuple-element.15.own_ref), channel_id=1, source_target_pairs={{0,2},{2,0},{1,3},{3,1},{4,6},{6,4},{5,7},{7,5},{8,10},{10,8},{9,1... | collective-permute-start | bytes 110600 | tf_op jit(solution)/shard_map/ppermute | solution.py:641
  13.4 3.2 %copy-start.8 = (bf16[8,48]{1,0:T(8,128)(2,1)S(1)}, bf16[8,48]{1,0:T(8,128)(2,1)}, u32[]{:S(2)}) copy-start(bf16[8,48]{1,0:T(8,128)(2,1)} %proj_ref.1) | copy-start | bytes 2308
  16.6 13.8 %copy-start = (bf16[64,128,128]{2,1,0:T(8,128)(2,1)S(1)}, bf16[64,128,128]{2,1,0:T(8,128)(2,1)}, u32[]{:S(2)}) copy-start(bf16[64,128,128]{2,1,0:T(8,128)(2,1)} %blocks_ref.3) | copy-start | bytes 6291460
  19.8 8.8 %collective-permute-start.6 = (bf16[304,128]{1,0:T(8,128)(2,1)S(1)}, bf16[304,128]{1,0:T(8,128)(2,1)S(1)}, u32[]{:S(2)}, u32[]{:S(2)}) collective-permute-start(bf16[304,128]{1,0:T(8,128)(2,1)S(1)} %get-tuple-element.17.refs_0_), channel_id=1, source_target_pairs={{0,8},{4,12},{8,0},{12,4},{1,9},{5,13},{9,1},{13,5},{2,10},{6,14},... | collective-permute-start | bytes 233480 | tf_op jit(solution)/shard_map/ppermute | solution.py:638
  20.8 7.8 %collective-permute-start.7 = (bf16[304,128]{1,0:T(8,128)(2,1)S(1)}, bf16[304,128]{1,0:T(8,128)(2,1)S(1)}, u32[]{:S(2)}, u32[]{:S(2)}) collective-permute-start(bf16[304,128]{1,0:T(8,128)(2,1)S(1)} %get-tuple-element.17.refs_0_), channel_id=1, source_target_pairs={{0,12},{4,8},{8,4},{12,0},{1,13},{5,9},{9,5},{13,1},{2,14},{6,10},... | collective-permute-start | bytes 233480 | tf_op jit(solution)/shard_map/ppermute | solution.py:638
  24.0 5.1 %collective-permute-start.5 = (bf16[304,128]{1,0:T(8,128)(2,1)S(1)}, bf16[304,128]{1,0:T(8,128)(2,1)S(1)}, u32[]{:S(2)}, u32[]{:S(2)}) collective-permute-start(bf16[304,128]{1,0:T(8,128)(2,1)S(1)} %get-tuple-element.17.refs_0_), channel_id=1, source_target_pairs={{0,4},{4,0},{8,12},{12,8},{1,5},{5,1},{9,13},{13,9},{2,6},{6,2},{1... | collective-permute-start | bytes 233480 | tf_op jit(solution)/shard_map/ppermute | solution.py:638
  24.0 5.2 %collective-permute-start.8 = (bf16[304,128]{1,0:T(8,128)(2,1)S(1)}, bf16[304,128]{1,0:T(8,128)(2,1)S(1)}, u32[]{:S(2)}, u32[]{:S(2)}) collective-permute-start(bf16[304,128]{1,0:T(8,128)(2,1)S(1)} %get-tuple-element.17.refs_0_), channel_id=1, source_target_pairs={{0,1},{1,0},{2,3},{3,2},{4,5},{5,4},{6,7},{7,6},{8,9},{9,8},{10,11... | collective-permute-start | bytes 233480 | tf_op jit(solution)/shard_map/ppermute | solution.py:641
  28.6 1.3 %collective-permute-start.10 = (bf16[304,128]{1,0:T(8,128)(2,1)S(1)}, bf16[304,128]{1,0:T(8,128)(2,1)S(1)}, u32[]{:S(2)}, u32[]{:S(2)}) collective-permute-start(bf16[304,128]{1,0:T(8,128)(2,1)S(1)} %collective-permute-done.6.refs_2_), channel_id=1, source_target_pairs={{0,1},{1,0},{2,3},{3,2},{4,5},{5,4},{6,7},{7,6},{8,9},{9,8},{10,11... | collective-permute-start | bytes 233480 | tf_op jit(solution)/shard_map/ppermute | solution.py:641
  28.6 1.4 %collective-permute-start.11 = (bf16[304,128]{1,0:T(8,128)(2,1)S(1)}, bf16[304,128]{1,0:T(8,128)(2,1)S(1)}, u32[]{:S(2)}, u32[]{:S(2)}) collective-permute-start(bf16[304,128]{1,0:T(8,128)(2,1)S(1)} %collective-permute-done.7.refs_3_), channel_id=1, source_target_pairs={{0,1},{1,0},{2,3},{3,2},{4,5},{5,4},{6,7},{7,6},{8,9},{9,8},{10,11... | collective-permute-start | bytes 233480 | tf_op jit(solution)/shard_map/ppermute | solution.py:641
  29.1 1.3 %collective-permute-start.9 = (bf16[304,128]{1,0:T(8,128)(2,1)S(1)}, bf16[304,128]{1,0:T(8,128)(2,1)S(1)}, u32[]{:S(2)}, u32[]{:S(2)}) collective-permute-start(bf16[304,128]{1,0:T(8,128)(2,1)S(1)} %collective-permute-done.5.refs_1_), channel_id=1, source_target_pairs={{0,1},{1,0},{2,3},{3,2},{4,5},{5,4},{6,7},{7,6},{8,9},{9,8},{10,11... | collective-permute-start | bytes 233480 | tf_op jit(solution)/shard_map/ppermute | solution.py:641
  30.4 4.2 %copy-start.1 = (bf16[2,9,128,48]{2,3,1,0:T(8,128)(2,1)S(1)}, bf16[2,9,128,48]{2,3,1,0:T(8,128)(2,1)}, u32[]{:S(2)}) copy-start(bf16[2,9,128,48]{2,3,1,0:T(8,128)(2,1)} %param.17) | copy-start | bytes 663556
  30.4 4.2 %copy-start.2 = (bf16[2,9,40,128]{3,2,1,0:T(8,128)(2,1)S(1)}, bf16[2,9,40,128]{3,2,1,0:T(8,128)(2,1)}, u32[]{:S(2)}) copy-start(bf16[2,9,40,128]{3,2,1,0:T(8,128)(2,1)} %param.18) | copy-start | bytes 552964
  34.0 4.2 %collective-permute-start.12 = (bf16[4,56,128]{2,1,0:T(8,128)(2,1)S(1)}, bf16[4,56,128]{2,1,0:T(8,128)(2,1)S(1)}, u32[]{:S(2)}, u32[]{:S(2)}) collective-permute-start(bf16[4,56,128]{2,1,0:T(8,128)(2,1)S(1)} %get-tuple-element.22.own_ref), channel_id=1, source_target_pairs={{0,2},{2,0},{1,3},{3,1},{4,6},{6,4},{5,7},{7,5},{8,10},{10,8},{9,1... | collective-permute-start | bytes 172040 | tf_op jit(solution)/shard_map/ppermute | solution.py:641
